TPU v7x, 32 devices: a whole 2x2x4 slice. The times are simulated.
32 devices in a mesh: groups: 2 (over y), dp: 8 (over z, x), mp: 2 (over core).
Axes of the slice: x: 2, y: 2, z: 4, core: 2. Of those that a mesh axis runs over, the one named last changes fastest.
Arguments:
- hidden: bfloat16 [2048, 3, 4096], P(('groups', 'dp'), None, 'mp'), parts along dimension 0, may hold values from -81 to 81
- row_owner: int32 [2048, 1], P(('groups', 'dp')), parts along dimension 0, may hold values from 0 to 7; in each aligned block of 128 rows (0 to 127, 128 to 255, ...) at most 32 rows name the same one
- candidate_shard: int32 [2048, 4], P(('groups', 'dp')), parts along dimension 0, may hold values from 0 to 7, all different within a row; in each aligned block of 128 rows (0 to 127, 128 to 255, ...) at most 96 rows name the same one
- candidate_offset: int32 [2048, 4], P(('groups', 'dp')), parts along dimension 0, may hold values from 0 to 511
- target_logits: bfloat16 [2048, 4], P(('groups', 'dp')), parts along dimension 0, may hold values from -9 to 240
- lengths: int32 [16, 4], P(('groups', 'dp')), parts along dimension 0, may hold values from 1 to 64, 128 in all within a row
- layer_mix: float32 [3, 4096], P(None, 'mp'), may hold values from 0.5 to 2
- draft_head: bfloat16 [4096, 4096], P('dp', 'mp'), may hold values from -0.09375 to 0.09375
Outputs:
- draft_logp: float32 [16, 256, 4], P(('groups', 'dp')), parts along dimension 0
- grad_mix: float32 [6, 4096], P('groups', 'mp'), parts along dimension 0
There are 2 independent parts, one for each index of `groups`. A program takes and returns all parts, laid end to end along the dimension named above; an argument that names none is the same for every part. Nothing has to cross between parts.
Inputs may be any that keep to these rules, and one draw needn't show every extreme that they name: `row_owner`: at most 32 positions of one device have one owner. `candidate_shard`: the 4 candidates of a position lie in different shards; at most 96 candidates of one device's positions lie in one shard. The lengths of one device sum to 128.
All inputs are finite; a program needn't handle non-finite values.
Results may differ from a plain program's by a relative error of at most 0.007.
Values may be sent and summed in bfloat16 or wider, within the bound.
No kernel may reach another device: no remote copies, remote signals or barrier semaphores. Data moves between devices by JAX's collectives and lax.ppermute only.
A program may use at most 64 MiB of HBM per device.

v0:
```python
import jax
import jax.numpy as jnp
from jax import lax
from jax.sharding import PartitionSpec as P

D = 4096


EPS = 1e-06
HIGHEST = lax.Precision.HIGHEST


def slot_ranks(target, number):
    one_hot = (target[:, None] == jnp.arange(number, dtype=jnp.int32)[None, :]).astype(jnp.int32)
    before = jnp.cumsum(one_hot, axis=0) - one_hot
    return jnp.sum(before * one_hot, axis=1)


def position_weights(lengths, positions, sequences):
    seq_ends = jnp.cumsum(lengths)
    seq_starts = seq_ends - lengths
    position = jnp.arange(positions, dtype=jnp.int32)[:, None]
    member = (position >= seq_starts[None, :]) & (position < seq_ends[None, :])
    own_length = jnp.sum(jnp.where(member, lengths[None, :], 0), axis=1)
    closing = jnp.any(member & (position == seq_ends[None, :] - 1), axis=1)
    portion = 1.0 / (own_length.astype(jnp.float32) * sequences)
    return jnp.where(closing, 0.0, portion).astype(jnp.bfloat16)


def draft_terms(tokens, head_rows, target_logits, weight, layer_mix):
    wide_tokens = tokens.astype(jnp.float32)
    wide_heads = head_rows.astype(jnp.float32)
    partial_value = jnp.einsum(
        "rlf,rkf->rkl", wide_tokens * layer_mix[None], wide_heads, precision=HIGHEST
    )
    squares = jnp.sum(wide_tokens * wide_tokens, axis=2)
    partial_value, squares = lax.psum((partial_value, squares), "mp")
    inverse = lax.rsqrt(squares / D + EPS)
    logits = jnp.einsum("rkl,rl->rk", partial_value, inverse, precision=HIGHEST)
    draft_logp = jax.nn.log_softmax(logits, axis=1)
    target = jax.nn.softmax(target_logits.astype(jnp.float32), axis=1)
    grad_logits = weight.astype(jnp.float32)[:, None] * (jnp.exp(draft_logp) - target)
    carried = jnp.einsum("rk,rkf->rf", grad_logits, wide_heads, precision=HIGHEST)
    gradient = jnp.einsum("rlf,rl,rf->lf", wide_tokens, inverse, carried, precision=HIGHEST)
    return (draft_logp, gradient)


def merge_front(values):
    return values.reshape((values.shape[0] * values.shape[1],) + values.shape[2:])


def local(
    hidden,
    row_owner,
    candidate_shard,
    candidate_offset,
    target_logits,
    lengths,
    layer_mix,
    draft_head,
):
    local_rows = hidden.shape[0]
    top_count = candidate_shard.shape[1]
    features = hidden.shape[2]
    peer_count = lax.axis_size("dp")
    capacity = max(2, 2 * local_rows // peer_count)
    spread = min(local_rows, max(2, 3 * local_rows * top_count // (2 * peer_count)))
    flat_shard = candidate_shard.reshape(-1)
    flat_rank = slot_ranks(flat_shard, peer_count)
    wanted = (
        jnp.zeros((peer_count, spread), jnp.int32)
        .at[flat_shard, flat_rank]
        .set(candidate_offset.reshape(-1))
    )
    picked = jnp.take(
        draft_head, lax.all_to_all(wanted, "dp", split_axis=0, concat_axis=0, tiled=True), axis=0
    )
    fetched = lax.all_to_all(picked, "dp", split_axis=0, concat_axis=0, tiled=True)
    head_rows = fetched[flat_shard, flat_rank].reshape(local_rows, top_count, features)
    weight = position_weights(lengths[0], local_rows, float(lengths.shape[1] * peer_count))
    owner_ids = row_owner[:, 0]
    owner_rank = slot_ranks(owner_ids, peer_count)
    source_logp, gradient = draft_terms(hidden, head_rows, target_logits, weight, layer_mix)
    sent_logp = (
        jnp.zeros((peer_count, capacity, top_count), jnp.float32)
        .at[owner_ids, owner_rank]
        .set(source_logp)
    )
    draft_logp = merge_front(
        lax.all_to_all(sent_logp, "dp", split_axis=0, concat_axis=0, tiled=True)
    )
    grad_mix = lax.psum(gradient, "dp")
    return (draft_logp[None], grad_mix)


def solution(mesh):
    return jax.shard_map(
        local,
        mesh=mesh,
        in_specs=(
            P(("groups", "dp"), None, "mp"),
            P(("groups", "dp"), None),
            P(("groups", "dp"), None),
            P(("groups", "dp"), None),
            P(("groups", "dp"), None),
            P(("groups", "dp"), None),
            P(None, "mp"),
            P("dp", "mp"),
        ),
        out_specs=(P(("groups", "dp"), None, None), P("groups", "mp")),
        check_vma=False,
    )
```

profile of v0, /device:TPU:0, one launch (start us, length us, event | category | flops | bytes accessed | tf_op | source)
XLA Modules:
  0.0 214.8 jit_solution(5594435827927525307)
XLA Ops:
  0.6 0.9 copy.33
  1.9 1.1 reduce-window.10
  3.1 0.2 slice_reduce_fusion
  3.3 0.8 copy.36
  4.3 22.1 %scatter_fusion = s32[8,96]{1,0:T(8,128)S(1)} fusion(s32[8,96]{1,0:T(8,128)S(1)} %broadcast_in_dim.57, s32[512]{0:T(512)S(1)} %bitcast.63, s32[512]{0:T(512)S(1)} %reshape.179), kind=kCustom, calls=%fused_computation.2 | custom fusion | bytes 10240 | tf_op jit(solution)/shard_map/scatter | solution.py:73
  26.4 13.5 %all_to_all.25 = s32[8,1,96]{2,1,0:T(1,128)S(1)} all-to-all(s32[8,1,96]{2,1,0:T(1,128)S(1)} %bitcast.61), channel_id=1, replica_groups=mesh['groups'=2,'dp'=8,'mp'=2] {'dp'}, dimensions={0} | all-to-all | bytes 6144 | tf_op jit(solution)/shard_map/all_to_all | solution.py:76
  40.1 4.3 %gather_fusion = bf16[768,2048]{1,0:T(8,128)(2,1)} fusion(bf16[512,2048]{1,0:T(8,128)(2,1)S(1)} %copy-done, s32[1024]{0:T(1024)S(1)} %pad_clamp_fusion), kind=kCustom, calls=%fused_computation | custom fusion | bytes 6294528 | tf_op jit(solution)/shard_map/jit(_take)/gather | solution.py:75
  44.3 3.9 %broadcast_select_fusion = bf16[8,96,2048]{2,1,0:T(8,128)(2,1)} fusion(bf16[8,96,2048]{2,1,0:T(8,128)(2,1)} %bitcast.64, pred[8,96]{1,0:T(8,128)(4,1)S(1)} %compare_and_fusion), kind=kLoop, calls=%fused_computation.13 | loop fusion | flops 1572864 | bytes 6292224 | tf_op jit(solution)/shard_map/jit(_take)/select_n | solution.py:75
  48.3 4.8 %all-to-all-start.1 = ((bf16[8,96,2048]{2,1,0:T(8,128)(2,1)}), bf16[8,96,2048]{2,1,0:T(8,128)(2,1)}, u32[]{:S(2)}, u32[]{:S(2)}) async-start(bf16[8,96,2048]{2,1,0:T(8,128)(2,1)} %broadcast_select_fusion), calls=%async_computation.1 | async-start | bytes 6291456 | tf_op jit(solution)/shard_map/all_to_all | solution.py:78
  53.1 0.2 reduce-window.14
  53.4 0.2 reduce_window_sum.33
  53.6 0.2 select_reduce_fusion
  54.0 3.5 %fusion.2 = (f32[128,3]{0,1:T(4,128)S(1)}, f32[128,3,2048]{2,0,1:T(8,128)}) fusion(bf16[128,3,2048]{2,0,1:T(8,128)(2,1)} %param.8, f32[3,2048]{1,0:T(4,128)S(1)} %copy-done.2), kind=kLoop, calls=%fused_computation.9 | loop fusion | flops 3145344 | bytes 4744704 | tf_op jit(solution)/shard_map/reduce_sum | solution.py:36
  57.5 65.0 %all-to-all-done.1 = bf16[8,96,2048]{2,1,0:T(8,128)(2,1)} async-done(((bf16[8,96,2048]{2,1,0:T(8,128)(2,1)}), bf16[8,96,2048]{2,1,0:T(8,128)(2,1)}, u32[]{:S(2)}, u32[]{:S(2)}) %all-to-all-start.1) | async-done | bytes 3145760 | tf_op jit(solution)/shard_map/all_to_all | solution.py:78
  122.4 13.0 %gather_fusion.1 = bf16[512,2048]{1,0:T(8,128)(2,1)} fusion(bf16[8,96,2048]{2,1,0:T(8,128)(2,1)} %all-to-all-done.1, s32[512]{0:T(512)S(1)} %bitcast.62), kind=kCustom, calls=%fused_computation.1 | custom fusion | bytes 4198400 | tf_op jit(solution)/shard_map/gather | solution.py:79
  135.4 4.1 %reshape.160 = bf16[128,4,2048]{2,1,0:T(4,128)(2,1)} reshape(bf16[512,2048]{1,0:T(8,128)(2,1)} %gather_fusion.1) | data formatting | bytes 4194304 | tf_op jit(solution)/shard_map/reshape | solution.py:79
  139.6 12.7 %fusion = f32[128,4,3]{1,2,0:T(4,128)S(1)} fusion(bf16[128,4,2048]{2,1,0:T(4,128)(2,1)} %reshape.160, f32[128,3,2048]{2,0,1:T(8,128)} %get-tuple-element.11), kind=kOutput, calls=%fused_computation.7 | convolution fusion | flops 37748736 | bytes 5249024 | tf_op jit(solution)/shard_map/rlf,rkf->rkl/dot_general | solution.py:33
  152.2 4.2 %all-reduce = (f32[128,4,3]{1,2,0:T(4,128)S(1)}, f32[128,3]{0,1:T(4,128)S(1)}) all-reduce(f32[128,4,3]{1,2,0:T(4,128)S(1)} %fusion, f32[128,3]{0,1:T(4,128)S(1)} %get-tuple-element.10), channel_id=1, replica_groups=mesh['groups'=2,'dp'=8,'mp'=2] {'mp'}, use_global_device_ids=true, to_apply=%region_6.7 | all-reduce | flops 1920 | bytes 15360 | tf_op jit(solution)/shard_map/psum | solution.py:37
  156.5 0.2 multiply_reduce_fusion
  156.8 0.1 reduce_max.24
  157.0 0.1 copy.47
  157.2 5.2 %fusion.19 = f32[128,1,2048]{2,1,0:T(1,128)S(1)} fusion(f32[128,4,1]{1,2,0:T(1,128)S(1)} %copy.47, bf16[128,4,2048]{2,1,0:T(4,128)(2,1)} %reshape.160), kind=kOutput, calls=%fused_computation.62 | convolution fusion | flops 12582912 | bytes 3147776 | tf_op jit(solution)/shard_map/rk,rkf->rf/dot_general | solution.py:43
  162.3 0.3 copy.63
  162.7 0.6 fusion.5
  163.3 0.1 copy.39
  163.4 6.9 %scatter_fusion.1 = f32[8,32,4]{2,1,0:T(8,128)S(1)} fusion(f32[8,32,4]{2,1,0:T(8,128)S(1)} %broadcast_in_dim.56, s32[128]{0:T(128)S(1)} %fusion.17, f32[128,4]{1,0:T(8,128)S(1)} %copy.39), kind=kCustom, calls=%fused_computation.3 | custom fusion | bytes 7168 | tf_op jit(solution)/shard_map/scatter | solution.py:87
  170.4 0.7 reshape.197
  171.1 3.6 %all-to-all-start.2 = ((f32[8,1,128]{2,1,0:T(1,128)}), f32[8,1,128]{2,1,0:T(1,128)S(1)}, u32[]{:S(2)}, u32[]{:S(2)}) async-start(f32[8,1,128]{2,1,0:T(1,128)} %reshape.197), calls=%async_computation.2 | async-start | bytes 8192 | tf_op jit(solution)/shard_map/all_to_all | solution.py:90
  174.7 38.2 %psum.23 = f32[3,2048]{1,0:T(4,128)} all-reduce(f32[3,2048]{1,0:T(4,128)S(1)} %bitcast.66), channel_id=1, replica_groups=mesh['groups'=2,'dp'=8,'mp'=2] {'dp'}, use_global_device_ids=true, to_apply=%region_17.18 | all-reduce | flops 6144 | bytes 49152 | tf_op jit(solution)/shard_map/psum | solution.py:92
  212.9 0.5 broadcast.227
  213.4 0.7 reduce.7
  214.2 0.7 broadcast_in_dim_reshape.4
  (47 shorter events, 1.5 us)
Async XLA Ops:
  0.6 39.4 %copy-start = (bf16[512,2048]{1,0:T(8,128)(2,1)S(1)}, bf16[512,2048]{1,0:T(8,128)(2,1)}, u32[]{:S(2)}) copy-start(bf16[512,2048]{1,0:T(8,128)(2,1)} %param.15) | copy-start | bytes 6291460
  48.3 4.8 %copy-start.5 = (s32[1,4]{1,0:T(1,128)S(1)}, s32[1,4]{1,0:T(1,128)}, u32[]{:S(2)}) copy-start(s32[1,4]{1,0:T(1,128)} %param.13) | copy-start | bytes 52
  48.3 5.0 %copy-start.3 = (bf16[128,4]{0,1:T(4,128)(2,1)S(1)}, bf16[128,4]{0,1:T(4,128)(2,1)}, u32[]{:S(2)}) copy-start(bf16[128,4]{0,1:T(4,128)(2,1)} %param.12) | copy-start | bytes 3076
  48.3 5.0 %copy-start.4 = (s32[128,1]{0,1:T(1,128)S(1)}, s32[128,1]{0,1:T(1,128)}, u32[]{:S(2)}) copy-start(s32[128,1]{0,1:T(1,128)} %param.9) | copy-start | bytes 1540
  48.3 5.7 %copy-start.2 = (f32[3,2048]{1,0:T(4,128)S(1)}, f32[3,2048]{1,0:T(4,128)}, u32[]{:S(2)}) copy-start(f32[3,2048]{1,0:T(4,128)} %param.14) | copy-start | bytes 73732
  48.3 74.1 %all-to-all-start.1 = ((bf16[8,96,2048]{2,1,0:T(8,128)(2,1)}), bf16[8,96,2048]{2,1,0:T(8,128)(2,1)}, u32[]{:S(2)}, u32[]{:S(2)}) async-start(bf16[8,96,2048]{2,1,0:T(8,128)(2,1)} %broadcast_select_fusion), calls=%async_computation.1 | async-start | bytes 6291456 | tf_op jit(solution)/shard_map/all_to_all | solution.py:78
  157.2 5.5 %copy-start.1 = (bf16[128,3,2048]{2,0,1:T(8,128)(2,1)S(1)}, bf16[128,3,2048]{2,0,1:T(8,128)(2,1)}, u32[]{:S(2)}) copy-start(bf16[128,3,2048]{2,0,1:T(8,128)(2,1)} %param.8) | copy-start | bytes 4718596
  171.1 41.8 %all-to-all-start.2 = ((f32[8,1,128]{2,1,0:T(1,128)}), f32[8,1,128]{2,1,0:T(1,128)S(1)}, u32[]{:S(2)}, u32[]{:S(2)}) async-start(f32[8,1,128]{2,1,0:T(1,128)} %reshape.197), calls=%async_computation.2 | async-start | bytes 8192 | tf_op jit(solution)/shard_map/all_to_all | solution.py:90
where the time goes:
time: 216 us; the launch traced here: 215 us
  waiting for transfers between devices  65 us (30%)
  blocking collectives  55.9 us (26%)
  local copies, waits for them, and re-layouts  55.7 us (26%)
  matrix products  17.8 us (8%)
  other arithmetic  11.2 us (5%)
  starting transfers between devices  8.37 us (4%)
    all_to_all x1, waiting for transfers between devices, local(): lax.all_to_all(picked, 'dp', split_axis=0, concat_axis=0, tiled=True)  65 us
    psum x1, blocking collectives, local(): grad_mix = lax.psum(gradient, 'dp')  38.2 us
    scatter x1, local copies, waits for them, and re-layouts, local(): wanted = jnp.zeros((peer_count, spread), jnp.int32).at[flat_shard, flat_r...  22.1 us
    all_to_all x1, blocking collectives, local(): lax.all_to_all(wanted, 'dp', split_axis=0, concat_axis=0, tiled=True)  13.5 us
    gather x1, local copies, waits for them, and re-layouts, local(): fetched[flat_shard, flat_rank].reshape(local_rows, top_count, features)  13 us
    dot_general x1, matrix products, draft_terms(): jnp.einsum('rlf,rkf->rkl', wide_tokens * layer_mix[None], wide_heads, pre...  12.7 us
    scatter x2, local copies, waits for them, and re-layouts, local(): sent_logp = jnp.zeros((peer_count, capacity, top_count), jnp.float32).at[...  7.01 us
    dot_general x1, matrix products, draft_terms(): jnp.einsum('rk,rkf->rf', grad_logits, wide_heads, precision=HIGHEST)  5.17 us
  transfers between devices with their start and end apart: 2, of which 1 were waited for; matrix products, arithmetic and copies ran while one was open for 2% of the time, Pallas kernels for 0%

commit v1 on v0

v1 whole, which is shorter than its diff:
```python
import functools

import jax
import jax.numpy as jnp
from jax import lax
from jax.experimental import pallas as pl
from jax.experimental.pallas import tpu as pltpu
from jax.sharding import PartitionSpec as P

EPS = 1e-06
HIGHEST = lax.Precision.HIGHEST
F32 = jnp.float32
BF16 = jnp.bfloat16
VMEM_LIMIT = 48 * 1024 * 1024


def iota(shape, axis):
    return lax.broadcasted_iota(jnp.int32, shape, axis)


def slot_mask(asked, spread):
    shards, rows = asked.shape
    held = asked >= 0
    earlier = (iota((rows, rows), 0) < iota((rows, rows), 1)).astype(BF16)
    rank = jnp.dot(held.astype(BF16), earlier, preferred_element_type=F32)
    rank = jnp.where(held, rank, -1.0)
    place = iota((shards, spread, rows), 1).astype(F32)
    return rank[:, None, :] == place


def pick_kernel(asked_ref, head_ref, out_ref, hot_ref, *, spread):
    @pl.when(pl.program_id(0) == 0)
    def _():
        asked = asked_ref[...]
        shards, rows = asked.shape
        mask = slot_mask(asked, spread)
        row = jnp.where(mask, (asked.astype(F32) + 1.0)[:, None, :], 0.0)
        row = jnp.sum(row.reshape(shards * spread, rows), axis=1, keepdims=True) - 1.0
        lane = iota((1, head_ref.shape[0]), 1).astype(F32)
        hot_ref[...] = jnp.where(row == lane, 1.0, 0.0).astype(BF16)

    out_ref[...] = jnp.dot(hot_ref[...], head_ref[...], preferred_element_type=F32).astype(BF16)


def score_kernel(asked_ref, mixed_ref, rows_ref, out_ref, total_ref, *, spread):
    step = pl.program_id(0)

    @pl.when(step == 0)
    def _():
        total_ref[...] = jnp.zeros_like(total_ref)

    total_ref[...] += lax.dot_general(
        rows_ref[...], mixed_ref[...], (((1,), (1,)), ((), ())), preferred_element_type=F32
    )

    @pl.when(step == pl.num_programs(0) - 1)
    def _():
        asked = asked_ref[...]
        shards, rows = asked.shape
        score = total_ref[:, :rows] + total_ref[:, rows:]
        mask = slot_mask(asked, spread)
        out_ref[...] = jnp.sum(
            jnp.where(mask, score.reshape(shards, spread, rows), 0.0), axis=1
        )


def grad_kernel(
    own_ref,
    other_ref,
    asked_ref,
    shard_ref,
    target_ref,
    weight_ref,
    slot_ref,
    inverse_ref,
    rows_ref,
    hidden_ref,
    sent_ref,
    grad_ref,
    part_ref,
    *,
    spread,
):
    @pl.when(pl.program_id(0) == 0)
    def _():
        asked = asked_ref[...]
        shards, rows = asked.shape
        top = shard_ref.shape[0]
        shard = shard_ref[...]
        by_shard = own_ref[...] + other_ref[...]
        number = iota((shards, rows), 0)
        logits = jnp.concatenate(
            [
                jnp.sum(jnp.where(shard[k : k + 1] == number, by_shard, 0.0), axis=0, keepdims=True)
                for k in range(top)
            ],
            axis=0,
        )
        logits = logits - jnp.max(logits, axis=0, keepdims=True)
        logp = logits - jnp.log(jnp.sum(jnp.exp(logits), axis=0, keepdims=True))
        grad = weight_ref[...] * (jnp.exp(logp) - target_ref[...])
        by_shard = jnp.zeros((shards, rows), F32)
        for k in range(top):
            by_shard = jnp.where(shard[k : k + 1] == number, grad[k : k + 1], by_shard)
        part = jnp.where(slot_mask(asked, spread), by_shard[:, None, :], 0.0)
        part_ref[...] = part.reshape(shards * spread, rows).astype(BF16)
        slots = sent_ref.shape[1]
        placed = (iota((slots, rows), 0) == slot_ref[...]).astype(F32)
        sent_ref[...] = lax.dot_general(
            logp, placed, (((1,), (1,)), ((), ())), preferred_element_type=F32, precision=HIGHEST
        )

    carried = lax.dot_general(
        part_ref[...], rows_ref[...], (((0,), (0,)), ((), ())), preferred_element_type=F32
    )
    for layer in range(hidden_ref.shape[0]):
        scaled = hidden_ref[layer].astype(F32) * inverse_ref[:, layer : layer + 1]
        grad_ref[layer : layer + 1, :] = jnp.sum(scaled * carried, axis=0, keepdims=True)


def whole(shape):
    return pl.BlockSpec(shape, lambda i: (0,) * len(shape))


def params():
    return pltpu.CompilerParams(vmem_limit_bytes=VMEM_LIMIT)


def block_of(features):
    return 512 if features % 512 == 0 else features


def pick(asked, head, spread):
    rows, features = head.shape
    slots, wide = asked.shape[0] * spread, block_of(features)
    return pl.pallas_call(
        functools.partial(pick_kernel, spread=spread),
        grid=(features // wide,),
        in_specs=[whole(asked.shape), pl.BlockSpec((rows, wide), lambda i: (0, i))],
        out_specs=pl.BlockSpec((slots, wide), lambda i: (0, i)),
        out_shape=jax.ShapeDtypeStruct((slots, features), BF16),
        scratch_shapes=[pltpu.VMEM((slots, rows), BF16)],
        compiler_params=params(),
        name="pick",
    )(asked, head)


def score(asked, mixed, fetched, spread):
    slots, features = fetched.shape
    wide = block_of(features)
    return pl.pallas_call(
        functools.partial(score_kernel, spread=spread),
        grid=(features // wide,),
        in_specs=[
            whole(asked.shape),
            pl.BlockSpec((mixed.shape[0], wide), lambda i: (0, i)),
            pl.BlockSpec((slots, wide), lambda i: (0, i)),
        ],
        out_specs=whole(asked.shape),
        out_shape=jax.ShapeDtypeStruct(asked.shape, F32),
        scratch_shapes=[pltpu.VMEM((slots, mixed.shape[0]), F32)],
        compiler_params=params(),
        name="score",
    )(asked, mixed, fetched)


def gradient(own, other, asked, shard, target, weight, slot, inverse, fetched, hidden, spread, slots):
    features = fetched.shape[1]
    wide = block_of(features)
    layers, rows = hidden.shape[:2]
    return pl.pallas_call(
        functools.partial(grad_kernel, spread=spread),
        grid=(features // wide,),
        in_specs=[
            whole(a.shape) for a in (own, other, asked, shard, target, weight, slot, inverse)
        ]
        + [
            pl.BlockSpec((fetched.shape[0], wide), lambda i: (0, i)),
            pl.BlockSpec((layers, rows, wide), lambda i: (0, 0, i)),
        ],
        out_specs=[
            whole((shard.shape[0], slots)),
            pl.BlockSpec((layers, wide), lambda i: (0, i)),
        ],
        out_shape=[
            jax.ShapeDtypeStruct((shard.shape[0], slots), F32),
            jax.ShapeDtypeStruct((layers, features), F32),
        ],
        scratch_shapes=[pltpu.VMEM((fetched.shape[0], rows), BF16)],
        compiler_params=params(),
        name="gradient",
    )(own, other, asked, shard, target, weight, slot, inverse, fetched, hidden)


def position_weights(lengths, positions, sequences):
    seq_ends = jnp.cumsum(lengths)
    seq_starts = seq_ends - lengths
    position = jnp.arange(positions, dtype=jnp.int32)[None, :]
    member = (position >= seq_starts[:, None]) & (position < seq_ends[:, None])
    own_length = jnp.sum(jnp.where(member, lengths[:, None], 0), axis=0, keepdims=True)
    closing = jnp.any(member & (position == seq_ends[:, None] - 1), axis=0, keepdims=True)
    portion = 1.0 / (own_length.astype(F32) * sequences)
    return jnp.where(closing, 0.0, portion).astype(BF16).astype(F32)


def swap_cores(value):
    size = lax.axis_size("mp")
    if size == 1:
        return jnp.zeros_like(value)
    return lax.ppermute(value, "mp", [(i, i ^ 1) for i in range(size)])


def sum_over(value, axis):
    size = lax.axis_size(axis)
    if size & (size - 1) or size > 16:
        return lax.psum(value, axis)
    step = 1
    while step < size:
        value = value + lax.ppermute(value, axis, [(i, i ^ step) for i in range(size)])
        step *= 2
    return value


def exchange(value):
    return lax.all_to_all(value, "dp", split_axis=0, concat_axis=0, tiled=True)


def local(
    hidden,
    row_owner,
    candidate_shard,
    candidate_offset,
    target_logits,
    lengths,
    layer_mix,
    draft_head,
):
    rows, layers, features = hidden.shape
    top = candidate_shard.shape[1]
    peers = lax.axis_size("dp")
    cores = lax.axis_size("mp")
    capacity = max(2, 2 * rows // peers)
    spread = min(rows, max(2, 3 * rows * top // (2 * peers)))
    spread = -(-spread // 8) * 8

    shard = candidate_shard.T
    offset = candidate_offset.T
    number = jnp.arange(peers, dtype=jnp.int32)[:, None]
    asked = jnp.max(
        jnp.where(shard[:, None, :] == number[None], offset[:, None, :], -1), axis=0
    )
    picked = pick(exchange(asked), draft_head, spread)
    fetched = exchange(picked.reshape(peers, spread, features)).reshape(peers * spread, features)

    tokens = hidden.transpose(1, 0, 2)
    wide = tokens.astype(F32)
    squares = jnp.sum(wide * wide, axis=2)
    squares = squares + swap_cores(squares)
    inverse = lax.rsqrt(squares / (features * cores) + EPS)
    mixed = jnp.sum(wide * layer_mix[:, None, :] * inverse[:, :, None], axis=0)
    high = mixed.astype(BF16)
    low = (mixed - high.astype(F32)).astype(BF16)
    mixed = jnp.concatenate([high, low], axis=0)

    weight = position_weights(lengths[0], rows, float(lengths.shape[1] * peers))
    target = jax.nn.softmax(target_logits.T.astype(F32), axis=0)
    owner = row_owner.T
    same = (owner.T == owner) & (iota((rows, rows), 1) < iota((rows, rows), 0))
    slot = owner * capacity + jnp.sum(same.astype(jnp.int32), axis=1)[None, :]

    own = score(asked, mixed, fetched, spread)
    sent, grad = gradient(
        own,
        swap_cores(own),
        asked,
        shard,
        target,
        weight,
        slot,
        inverse.T,
        fetched,
        tokens,
        spread,
        peers * capacity,
    )
    sent = sent.reshape(top, peers, capacity).transpose(1, 0, 2)
    draft_logp = exchange(sent).transpose(0, 2, 1).reshape(1, peers * capacity, top)
    return (draft_logp, sum_over(grad, "dp"))


def solution(mesh):
    return jax.shard_map(
        local,
        mesh=mesh,
        in_specs=(
            P(("groups", "dp"), None, "mp"),
            P(("groups", "dp"), None),
            P(("groups", "dp"), None),
            P(("groups", "dp"), None),
            P(("groups", "dp"), None),
            P(("groups", "dp"), None),
            P(None, "mp"),
            P("dp", "mp"),
        ),
        out_specs=(P(("groups", "dp"), None, None), P("groups", "mp")),
        check_vma=False,
    )
```

time: 216 us -> 125 us (0.58)
  local copies, waits for them, and re-layouts: 55.7 us -> 7.46 us
  blocking collectives: 55.9 us -> 24.1 us
  matrix products: 17.8 us -> 0 us
  Pallas kernels: 0 us -> 7.28 us
  waiting for transfers between devices: 65 us -> 71.1 us
  other arithmetic: 11.2 us -> 7.6 us
    psum x2 -> x0, blocking collectives: 42.3 us -> none  [the longest x1 38.2 us: local(): grad_mix = lax.psum(gradient, 'dp')]
    scatter x3 -> x0, local copies, waits for them, and re-layouts: 29.1 us -> none  [the longest x1 22.1 us: local(): wanted = jnp.zeros((peer_count, spread), jnp.int32).at[flat_shard, flat_r...]
    dot_general x2 -> x0, matrix products: 17.8 us -> none  [the longest x1 12.7 us: draft_terms(): jnp.einsum('rlf,rkf->rkl', wide_tokens * layer_mix[None], wide_heads, pre...]
    gather x2 -> x0, local copies, waits for them, and re-layouts: 17.3 us -> none  [the longest x1 13 us: local(): fetched[flat_shard, flat_rank].reshape(local_rows, top_count, features)]
    all_to_all x1 -> x2, blocking collectives: 13.5 us -> 24.1 us  [exchange(): return lax.all_to_all(value, 'dp', split_axis=0, concat_axis=0, tiled=True)]
    ppermute x0 -> x5, waiting for transfers between devices: none -> 7.86 us  [the longest x3 6.34 us: sum_over(): lax.ppermute(value, axis, [(i, i ^ step) for i in range(size)])]
    pallas_call x0 -> x3, Pallas kernels: none -> 7.28 us  [the longest x1 3.02 us: pick(): pl.pallas_call(functools.partial(pick_kernel, spread=spread), grid=(featu...]
    all_to_all x2 -> x1, starting transfers between devices: 8.37 us -> 3.79 us  [exchange(): return lax.all_to_all(value, 'dp', split_axis=0, concat_axis=0, tiled=True)]
  transfers between devices with their start and end apart: 2 -> 6, of which waited for: 1 -> 5; matrix products, arithmetic and copies ran while one was open for 2% -> 6% of each run, Pallas kernels for 0% -> 0%
where the time goes in v1:
time: 125 us
  waiting for transfers between devices  71.1 us (57%)
  blocking collectives  24.1 us (19%)
  other arithmetic  7.6 us (6%)
  local copies, waits for them, and re-layouts  7.46 us (6%)
  Pallas kernels  7.28 us (6%)
  starting transfers between devices  6.44 us (5%)
    all_to_all x1, waiting for transfers between devices, exchange(): return lax.all_to_all(value, 'dp', split_axis=0, concat_axis=0, tiled=True)  63.3 us
    all_to_all x2, blocking collectives, exchange(): return lax.all_to_all(value, 'dp', split_axis=0, concat_axis=0, tiled=True)  24.1 us
    ppermute x3, waiting for transfers between devices, sum_over(): lax.ppermute(value, axis, [(i, i ^ step) for i in range(size)])  6.34 us
    unnamed x20, local copies, waits for them, and re-layouts  6.07 us
    all_to_all x1, starting transfers between devices, exchange(): return lax.all_to_all(value, 'dp', split_axis=0, concat_axis=0, tiled=True)  3.79 us
    pallas_call x1, Pallas kernels, pick(): pl.pallas_call(functools.partial(pick_kernel, spread=spread), grid=(featu...  3.02 us
    ppermute x3, starting transfers between devices, sum_over(): lax.ppermute(value, axis, [(i, i ^ step) for i in range(size)])  2.51 us
  transfers between devices with their start and end apart: 6, of which 5 were waited for; matrix products, arithmetic and copies ran while one was open for 6% of the time, Pallas kernels for 0%

profile of v1, /device:TPU:0, one launch (start us, length us, event | category | flops | bytes accessed | tf_op | source)
XLA Modules:
  0.0 124.7 jit_solution(15155965027433450199)
XLA Ops:
  0.6 0.7 select_reduce_fusion.asked_ref
  1.3 13.5 %all_to_all.21 = s32[8,1,128]{2,1,0:T(1,128)S(1)} all-to-all(s32[8,1,128]{2,1,0:T(1,128)S(1)} %bitcast.39), channel_id=1, replica_groups=mesh['groups'=2,'dp'=8,'mp'=2] {'dp'}, dimensions={0} | all-to-all | bytes 8192 | tf_op jit(solution)/shard_map/all_to_all | solution.py:225
  14.9 1.6 %copy-done.3 = bf16[512,2048]{1,0:T(8,128)(2,1)S(1)} copy-done((bf16[512,2048]{1,0:T(8,128)(2,1)S(1)}, bf16[512,2048]{1,0:T(8,128)(2,1)}, u32[]{:S(2)}) %copy-start.3) | copy-done | bytes 2097176
  16.4 3.0 %pick.1 = bf16[768,2048]{1,0:T(8,128)(2,1)S(1)} custom-call(s32[8,128]{1,0:T(8,128)S(1)} %bitcast.40, bf16[512,2048]{1,0:T(8,128)(2,1)S(1)} %copy-done.3), custom_call_target="tpu_custom_call" | custom-call | tf_op jit(solution)/shard_map/pick/pallas_call | solution.py:136
  19.5 1.7 %copy-done.1 = bf16[768,2048]{1,0:T(8,128)(2,1)} copy-done((bf16[768,2048]{1,0:T(8,128)(2,1)}, bf16[768,2048]{1,0:T(8,128)(2,1)S(1)}, u32[]{:S(2)}) %copy-start.1) | copy-done | bytes 3145752
  21.1 3.8 %all-to-all-start.1 = ((bf16[8,96,2048]{2,1,0:T(8,128)(2,1)}), bf16[8,96,2048]{2,1,0:T(8,128)(2,1)S(1)}, u32[]{:S(2)}, u32[]{:S(2)}) async-start(bf16[8,96,2048]{2,1,0:T(8,128)(2,1)} %bitcast.37), calls=%async_computation.1 | async-start | bytes 6291456 | tf_op jit(solution)/shard_map/all_to_all | solution.py:225
  24.9 1.8 %fusion.2 = f32[3,128]{1,0:T(4,128)S(1)} fusion(bf16[128,3,2048]{2,0,1:T(8,128)(2,1)} %param.8), kind=kLoop, calls=%fused_computation.4 | loop fusion | flops 2358912 | bytes 1574400 | tf_op jit(solution)/shard_map/reduce_sum | solution.py:257
  26.9 0.2 reduce-window.7
  27.1 0.2 convert_reduce_fusion
  27.3 0.1 fusion.7
  27.4 0.1 select_reduce_fusion.1
  27.5 0.5 collective-permute-done
  28.0 1.9 %fusion.1 = f32[128,2048]{1,0:T(8,128)S(1)} fusion(f32[3,128]{1,0:T(4,128)S(1)} %add_rsqrt_fusion, f32[3,2048]{1,0:T(4,128)S(1)} %copy-done.5, bf16[128,3,2048]{2,0,1:T(8,128)(2,1)} %param.8), kind=kLoop, calls=%fused_computation.3 | loop fusion | flops 2883584 | bytes 2647552 | tf_op jit(solution)/shard_map/reduce_sum | solution.py:260
  29.9 0.1 subtract_convert_fusion
  30.1 1.1 pad_maximum_fusion.mixed_ref
  31.2 63.3 %all-to-all-done.1 = bf16[8,96,2048]{2,1,0:T(8,128)(2,1)S(1)} async-done(((bf16[8,96,2048]{2,1,0:T(8,128)(2,1)}), bf16[8,96,2048]{2,1,0:T(8,128)(2,1)S(1)}, u32[]{:S(2)}, u32[]{:S(2)}) %all-to-all-start.1) | async-done | bytes 3145760 | tf_op jit(solution)/shard_map/all_to_all | solution.py:225
  94.4 1.2 copy-done.2
  95.6 2.2 %score.1.own_ref = f32[8,128]{1,0:T(8,128)S(1)} custom-call(s32[8,128]{1,0:T(8,128)S(1)} %select_reduce_fusion.asked_ref, bf16[256,2048]{1,0:T(8,128)(2,1)S(1)} %copy-done.2, bf16[768,2048]{1,0:T(8,128)(2,1)S(1)} %bitcast.34), custom_call_target="tpu_custom_call" | custom-call | tf_op jit(solution)/shard_map/score/pallas_call | solution.py:151
  98.0 0.1 copy.31
  98.1 1.0 collective-permute-done.1.other_ref
  99.1 1.4 %copy-done = bf16[128,3,2048]{2,0,1:T(8,128)(2,1)S(1)} copy-done((bf16[128,3,2048]{2,0,1:T(8,128)(2,1)S(1)}, bf16[128,3,2048]{2,0,1:T(8,128)(2,1)}, u32[]{:S(2)}) %copy-start) | copy-done | bytes 1572888
  100.5 2.0 %gradient.1 = (f32[4,256]{1,0:T(4,128)S(1)}, f32[3,2048]{1,0:T(4,128)S(1)}) custom-call(f32[8,128]{1,0:T(8,128)S(1)} %score.1.own_ref, f32[8,128]{1,0:T(8,128)S(1)} %collective-permute-done.1.other_ref, s32[8,128]{1,0:T(8,128)S(1)} %select_reduce_fusion.asked_ref, s32[4,128]{1,0:T(4,128)S(1)} %bitcast.42, f32[4,128]{1,0:T(4,128)S(1)} %divide_bitcast_fusion.target_ref, ...), custom_call_target="tpu_custom_call" | custom-call | tf_op jit(solution)/shard_map/gradient/pallas_call | solution.py:171
  102.6 1.5 %collective-permute-start.2 = (f32[3,2048]{1,0:T(4,128)S(1)}, f32[3,2048]{1,0:T(4,128)S(1)}, u32[]{:S(2)}, u32[]{:S(2)}) collective-permute-start(f32[3,2048]{1,0:T(4,128)S(1)} %get-tuple-element.5), channel_id=1, source_target_pairs={{0,2},{2,0},{4,6},{6,4},{8,10},{10,8},{12,14},{14,12},{1,3},{3,1},... | collective-permute-start | bytes 73736 | tf_op jit(solution)/shard_map/ppermute | solution.py:219
  104.1 2.4 %collective-permute-done.2 = f32[3,2048]{1,0:T(4,128)S(1)} collective-permute-done((f32[3,2048]{1,0:T(4,128)S(1)}, f32[3,2048]{1,0:T(4,128)S(1)}, u32[]{:S(2)}, u32[]{:S(2)}) %collective-permute-start.2) | collective-permute-done | bytes 24608 | tf_op jit(solution)/shard_map/ppermute | solution.py:219
  106.6 3.9 %collective-permute-done.3 = f32[3,2048]{1,0:T(4,128)S(1)} collective-permute-done((f32[3,2048]{1,0:T(4,128)S(1)}, f32[3,2048]{1,0:T(4,128)S(1)}, u32[]{:S(2)}, u32[]{:S(2)}) %collective-permute-start.3) | collective-permute-done | bytes 24608 | tf_op jit(solution)/shard_map/ppermute | solution.py:219
  110.6 0.9 collective-permute-start.4
  111.5 0.1 reshape.130
  111.6 10.5 %all_to_all.22 = f32[8,1,128]{2,1,0:T(1,128)S(1)} all-to-all(f32[8,1,128]{2,1,0:T(1,128)S(1)} %reshape.130), channel_id=1, replica_groups=mesh['groups'=2,'dp'=8,'mp'=2] {'dp'}, dimensions={0} | all-to-all | bytes 8192 | tf_op jit(solution)/shard_map/all_to_all | solution.py:225
  122.2 0.5 broadcast.59
  122.7 0.7 reduce.3
  123.4 0.7 reshape.128
  124.1 0.6 add.33
  (32 shorter events, 0.5 us)
Async XLA Ops:
  14.8 1.6 %copy-start.3 = (bf16[512,2048]{1,0:T(8,128)(2,1)S(1)}, bf16[512,2048]{1,0:T(8,128)(2,1)}, u32[]{:S(2)}) copy-start(bf16[512,2048]{1,0:T(8,128)(2,1)} %head_ref.1) | copy-start | bytes 6291460
  19.5 1.7 %copy-start.1 = (bf16[768,2048]{1,0:T(8,128)(2,1)}, bf16[768,2048]{1,0:T(8,128)(2,1)S(1)}, u32[]{:S(2)}) copy-start(bf16[768,2048]{1,0:T(8,128)(2,1)S(1)} %pick.1) | copy-start | bytes 9437188
  21.1 5.7 %copy-start.6 = (bf16[128,4]{0,1:T(4,128)(2,1)S(1)}, bf16[128,4]{0,1:T(4,128)(2,1)}, u32[]{:S(2)}) copy-start(bf16[128,4]{0,1:T(4,128)(2,1)} %param.12) | copy-start | bytes 3076
  21.1 5.7 %copy-start.7 = (s32[1,4]{1,0:T(1,128)S(1)}, s32[1,4]{1,0:T(1,128)}, u32[]{:S(2)}) copy-start(s32[1,4]{1,0:T(1,128)} %param.13) | copy-start | bytes 52
  21.1 5.9 %copy-start.8 = (s32[128,1]{0,1:T(1,128)S(1)}, s32[128,1]{0,1:T(1,128)}, u32[]{:S(2)}) copy-start(s32[128,1]{0,1:T(1,128)} %param.9) | copy-start | bytes 1540
  21.1 6.8 %copy-start.5 = (f32[3,2048]{1,0:T(4,128)S(1)}, f32[3,2048]{1,0:T(4,128)}, u32[]{:S(2)}) copy-start(f32[3,2048]{1,0:T(4,128)} %param.14) | copy-start | bytes 73732
  21.1 73.3 %all-to-all-start.1 = ((bf16[8,96,2048]{2,1,0:T(8,128)(2,1)}), bf16[8,96,2048]{2,1,0:T(8,128)(2,1)S(1)}, u32[]{:S(2)}, u32[]{:S(2)}) async-start(bf16[8,96,2048]{2,1,0:T(8,128)(2,1)} %bitcast.37), calls=%async_computation.1 | async-start | bytes 6291456 | tf_op jit(solution)/shard_map/all_to_all | solution.py:225
  26.7 1.2 collective-permute-start
  30.1 69.1 %copy-start.4 = (s32[128,4]{0,1:T(4,128)S(1)}, s32[128,4]{0,1:T(4,128)}, u32[]{:S(2)}) copy-start(s32[128,4]{0,1:T(4,128)} %param.10) | copy-start | bytes 6148
  94.4 1.2 copy-start.2
  97.9 1.2 collective-permute-start.1
  99.1 1.4 %copy-start = (bf16[128,3,2048]{2,0,1:T(8,128)(2,1)S(1)}, bf16[128,3,2048]{2,0,1:T(8,128)(2,1)}, u32[]{:S(2)}) copy-start(bf16[128,3,2048]{2,0,1:T(8,128)(2,1)} %param.8) | copy-start | bytes 4718596
  102.6 4.0 %collective-permute-start.2 = (f32[3,2048]{1,0:T(4,128)S(1)}, f32[3,2048]{1,0:T(4,128)S(1)}, u32[]{:S(2)}, u32[]{:S(2)}) collective-permute-start(f32[3,2048]{1,0:T(4,128)S(1)} %get-tuple-element.5), channel_id=1, source_target_pairs={{0,2},{2,0},{4,6},{6,4},{8,10},{10,8},{12,14},{14,12},{1,3},{3,1},... | collective-permute-start | bytes 73736 | tf_op jit(solution)/shard_map/ppermute | solution.py:219
  106.6 4.0 %collective-permute-start.3 = (f32[3,2048]{1,0:T(4,128)S(1)}, f32[3,2048]{1,0:T(4,128)S(1)}, u32[]{:S(2)}, u32[]{:S(2)}) collective-permute-start(f32[3,2048]{1,0:T(4,128)S(1)} %add.31), channel_id=1, source_target_pairs={{0,4},{2,6},{4,0},{6,2},{8,12},{10,14},{12,8},{14,10},{1,5},{3,7},... | collective-permute-start | bytes 73736 | tf_op jit(solution)/shard_map/ppermute | solution.py:219
  110.6 13.6 %collective-permute-start.4 = (f32[3,2048]{1,0:T(4,128)S(1)}, f32[3,2048]{1,0:T(4,128)S(1)}, u32[]{:S(2)}, u32[]{:S(2)}) collective-permute-start(f32[3,2048]{1,0:T(4,128)S(1)} %add.32), channel_id=1, source_target_pairs={{0,8},{2,10},{4,12},{6,14},{8,0},{10,2},{12,4},{14,6},{1,9},{3,11}... | collective-permute-start | bytes 73736 | tf_op jit(solution)/shard_map/ppermute | solution.py:219

commit v2 on v0

v2 whole, which is shorter than its diff:
```python
import functools

import jax
import jax.numpy as jnp
from jax import lax
from jax.experimental import pallas as pl
from jax.experimental.pallas import tpu as pltpu
from jax.sharding import PartitionSpec as P

EPS = 1e-06
HIGHEST = lax.Precision.HIGHEST
F32 = jnp.float32
BF16 = jnp.bfloat16
VMEM_LIMIT = 40 * 1024 * 1024


def iota(shape, axis):
    return lax.broadcasted_iota(jnp.int32, shape, axis)


def slot_mask(asked, spread):
    shards, rows = asked.shape
    held = asked >= 0
    earlier = (iota((rows, rows), 0) < iota((rows, rows), 1)).astype(BF16)
    rank = jnp.dot(held.astype(BF16), earlier, preferred_element_type=F32)
    rank = jnp.where(held, rank, -1.0)
    place = iota((shards, spread, rows), 1).astype(F32)
    return rank[:, None, :] == place


def pieces(features):
    wide = 512 if features % 512 == 0 else features
    return [pl.ds(start, wide) for start in range(0, features, wide)]


def fetch(source, target, sems):
    lead = (slice(None),) * (len(source.shape) - 1)
    copies = [
        pltpu.make_async_copy(source.at[(*lead, cut)], target.at[(*lead, cut)], sems.at[i])
        for i, cut in enumerate(pieces(source.shape[-1]))
    ]
    for copy in copies:
        copy.start()
    return copies


def pick_kernel(asked_ref, head_hbm, out_hbm, head_ref, picked_ref, in_sems, out_sems, *, spread):
    arrivals = fetch(head_hbm, head_ref, in_sems)
    asked = asked_ref[...]
    shards, rows = asked.shape
    mask = slot_mask(asked, spread)
    row = jnp.where(mask, (asked.astype(F32) + 1.0)[:, None, :], 0.0)
    row = jnp.sum(row.reshape(shards * spread, rows), axis=1, keepdims=True) - 1.0
    lane = iota((1, head_ref.shape[0]), 1).astype(F32)
    hot = jnp.where(row == lane, 1.0, 0.0).astype(BF16)
    departures = []
    for i, cut in enumerate(pieces(head_ref.shape[1])):
        arrivals[i].wait()
        picked_ref[:, cut] = jnp.dot(
            hot, head_ref[:, cut], preferred_element_type=F32
        ).astype(BF16)
        copy = pltpu.make_async_copy(picked_ref.at[:, cut], out_hbm.at[:, cut], out_sems.at[i])
        copy.start()
        departures.append(copy)
    for copy in departures:
        copy.wait()


def score_kernel(pack_ref, mixed_hbm, rows_ref, out_ref, mask_ref, mixed_ref, sems):
    arrivals = fetch(mixed_hbm, mixed_ref, sems)
    shards, rows = out_ref.shape
    spread = rows_ref.shape[0] // shards
    mask = slot_mask(pack_ref[:shards, :], spread).astype(F32)
    mask_ref[...] = mask.reshape(mask_ref.shape).astype(BF16)
    for copy in arrivals:
        copy.wait()
    score = lax.dot_general(
        rows_ref[...], mixed_ref[...], (((1,), (1,)), ((), ())), preferred_element_type=F32
    )
    score = (score[:, :rows] + score[:, rows:]).reshape(mask.shape)
    out_ref[...] = jnp.sum(score * mask, axis=1)


def grad_kernel(
    own_ref,
    other_ref,
    pack_ref,
    mask_ref,
    rows_ref,
    hidden_hbm,
    out_ref,
    hidden_ref,
    grad_ref,
    sems,
    *,
    top,
):
    arrivals = fetch(hidden_hbm, hidden_ref, sems)
    layers, rows, features = hidden_ref.shape
    shards = own_ref.shape[0]
    lines = grad_ref.shape[0]
    slots = 128 * ((out_ref.shape[1] - lines) // (2 * top))
    pack = pack_ref[shards:, :]
    shard, target = pack[:top], pack[top : 2 * top]
    weight, owner, column = [pack[2 * top + i : 2 * top + i + 1] for i in range(3)]
    inverse = pack[2 * top + 3 :].T

    by_shard = own_ref[...] + other_ref[...]
    number = iota((shards, rows), 0).astype(F32)
    logits = jnp.concatenate(
        [
            jnp.sum(jnp.where(shard[k : k + 1] == number, by_shard, 0.0), axis=0, keepdims=True)
            for k in range(top)
        ],
        axis=0,
    )
    logits = logits - jnp.max(logits, axis=0, keepdims=True)
    logp = logits - jnp.log(jnp.sum(jnp.exp(logits), axis=0, keepdims=True))
    grad = weight * (jnp.exp(logp) - target)
    by_shard = jnp.zeros((shards, rows), F32)
    for k in range(top):
        by_shard = jnp.where(shard[k : k + 1] == number, grad[k : k + 1], by_shard)
    mask = mask_ref[...].astype(F32).reshape(shards, mask_ref.shape[0] // shards, rows)
    part = (mask * by_shard[:, None, :]).reshape(mask_ref.shape).astype(BF16)

    for i, cut in enumerate(pieces(features)):
        carried = lax.dot_general(
            part, rows_ref[:, cut], (((0,), (0,)), ((), ())), preferred_element_type=F32
        )
        arrivals[i].wait()
        wide = carried.shape[1]
        for layer in range(layers):
            scaled = hidden_ref[layer, :, cut].astype(F32) * inverse[:, layer : layer + 1]
            total = jnp.sum(scaled * carried, axis=0, keepdims=True)
            for j in range(wide // 128):
                line = layer * (features // 128) + i * (wide // 128) + j
                grad_ref[line : line + 1, :] = total[:, j * 128 : (j + 1) * 128]

    high = logp.astype(BF16).astype(F32)
    halves = jnp.concatenate([high, logp - high], axis=0)
    owned = jnp.where(owner == iota((shards, 1, rows), 0).astype(F32), halves[None], 0.0)
    owned = owned.reshape(shards * 2 * top, rows).astype(BF16)
    placed = (iota((slots, rows), 0).astype(F32) == column).astype(BF16)
    sent = lax.dot_general(owned, placed, (((1,), (1,)), ((), ())), preferred_element_type=F32)
    sent = [
        sent[:, j * 128 : (j + 1) * 128].reshape(shards, 2 * top, 128) for j in range(slots // 128)
    ]
    out_ref[:, lines:, :] = jnp.concatenate(sent, axis=1).astype(BF16)
    grad = grad_ref[...].astype(BF16)
    for peer in range(shards):
        out_ref[peer, 0:lines, :] = grad


def sum_kernel(parts_ref, grad_ref, logp_ref):
    total = parts_ref[0].astype(F32)
    for peer in range(1, parts_ref.shape[0]):
        total = total + parts_ref[peer].astype(F32)
    layers, features = grad_ref.shape
    top, slots = logp_ref.shape
    each = features // 128
    for layer in range(layers):
        for j in range(each):
            line = layer * each + j
            grad_ref[layer : layer + 1, j * 128 : (j + 1) * 128] = total[line : line + 1]
    for j in range(slots // 128):
        first = layers * each + j * 2 * top
        logp_ref[:, j * 128 : (j + 1) * 128] = (
            total[first : first + top] + total[first + top : first + 2 * top]
        )


VMEM = pl.BlockSpec(memory_space=pltpu.VMEM)
HBM = pl.BlockSpec(memory_space=pltpu.HBM)


def params():
    return pltpu.CompilerParams(vmem_limit_bytes=VMEM_LIMIT)


def in_hbm(value):
    return pltpu.with_memory_space_constraint(value, pltpu.HBM)


def pick(asked, head, spread):
    rows, features = head.shape
    slots, count = asked.shape[0] * spread, len(pieces(features))
    return pl.pallas_call(
        functools.partial(pick_kernel, spread=spread),
        in_specs=[VMEM, HBM],
        out_specs=HBM,
        out_shape=pltpu.HBM((slots, features), BF16),
        scratch_shapes=[
            pltpu.VMEM((rows, features), BF16),
            pltpu.VMEM((slots, features), BF16),
            pltpu.SemaphoreType.DMA((count,)),
            pltpu.SemaphoreType.DMA((count,)),
        ],
        compiler_params=params(),
        name="pick",
    )(asked, in_hbm(head))


def score(pack, mixed, fetched, shards):
    rows = pack.shape[1]
    return pl.pallas_call(
        score_kernel,
        in_specs=[VMEM, HBM, VMEM],
        out_specs=[VMEM, VMEM],
        out_shape=[
            jax.ShapeDtypeStruct((shards, rows), F32),
            jax.ShapeDtypeStruct((fetched.shape[0], rows), BF16),
        ],
        scratch_shapes=[
            pltpu.VMEM(mixed.shape, BF16),
            pltpu.SemaphoreType.DMA((len(pieces(mixed.shape[1])),)),
        ],
        compiler_params=params(),
        name="score",
    )(pack, in_hbm(mixed), fetched)


def gradient(own, other, pack, mask, fetched, hidden, lines, total_lines, top):
    count = len(pieces(hidden.shape[2]))
    return pl.pallas_call(
        functools.partial(grad_kernel, top=top),
        in_specs=[VMEM] * 5 + [HBM],
        out_specs=VMEM,
        out_shape=jax.ShapeDtypeStruct((own.shape[0], total_lines, 128), BF16),
        scratch_shapes=[
            pltpu.VMEM(hidden.shape, BF16),
            pltpu.VMEM((lines, 128), F32),
            pltpu.SemaphoreType.DMA((count,)),
        ],
        compiler_params=params(),
        name="gradient",
    )(own, other, pack, mask, fetched, in_hbm(hidden))


def add_up(parts, layers, features, top, slots):
    return pl.pallas_call(
        sum_kernel,
        in_specs=[VMEM],
        out_specs=[VMEM] * 2,
        out_shape=[
            jax.ShapeDtypeStruct((layers, features), F32),
            jax.ShapeDtypeStruct((top, slots), F32),
        ],
        compiler_params=params(),
        name="add_up",
    )(parts)


def rounded(value):
    return lax.reduce_precision(value, exponent_bits=8, mantissa_bits=7)


def position_weights(lengths, positions, sequences):
    seq_ends = jnp.cumsum(lengths)
    seq_starts = seq_ends - lengths
    position = jnp.arange(positions, dtype=jnp.int32)[None, :]
    member = (position >= seq_starts[:, None]) & (position < seq_ends[:, None])
    own_length = jnp.sum(jnp.where(member, lengths[:, None], 0), axis=0, keepdims=True)
    closing = jnp.any(member & (position == seq_ends[:, None] - 1), axis=0, keepdims=True)
    portion = 1.0 / (own_length.astype(F32) * sequences)
    return rounded(jnp.where(closing, 0.0, portion))


def swap_cores(value):
    size = lax.axis_size("mp")
    if size == 1:
        return jnp.zeros_like(value)
    return lax.ppermute(value, "mp", [(i, i ^ 1) for i in range(size)])


def exchange(value):
    return lax.all_to_all(value, "dp", split_axis=0, concat_axis=0, tiled=True)


def local(
    hidden,
    row_owner,
    candidate_shard,
    candidate_offset,
    target_logits,
    lengths,
    layer_mix,
    draft_head,
):
    rows, layers, features = hidden.shape
    top = candidate_shard.shape[1]
    peers = lax.axis_size("dp")
    cores = lax.axis_size("mp")
    capacity = max(2, 2 * rows // peers)
    spread = min(rows, max(2, 3 * rows * top // (2 * peers)))
    spread = -(-spread // 8) * 8

    shard = candidate_shard.T
    offset = candidate_offset.T
    number = jnp.arange(peers, dtype=jnp.int32)[:, None]
    asked = jnp.max(
        jnp.where(shard[:, None, :] == number[None], offset[:, None, :], -1), axis=0
    )
    picked = pick(exchange(asked), draft_head, spread)
    fetched = exchange(picked.reshape(peers, spread, features)).reshape(peers * spread, features)

    tokens = hidden.transpose(1, 0, 2)
    wide = tokens.astype(F32)
    squares = jnp.sum(wide * wide, axis=2)
    squares = squares + swap_cores(squares)
    inverse = lax.rsqrt(squares / (features * cores) + EPS)
    mixed = jnp.sum(wide * layer_mix[:, None, :] * inverse[:, :, None], axis=0)
    high = rounded(mixed)
    mixed = jnp.concatenate([high, mixed - high], axis=0).astype(BF16)

    weight = position_weights(lengths[0], rows, float(lengths.shape[1] * peers))
    target = jax.nn.softmax(target_logits.T.astype(F32), axis=0)
    owner = row_owner.T
    same = (owner.T == owner) & (iota((rows, rows), 1) < iota((rows, rows), 0))
    column = lax.axis_index("dp") * capacity + jnp.sum(same.astype(jnp.int32), axis=1)[None, :]
    pack = [asked, shard, target, weight, owner, column, inverse]
    pack = jnp.concatenate([value.astype(F32) for value in pack], axis=0)
    pack = jnp.pad(pack, ((0, -pack.shape[0] % 8), (0, 0)))

    slots = peers * capacity
    lines = layers * features // 128
    total_lines = lines + 2 * top * slots // 128
    own, mask = score(pack, mixed, fetched, peers)
    parts = gradient(own, swap_cores(own), pack, mask, fetched, tokens, lines, total_lines, top)
    grad, logp = add_up(exchange(parts), layers, features, top, slots)
    return (logp.T[None], grad)


def solution(mesh):
    return jax.shard_map(
        local,
        mesh=mesh,
        in_specs=(
            P(("groups", "dp"), None, "mp"),
            P(("groups", "dp"), None),
            P(("groups", "dp"), None),
            P(("groups", "dp"), None),
            P(("groups", "dp"), None),
            P(("groups", "dp"), None),
            P(None, "mp"),
            P("dp", "mp"),
        ),
        out_specs=(P(("groups", "dp"), None, None), P("groups", "mp")),
        check_vma=False,
    )
```

time: 216 us -> 110 us (0.51)
  local copies, waits for them, and re-layouts: 55.7 us -> 0.08 us
  blocking collectives: 55.9 us -> 24.3 us
  matrix products: 17.8 us -> 0 us
  Pallas kernels: 0 us -> 9.54 us
  other arithmetic: 11.2 us -> 6.34 us
  starting transfers between devices: 8.37 us -> 3.93 us
    psum x2 -> x0, blocking collectives: 42.3 us -> none  [the longest x1 38.2 us: local(): grad_mix = lax.psum(gradient, 'dp')]
    scatter x3 -> x0, local copies, waits for them, and re-layouts: 29.1 us -> none  [the longest x1 22.1 us: local(): wanted = jnp.zeros((peer_count, spread), jnp.int32).at[flat_shard, flat_r...]
    dot_general x2 -> x0, matrix products: 17.8 us -> none  [the longest x1 12.7 us: draft_terms(): jnp.einsum('rlf,rkf->rkl', wide_tokens * layer_mix[None], wide_heads, pre...]
    gather x2 -> x0, local copies, waits for them, and re-layouts: 17.3 us -> none  [the longest x1 13 us: local(): fetched[flat_shard, flat_rank].reshape(local_rows, top_count, features)]
    all_to_all x1 -> x2, blocking collectives: 13.5 us -> 24.3 us  [exchange(): return lax.all_to_all(value, 'dp', split_axis=0, concat_axis=0, tiled=True)]
    pallas_call x0 -> x4, Pallas kernels: none -> 9.54 us  [the longest x1 4.36 us: pick(): pl.pallas_call(functools.partial(pick_kernel, spread=spread), in_specs=[V...]
    all_to_all x2 -> x1, starting transfers between devices: 8.37 us -> 3.79 us  [exchange(): return lax.all_to_all(value, 'dp', split_axis=0, concat_axis=0, tiled=True)]
    reshape x3 -> x0, local copies, waits for them, and re-layouts: 4.33 us -> none  [the longest x1 4.11 us: local(): fetched[flat_shard, flat_rank].reshape(local_rows, top_count, features)]
  transfers between devices with their start and end apart: 2 -> 3, of which waited for: 1 -> 3; matrix products, arithmetic and copies ran while one was open for 2% -> 5% of each run, Pallas kernels for 0% -> 0%
where the time goes in v2:
time: 110 us
  waiting for transfers between devices  64.8 us (59%)
  blocking collectives  24.3 us (22%)
  Pallas kernels  9.54 us (9%)
  other arithmetic  6.34 us (6%)
  starting transfers between devices  3.93 us (4%)
    all_to_all x1, waiting for transfers between devices, exchange(): return lax.all_to_all(value, 'dp', split_axis=0, concat_axis=0, tiled=True)  63.2 us
    all_to_all x2, blocking collectives, exchange(): return lax.all_to_all(value, 'dp', split_axis=0, concat_axis=0, tiled=True)  24.3 us
    pallas_call x1, Pallas kernels, pick(): pl.pallas_call(functools.partial(pick_kernel, spread=spread), in_specs=[V...  4.36 us
    all_to_all x1, starting transfers between devices, exchange(): return lax.all_to_all(value, 'dp', split_axis=0, concat_axis=0, tiled=True)  3.79 us
    pallas_call x1, Pallas kernels, gradient(): pl.pallas_call(functools.partial(grad_kernel, top=top), in_specs=[VMEM] *...  2.28 us
    pallas_call x1, Pallas kernels, score(): pl.pallas_call(score_kernel, in_specs=[VMEM, HBM, VMEM], out_specs=[VMEM,...  2.26 us
  transfers between devices with their start and end apart: 3, of which 3 were waited for; matrix products, arithmetic and copies ran while one was open for 5% of the time, Pallas kernels for 0%

profile of v2, /device:TPU:0, one launch (start us, length us, event | category | flops | bytes accessed | tf_op | source)
XLA Modules:
  0.0 109.7 jit_solution(16789585461155367232)
XLA Ops:
  0.6 0.7 select_reduce_fusion
  1.3 13.5 %all_to_all.21 = s32[8,1,128]{2,1,0:T(1,128)S(1)} all-to-all(s32[8,1,128]{2,1,0:T(1,128)S(1)} %bitcast.35), channel_id=1, replica_groups=mesh['groups'=2,'dp'=8,'mp'=2] {'dp'}, dimensions={0} | all-to-all | bytes 8192 | tf_op jit(solution)/shard_map/all_to_all | solution.py:276
  14.8 4.4 %pick.1 = bf16[768,2048]{1,0:T(8,128)(2,1)} custom-call(s32[8,128]{1,0:T(8,128)S(1)} %bitcast.32, bf16[512,2048]{1,0:T(8,128)(2,1)} %head_hbm.1), custom_call_target="tpu_custom_call" | custom-call | tf_op jit(solution)/shard_map/pick/pallas_call | solution.py:187
  19.2 0.0 copy-start.1
  19.2 0.0 copy-start.3
  19.2 0.0 copy-start.4
  19.2 0.0 copy-start.2
  19.3 0.0 copy-start
  19.3 3.8 %all-to-all-start.1 = ((bf16[8,96,2048]{2,1,0:T(8,128)(2,1)}), bf16[8,96,2048]{2,1,0:T(8,128)(2,1)S(1)}, u32[]{:S(2)}, u32[]{:S(2)}) async-start(bf16[8,96,2048]{2,1,0:T(8,128)(2,1)} %bitcast.34), calls=%async_computation.1 | async-start | bytes 6291456 | tf_op jit(solution)/shard_map/all_to_all | solution.py:276
  23.1 1.8 %fusion = f32[3,128]{1,0:T(4,128)S(1)} fusion(bf16[128,3,2048]{2,0,1:T(8,128)(2,1)} %param.8), kind=kLoop, calls=%fused_computation.2 | loop fusion | flops 2358912 | bytes 1574400 | tf_op jit(solution)/shard_map/reduce_sum | solution.py:308
  24.9 0.1 collective-permute-start
  24.9 0.0 copy-done.1
  25.0 0.0 copy-done.3
  25.0 0.2 reduce-window.7
  25.2 0.0 copy-done.4
  25.2 0.2 convert_reduce_fusion
  25.4 0.1 fusion.8
  25.5 0.1 select_reduce_fusion.1
  25.6 0.0 copy-done.2
  25.6 0.4 collective-permute-done
  26.1 0.0 copy-done
  26.2 2.0 %fusion.2 = f32[128,2048]{1,0:T(8,128)S(1)} fusion(f32[3,128]{1,0:T(4,128)S(1)} %add_rsqrt_fusion, f32[3,2048]{1,0:T(4,128)S(1)} %copy-done, bf16[128,3,2048]{2,0,1:T(8,128)(2,1)} %param.8), kind=kLoop, calls=%fused_computation.4 | loop fusion | flops 2883584 | bytes 2647552 | tf_op jit(solution)/shard_map/reduce_sum | solution.py:311
  28.1 0.2 reduce-precision_convert_fusion
  28.3 1.1 pad_maximum_fusion.mixed_hbm
  29.4 63.2 %all-to-all-done.1 = bf16[8,96,2048]{2,1,0:T(8,128)(2,1)S(1)} async-done(((bf16[8,96,2048]{2,1,0:T(8,128)(2,1)}), bf16[8,96,2048]{2,1,0:T(8,128)(2,1)S(1)}, u32[]{:S(2)}, u32[]{:S(2)}) %all-to-all-start.1) | async-done | bytes 3145760 | tf_op jit(solution)/shard_map/all_to_all | solution.py:276
  92.5 2.3 %score.1 = (f32[8,128]{1,0:T(8,128)S(1)}, bf16[768,128]{1,0:T(8,128)(2,1)S(1)}) custom-call(f32[24,128]{1,0:T(8,128)S(1)} %pad.4.pack_ref, bf16[256,2048]{1,0:T(8,128)(2,1)} %pad_maximum_fusion.mixed_hbm, bf16[768,2048]{1,0:T(8,128)(2,1)S(1)} %bitcast.30), custom_call_target="tpu_custom_call" | custom-call | tf_op jit(solution)/shard_map/score/pallas_call | solution.py:205
  94.8 0.1 collective-permute-start.1
  94.9 1.2 %collective-permute-done.1.other_ref = f32[8,128]{1,0:T(8,128)S(1)} collective-permute-done((f32[8,128]{1,0:T(8,128)S(1)}, f32[8,128]{1,0:T(8,128)S(1)}, u32[]{:S(2)}, u32[]{:S(2)}) %collective-permute-start.1) | collective-permute-done | bytes 4128 | tf_op jit(solution)/shard_map/ppermute | solution.py:272
  96.1 2.3 %gradient.1 = bf16[8,64,128]{2,1,0:T(8,128)(2,1)S(1)} custom-call(f32[8,128]{1,0:T(8,128)S(1)} %get-tuple-element.6.own_ref, f32[8,128]{1,0:T(8,128)S(1)} %collective-permute-done.1.other_ref, f32[24,128]{1,0:T(8,128)S(1)} %pad.4.pack_ref, bf16[768,128]{1,0:T(8,128)(2,1)S(1)} %get-tuple-element.7.mask_ref, bf16[768,2048]{1,0:T(8,128)(2,1)S(1)} %bitcast.31, ...), custom_call_target="tpu_custom_call" | custom-call | tf_op jit(solution)/shard_map/gradient/pallas_call | solution.py:224
  98.3 10.8 %all_to_all.22.parts_ref = bf16[8,64,128]{2,1,0:T(8,128)(2,1)S(1)} all-to-all(bf16[8,64,128]{2,1,0:T(8,128)(2,1)S(1)} %gradient.1), channel_id=1, replica_groups=mesh['groups'=2,'dp'=8,'mp'=2] {'dp'}, dimensions={0} | all-to-all | bytes 262144 | tf_op jit(solution)/shard_map/all_to_all | solution.py:276
  109.1 0.6 add_up.1
  (13 shorter events, 0.1 us)
Async XLA Ops:
  19.2 5.7 %copy-start.1 = (bf16[128,4]{0,1:T(4,128)(2,1)S(1)}, bf16[128,4]{0,1:T(4,128)(2,1)}, u32[]{:S(2)}) copy-start(bf16[128,4]{0,1:T(4,128)(2,1)} %param.12) | copy-start | bytes 3076
  19.2 5.8 %copy-start.3 = (s32[1,4]{1,0:T(1,128)S(1)}, s32[1,4]{1,0:T(1,128)}, u32[]{:S(2)}) copy-start(s32[1,4]{1,0:T(1,128)} %param.13) | copy-start | bytes 52
  19.2 6.0 %copy-start.4 = (s32[128,1]{0,1:T(1,128)S(1)}, s32[128,1]{0,1:T(1,128)}, u32[]{:S(2)}) copy-start(s32[128,1]{0,1:T(1,128)} %param.9) | copy-start | bytes 1540
  19.2 6.3 %copy-start.2 = (s32[128,4]{0,1:T(4,128)S(1)}, s32[128,4]{0,1:T(4,128)}, u32[]{:S(2)}) copy-start(s32[128,4]{0,1:T(4,128)} %param.10) | copy-start | bytes 6148
  19.3 6.9 %copy-start = (f32[3,2048]{1,0:T(4,128)S(1)}, f32[3,2048]{1,0:T(4,128)}, u32[]{:S(2)}) copy-start(f32[3,2048]{1,0:T(4,128)} %param.14) | copy-start | bytes 73732
  19.3 73.3 %all-to-all-start.1 = ((bf16[8,96,2048]{2,1,0:T(8,128)(2,1)}), bf16[8,96,2048]{2,1,0:T(8,128)(2,1)S(1)}, u32[]{:S(2)}, u32[]{:S(2)}) async-start(bf16[8,96,2048]{2,1,0:T(8,128)(2,1)} %bitcast.34), calls=%async_computation.1 | async-start | bytes 6291456 | tf_op jit(solution)/shard_map/all_to_all | solution.py:276
  24.9 1.2 %collective-permute-start = (f32[3,128]{1,0:T(4,128)S(1)}, f32[3,128]{1,0:T(4,128)S(1)}, u32[]{:S(2)}, u32[]{:S(2)}) collective-permute-start(f32[3,128]{1,0:T(4,128)S(1)} %fusion), channel_id=1, source_target_pairs={{0,1},{1,0},{2,3},{3,2},{4,5},{5,4},{6,7},{7,6},{8,9},{9,8},{10,11... | collective-permute-start | bytes 4616 | tf_op jit(solution)/shard_map/ppermute | solution.py:272
  94.8 1.2 %collective-permute-start.1 = (f32[8,128]{1,0:T(8,128)S(1)}, f32[8,128]{1,0:T(8,128)S(1)}, u32[]{:S(2)}, u32[]{:S(2)}) collective-permute-start(f32[8,128]{1,0:T(8,128)S(1)} %get-tuple-element.6.own_ref), channel_id=1, source_target_pairs={{0,1},{1,0},{2,3},{3,2},{4,5},{5,4},{6,7},{7,6},{8,9},{9,8},{10,11... | collective-permute-start | bytes 12296 | tf_op jit(solution)/shard_map/ppermute | solution.py:272

commit v3 on v2

--- a/solution.py
+++ b/solution.py
@@ -12,6 +12,7 @@
 F32 = jnp.float32
 BF16 = jnp.bfloat16
 VMEM_LIMIT = 40 * 1024 * 1024
+CHUNKS = (256, 256)
 
 
 def iota(shape, axis):
@@ -29,8 +30,7 @@
 
 
 def pieces(features):
-    wide = 512 if features % 512 == 0 else features
-    return [pl.ds(start, wide) for start in range(0, features, wide)]
+    return [pl.ds(start, min(512, features - start)) for start in range(0, features, 512)]
 
 
 def fetch(source, target, sems):
@@ -44,17 +44,25 @@
     return copies
 
 
-def pick_kernel(asked_ref, head_hbm, out_hbm, head_ref, picked_ref, in_sems, out_sems, *, spread):
-    arrivals = fetch(head_hbm, head_ref, in_sems)
-    asked = asked_ref[...]
+def hot_rows(asked, spread, count):
     shards, rows = asked.shape
     mask = slot_mask(asked, spread)
     row = jnp.where(mask, (asked.astype(F32) + 1.0)[:, None, :], 0.0)
     row = jnp.sum(row.reshape(shards * spread, rows), axis=1, keepdims=True) - 1.0
-    lane = iota((1, head_ref.shape[0]), 1).astype(F32)
-    hot = jnp.where(row == lane, 1.0, 0.0).astype(BF16)
+    return jnp.where(row == iota((1, count), 1).astype(F32), 1.0, 0.0).astype(BF16)
+
+
+def every_other(ref, first):
+    lines = [ref[i : i + 1, :] for i in range(first, ref.shape[0], 2)]
+    return jnp.concatenate(lines, axis=0)
+
+
+def pick_kernel(asked_ref, head_hbm, out_hbm, head_ref, picked_ref, in_sems, out_sems, *, spread):
+    late = head_ref.shape[1]
+    arrivals = fetch(head_hbm.at[:, :late], head_ref, in_sems)
+    hot = hot_rows(every_other(asked_ref, 0), spread, head_ref.shape[0])
     departures = []
-    for i, cut in enumerate(pieces(head_ref.shape[1])):
+    for i, cut in enumerate(pieces(late)):
         arrivals[i].wait()
         picked_ref[:, cut] = jnp.dot(
             hot, head_ref[:, cut], preferred_element_type=F32
@@ -66,44 +74,111 @@
         copy.wait()
 
 
-def score_kernel(pack_ref, mixed_hbm, rows_ref, out_ref, mask_ref, mixed_ref, sems):
+def early_kernel(asked_ref, head_hbm, near_hbm, far_hbm, *refs, spread, start):
+    *out_refs, own_ref, other_ref, sems = refs
+    count, wide = own_ref.shape
+    copies = [
+        pltpu.make_async_copy(head_hbm.at[:, pl.ds(start, wide)], own_ref, sems.at[0]),
+        pltpu.make_async_copy(near_hbm, other_ref.at[: count // 2, :], sems.at[1]),
+        pltpu.make_async_copy(far_hbm, other_ref.at[count // 2 :, :], sems.at[2]),
+    ]
+    for copy in copies:
+        copy.start()
+    peers = asked_ref.shape[0] // 2
+    hot = [hot_rows(every_other(asked_ref, i), spread, count) for i in range(2)]
+    for copy in copies:
+        copy.wait()
+    each = 2 * peers * spread // len(out_refs)
+    for i, table in enumerate((own_ref, other_ref)):
+        picked = jnp.dot(hot[i], table[...], preferred_element_type=F32).astype(BF16)
+        for peer in range(peers):
+            first = (2 * peer + i) * spread
+            out_refs[first // each][first % each : first % each + spread, :] = picked[
+                peer * spread : (peer + 1) * spread
+            ]
+
+
+def swapped(value, flags):
+    size = value.shape[0]
+    for bit, flag in enumerate(flags):
+        if flag is None:
+            continue
+        step = 1 << bit
+        other = [value[start ^ step : (start ^ step) + step] for start in range(0, size, step)]
+        value = jnp.where(flag, jnp.concatenate(other, axis=0), value)
+    return value
+
+
+def to_pairs(value, flags):
+    half = value.shape[0] // 2
+    value = swapped(value, flags)
+    lines = [value[j * half + i : j * half + i + 1] for i in range(half) for j in range(2)]
+    return jnp.concatenate(lines, axis=0)
+
+
+def from_pairs(value, flags):
+    size = value.shape[0]
+    lines = [value[i : i + 1] for j in range(2) for i in range(j, size, 2)]
+    return swapped(jnp.concatenate(lines, axis=0), flags)
+
+
+def flags_of(pack_ref, shards, used):
+    lines = pack_ref[2 * shards : 2 * shards + 8, :]
+    return [lines[b : b + 1] > 0.5 if use else None for b, use in enumerate(used)]
+
+
+def chunks_of(refs, parts, start):
+    for i in range(0, len(refs), parts):
+        yield refs[i : i + parts], start
+        start += refs[i].shape[1]
+
+
+def score_kernel(pack_ref, mixed_hbm, late_ref, *refs, used, parts):
+    *early_refs, out_ref, late_mask_ref, early_mask_ref, mixed_ref, sems = refs
     arrivals = fetch(mixed_hbm, mixed_ref, sems)
     shards, rows = out_ref.shape
-    spread = rows_ref.shape[0] // shards
-    mask = slot_mask(pack_ref[:shards, :], spread).astype(F32)
-    mask_ref[...] = mask.reshape(mask_ref.shape).astype(BF16)
+    spread = late_ref.shape[0] // shards
+    late = late_ref.shape[1]
+    late_mask = slot_mask(pack_ref[:shards, :], spread).astype(F32)
+    early_mask = slot_mask(pack_ref[shards : 2 * shards, :], spread).astype(F32)
+    late_mask_ref[...] = late_mask.reshape(late_mask_ref.shape).astype(BF16)
+    early_mask_ref[...] = early_mask.reshape(early_mask_ref.shape).astype(BF16)
+    flags = flags_of(pack_ref, shards, used)
     for copy in arrivals:
         copy.wait()
-    score = lax.dot_general(
-        rows_ref[...], mixed_ref[...], (((1,), (1,)), ((), ())), preferred_element_type=F32
-    )
-    score = (score[:, :rows] + score[:, rows:]).reshape(mask.shape)
-    out_ref[...] = jnp.sum(score * mask, axis=1)
+
+    def scored(rows_ref, mixed, mask):
+        score = lax.dot_general(
+            rows_ref[...], mixed, (((1,), (1,)), ((), ())), preferred_element_type=F32
+        )
+        score = (score[:, :rows] + score[:, rows:]).reshape(mask.shape)
+        return jnp.sum(score * mask, axis=1)
+
+    total = scored(late_ref, mixed_ref[:, :late], late_mask)
+    for group, start in chunks_of(early_refs, parts, late):
+        lines, each = [], shards // parts
+        for i, early_ref in enumerate(group):
+            mixed = mixed_ref[:, pl.ds(start, early_ref.shape[1])]
+            lines.append(scored(early_ref, mixed, early_mask[i * each : (i + 1) * each]))
+        total = total + from_pairs(jnp.concatenate(lines, axis=0), flags)
+    out_ref[...] = total
 
 
 def grad_kernel(
-    own_ref,
-    other_ref,
-    pack_ref,
-    mask_ref,
-    rows_ref,
-    hidden_hbm,
-    out_ref,
-    hidden_ref,
-    grad_ref,
-    sems,
-    *,
-    top,
+    own_ref, other_ref, pack_ref, late_mask_ref, early_mask_ref, late_ref, *refs, top, used, parts
 ):
+    *early_refs, hidden_hbm, out_ref, hidden_ref, grad_ref, sems = refs
     arrivals = fetch(hidden_hbm, hidden_ref, sems)
     layers, rows, features = hidden_ref.shape
     shards = own_ref.shape[0]
     lines = grad_ref.shape[0]
     slots = 128 * ((out_ref.shape[1] - lines) // (2 * top))
-    pack = pack_ref[shards:, :]
+    flags = flags_of(pack_ref, shards, used)
+    pack = pack_ref[2 * shards + 8 :, :]
     shard, target = pack[:top], pack[top : 2 * top]
     weight, owner, column = [pack[2 * top + i : 2 * top + i + 1] for i in range(3)]
-    inverse = pack[2 * top + 3 :].T
+    inverse = pack[2 * top + 3 : 2 * top + 3 + layers]
+    inverse = jnp.pad(inverse, ((0, 8 - layers), (0, 0))).T
 
     by_shard = own_ref[...] + other_ref[...]
     number = iota((shards, rows), 0).astype(F32)
@@ -120,21 +195,37 @@
     by_shard = jnp.zeros((shards, rows), F32)
     for k in range(top):
         by_shard = jnp.where(shard[k : k + 1] == number, grad[k : k + 1], by_shard)
-    mask = mask_ref[...].astype(F32).reshape(shards, mask_ref.shape[0] // shards, rows)
-    part = (mask * by_shard[:, None, :]).reshape(mask_ref.shape).astype(BF16)
-
-    for i, cut in enumerate(pieces(features)):
-        carried = lax.dot_general(
-            part, rows_ref[:, cut], (((0,), (0,)), ((), ())), preferred_element_type=F32
-        )
-        arrivals[i].wait()
-        wide = carried.shape[1]
-        for layer in range(layers):
-            scaled = hidden_ref[layer, :, cut].astype(F32) * inverse[:, layer : layer + 1]
-            total = jnp.sum(scaled * carried, axis=0, keepdims=True)
-            for j in range(wide // 128):
-                line = layer * (features // 128) + i * (wide // 128) + j
-                grad_ref[line : line + 1, :] = total[:, j * 128 : (j + 1) * 128]
+
+    def spread_out(mask, values):
+        mask = mask.astype(F32).reshape(values.shape[0], -1, rows)
+        return (mask * values[:, None, :]).reshape(-1, rows).astype(BF16)
+
+    late = late_ref.shape[1]
+    pairs = to_pairs(by_shard, flags)
+    part = spread_out(early_mask_ref[...], pairs)
+    each = part.shape[0] // parts
+    part = [part[i * each : (i + 1) * each] for i in range(parts)]
+    sources = [([late_ref], [spread_out(late_mask_ref[...], by_shard)], 0)]
+    for group, start in chunks_of(early_refs, parts, late):
+        sources.append((group, part, start))
+    for copy in arrivals:
+        copy.wait()
+    for rows_refs, grads, start in sources:
+        for cut in pieces(rows_refs[0].shape[1]):
+            carried = sum(
+                lax.dot_general(
+                    grad, rows_ref[:, cut], (((0,), (0,)), ((), ())), preferred_element_type=F32
+                )
+                for rows_ref, grad in zip(rows_refs, grads)
+            )
+            wide, first = carried.shape[1], start + cut.start
+            for layer in range(layers):
+                scaled = hidden_ref[layer, :, pl.ds(first, wide)].astype(F32)
+                scaled = scaled * inverse[:, layer : layer + 1]
+                total = jnp.sum(scaled * carried, axis=0, keepdims=True)
+                for j in range(wide // 128):
+                    line = (layer * features + first) // 128 + j
+                    grad_ref[line : line + 1, :] = total[:, j * 128 : (j + 1) * 128]
 
     high = logp.astype(BF16).astype(F32)
     halves = jnp.concatenate([high, logp - high], axis=0)
@@ -181,17 +272,17 @@
     return pltpu.with_memory_space_constraint(value, pltpu.HBM)
 
 
-def pick(asked, head, spread):
-    rows, features = head.shape
-    slots, count = asked.shape[0] * spread, len(pieces(features))
+def pick(asked, head, spread, late):
+    rows = head.shape[0]
+    slots, count = asked.shape[0] // 2 * spread, len(pieces(late))
     return pl.pallas_call(
         functools.partial(pick_kernel, spread=spread),
         in_specs=[VMEM, HBM],
         out_specs=HBM,
-        out_shape=pltpu.HBM((slots, features), BF16),
+        out_shape=pltpu.HBM((slots, late), BF16),
         scratch_shapes=[
-            pltpu.VMEM((rows, features), BF16),
-            pltpu.VMEM((slots, features), BF16),
+            pltpu.VMEM((rows, late), BF16),
+            pltpu.VMEM((slots, late), BF16),
             pltpu.SemaphoreType.DMA((count,)),
             pltpu.SemaphoreType.DMA((count,)),
         ],
@@ -200,15 +291,35 @@
     )(asked, in_hbm(head))
 
 
-def score(pack, mixed, fetched, shards):
+def pick_early(asked, head, near, far, spread, start, count):
+    rows, wide = head.shape[0], near.shape[1]
+    slots = asked.shape[0] * spread
+    return pl.pallas_call(
+        functools.partial(early_kernel, spread=spread, start=start),
+        in_specs=[VMEM, HBM, HBM, HBM],
+        out_specs=[VMEM] * count,
+        out_shape=[jax.ShapeDtypeStruct((slots // count, wide), BF16)] * count,
+        scratch_shapes=[
+            pltpu.VMEM((rows, wide), BF16),
+            pltpu.VMEM((rows, wide), BF16),
+            pltpu.SemaphoreType.DMA((3,)),
+        ],
+        compiler_params=params(),
+        name="pick_early",
+    )(asked, in_hbm(head), in_hbm(near), in_hbm(far))
+
+
+def score(pack, mixed, late, early, shards, used, parts):
     rows = pack.shape[1]
+    slots = sum(array.shape[0] for array in early[:parts])
     return pl.pallas_call(
-        score_kernel,
-        in_specs=[VMEM, HBM, VMEM],
-        out_specs=[VMEM, VMEM],
+        functools.partial(score_kernel, used=used, parts=parts),
+        in_specs=[VMEM, HBM, VMEM] + [VMEM] * len(early),
+        out_specs=[VMEM] * 3,
         out_shape=[
             jax.ShapeDtypeStruct((shards, rows), F32),
-            jax.ShapeDtypeStruct((fetched.shape[0], rows), BF16),
+            jax.ShapeDtypeStruct((late.shape[0], rows), BF16),
+            jax.ShapeDtypeStruct((slots, rows), BF16),
         ],
         scratch_shapes=[
             pltpu.VMEM(mixed.shape, BF16),
@@ -216,14 +327,14 @@
         ],
         compiler_params=params(),
         name="score",
-    )(pack, in_hbm(mixed), fetched)
-
-
-def gradient(own, other, pack, mask, fetched, hidden, lines, total_lines, top):
+    )(pack, in_hbm(mixed), late, *early)
+
+
+def gradient(own, other, pack, masks, late, early, hidden, lines, total_lines, top, used, parts):
     count = len(pieces(hidden.shape[2]))
     return pl.pallas_call(
-        functools.partial(grad_kernel, top=top),
-        in_specs=[VMEM] * 5 + [HBM],
+        functools.partial(grad_kernel, top=top, used=used, parts=parts),
+        in_specs=[VMEM] * (6 + len(early)) + [HBM],
         out_specs=VMEM,
         out_shape=jax.ShapeDtypeStruct((own.shape[0], total_lines, 128), BF16),
         scratch_shapes=[
@@ -233,7 +344,11 @@
         ],
         compiler_params=params(),
         name="gradient",
-    )(own, other, pack, mask, fetched, in_hbm(hidden))
+    )(own, other, pack, *masks, late, *early, in_hbm(hidden))
+
+
+def after(value, first):
+    return lax.optimization_barrier((value, first))[0]
 
 
 def add_up(parts, layers, features, top, slots):
@@ -272,8 +387,10 @@
     return lax.ppermute(value, "mp", [(i, i ^ 1) for i in range(size)])
 
 
-def exchange(value):
-    return lax.all_to_all(value, "dp", split_axis=0, concat_axis=0, tiled=True)
+def exchange(value, groups=None):
+    return lax.all_to_all(
+        value, "dp", split_axis=0, concat_axis=0, tiled=True, axis_index_groups=groups
+    )
 
 
 def local(
@@ -292,7 +409,20 @@
     cores = lax.axis_size("mp")
     capacity = max(2, 2 * rows // peers)
     spread = min(rows, max(2, 3 * rows * top // (2 * peers)))
-    spread = -(-spread // 8) * 8
+    spread = -(-spread // 16) * 16
+    half = peers // 2
+    late = features - sum(CHUNKS) * features // 2048
+    place, group = lax.axis_index("dp"), lax.axis_index("groups")
+
+    count = draft_head.shape[0]
+    part = count // 2
+    chunks, start = [], late
+    for wide in CHUNKS:
+        wide = wide * features // 2048
+        near = lax.dynamic_slice(draft_head, (group * part, start), (part, wide))
+        near = lax.ppermute(near, "dp", [(i, (i + half) % peers) for i in range(peers)])
+        chunks.append((start, near))
+        start += wide
 
     shard = candidate_shard.T
     offset = candidate_offset.T
@@ -300,9 +430,37 @@
     asked = jnp.max(
         jnp.where(shard[:, None, :] == number[None], offset[:, None, :], -1), axis=0
     )
-    picked = pick(exchange(asked), draft_head, spread)
-    fetched = exchange(picked.reshape(peers, spread, features)).reshape(peers * spread, features)
-
+    partner = jnp.concatenate([asked[half:], asked[:half]], axis=0)
+    partner = jnp.where(partner >= 0, (partner + group * part) % count, -1)
+    wanted = exchange(jnp.stack([asked, partner], axis=1)).reshape(2 * peers, rows)
+
+    picked = pick(wanted, draft_head, spread, late)
+    rows_late = exchange(picked.reshape(peers, spread, late)).reshape(peers * spread, late)
+
+    few = half <= 4
+    parts = half if few else 1
+    bits = [b for b in range(peers.bit_length() - 1) if few or 1 << b == half]
+    used = [b in bits for b in range(peers.bit_length() - 1)]
+    flags = [(place >> b) & 1 if use else None for b, use in enumerate(used)]
+    wanted = lax.dynamic_slice(wanted, (place // half * half * 2, 0), (half * 2, rows))
+    wanted = swapped(wanted, [None] + [None if flag is None else flag > 0 for flag in flags[:-1]])
+    rows_early = []
+    for start, near in chunks:
+        near = after(near, picked)
+        far = lax.ppermute(near, "groups", [(0, 1), (1, 0)])
+        rows_here = list(pick_early(wanted, draft_head, near, far, spread, start, parts))
+        if few:
+            for i in range(1, half):
+                rows_here[i] = lax.ppermute(rows_here[i], "dp", [(j, j ^ i) for j in range(peers)])
+        else:
+            halves = [list(range(half)), list(range(half, peers))]
+            rows_here = exchange(rows_here[0].reshape(half, 2 * spread, -1), halves)
+            rows_here = [rows_here.reshape(peers * spread, -1)]
+        rows_early += rows_here
+
+    hidden, row_owner, shard, target_logits, lengths, layer_mix = after(
+        (hidden, row_owner, shard, target_logits, lengths, layer_mix), picked
+    )
     tokens = hidden.transpose(1, 0, 2)
     wide = tokens.astype(F32)
     squares = jnp.sum(wide * wide, axis=2)
@@ -317,16 +475,22 @@
     owner = row_owner.T
     same = (owner.T == owner) & (iota((rows, rows), 1) < iota((rows, rows), 0))
     column = lax.axis_index("dp") * capacity + jnp.sum(same.astype(jnp.int32), axis=1)[None, :]
-    pack = [asked, shard, target, weight, owner, column, inverse]
+    held = [jnp.full((1, rows), 0 if flag is None else flag, jnp.int32) for flag in flags]
+    held = jnp.pad(jnp.concatenate(held, axis=0), ((0, 8 - len(held)), (0, 0)))
+    pairs = to_pairs(asked, [None if flag is None else flag > 0 for flag in flags])
+    pack = [asked, pairs, held, shard, target, weight, owner, column, inverse]
     pack = jnp.concatenate([value.astype(F32) for value in pack], axis=0)
     pack = jnp.pad(pack, ((0, -pack.shape[0] % 8), (0, 0)))
 
     slots = peers * capacity
     lines = layers * features // 128
     total_lines = lines + 2 * top * slots // 128
-    own, mask = score(pack, mixed, fetched, peers)
-    parts = gradient(own, swap_cores(own), pack, mask, fetched, tokens, lines, total_lines, top)
-    grad, logp = add_up(exchange(parts), layers, features, top, slots)
+    own, *masks = score(pack, mixed, rows_late, rows_early, peers, used, parts)
+    other = swap_cores(own)
+    sent = gradient(
+        own, other, pack, masks, rows_late, rows_early, tokens, lines, total_lines, top, used, parts
+    )
+    grad, logp = add_up(exchange(sent), layers, features, top, slots)
     return (logp.T[None], grad)
 
 

time: 110 us -> 96.4 us (0.88)
  waiting for transfers between devices: 64.8 us -> 30.2 us
  starting transfers between devices: 3.93 us -> 30.5 us
  blocking collectives: 24.3 us -> 13.3 us
  local copies, waits for them, and re-layouts: 0.08 us -> 3.17 us
  Pallas kernels: 9.54 us -> 12.6 us
  other arithmetic: 6.34 us -> 5.1 us
    all_to_all x1 -> x2, waiting for transfers between devices: 63.2 us -> 9.53 us  [exchange(): lax.all_to_all(value, 'dp', split_axis=0, concat_axis=0, tiled=True, axis...]
    ppermute x0 -> x10, starting transfers between devices: none -> 19.4 us  [the longest x6 14.1 us: local(): lax.ppermute(rows_here[i], 'dp', [(j, j ^ i) for j in range(peers)])]
    ppermute x0 -> x10, waiting for transfers between devices: none -> 18.9 us  [the longest x6 15.2 us: local(): lax.ppermute(rows_here[i], 'dp', [(j, j ^ i) for j in range(peers)])]
    all_to_all x2 -> x1, blocking collectives: 24.3 us -> 13.3 us  [exchange(): lax.all_to_all(value, 'dp', split_axis=0, concat_axis=0, tiled=True, axis...]
    all_to_all x1 -> x2, starting transfers between devices: 3.79 us -> 11 us  [exchange(): lax.all_to_all(value, 'dp', split_axis=0, concat_axis=0, tiled=True, axis...]
    pallas_call x2 -> x4, Pallas kernels: 4.55 us -> 8.11 us  [the longest x2 3.54 us: pick_early(): pl.pallas_call(functools.partial(early_kernel, spread=spread, start=start...]
    reduce_sum x1, other arithmetic: 1.95 us -> 0.45 us  [local(): mixed = jnp.sum(wide * layer_mix[:, None, :] * inverse[:, :, None], axis=0)]
    unnamed x10 -> x20, local copies, waits for them, and re-layouts: 0.03 us -> 1.35 us
  transfers between devices with their start and end apart: 3 -> 14, of which waited for: 3 -> 9; matrix products, arithmetic and copies ran while one was open for 5% -> 6% of each run, Pallas kernels for 0% -> 8%
where the time goes in v3:
time: 96.4 us; the launch traced here: 95.9 us
  starting transfers between devices  30.5 us (32%)
  waiting for transfers between devices  30.2 us (31%)
  blocking collectives  13.3 us (14%)
  Pallas kernels  12.6 us (13%)
  other arithmetic  5.1 us (5%)
  local copies, waits for them, and re-layouts  3.17 us (3%)
  between operations  0.99 us (1%)
    ppermute x6, waiting for transfers between devices, local(): lax.ppermute(rows_here[i], 'dp', [(j, j ^ i) for j in range(peers)])  15.2 us
    ppermute x6, starting transfers between devices, local(): lax.ppermute(rows_here[i], 'dp', [(j, j ^ i) for j in range(peers)])  14.1 us
    all_to_all x1, blocking collectives, exchange(): lax.all_to_all(value, 'dp', split_axis=0, concat_axis=0, tiled=True, axis...  13.3 us
    all_to_all x2, starting transfers between devices, exchange(): lax.all_to_all(value, 'dp', split_axis=0, concat_axis=0, tiled=True, axis...  11 us
    all_to_all x2, waiting for transfers between devices, exchange(): lax.all_to_all(value, 'dp', split_axis=0, concat_axis=0, tiled=True, axis...  9.53 us
    pallas_call x1, Pallas kernels, pick(): pl.pallas_call(functools.partial(pick_kernel, spread=spread), in_specs=[V...  3.81 us
    ppermute x2, waiting for transfers between devices, local(): far = lax.ppermute(near, 'groups', [(0, 1), (1, 0)])  3.78 us
    pallas_call x2, Pallas kernels, pick_early(): pl.pallas_call(functools.partial(early_kernel, spread=spread, start=start...  3.54 us
  transfers between devices with their start and end apart: 14, of which 9 were waited for; matrix products, arithmetic and copies ran while one was open for 6% of the time, Pallas kernels for 8%

profile of v3, /device:TPU:0, one launch (start us, length us, event | category | flops | bytes accessed | tf_op | source)
XLA Modules:
  0.0 95.9 jit_solution(4032284930724481414)
XLA Ops:
  0.6 0.7 select_reduce_fusion
  1.4 0.6 copy.12
  2.0 7.3 %all-to-all-start = ((s32[8,2,128]{2,1,0:T(2,128)}), s32[8,2,128]{2,1,0:T(2,128)S(1)}, u32[]{:S(2)}, u32[]{:S(2)}) async-start(s32[8,2,128]{2,1,0:T(2,128)} %copy.12), calls=%async_computation | async-start | bytes 16384 | tf_op jit(solution)/shard_map/all_to_all | solution.py:391
  9.2 1.0 %constant_dynamic-slice_fusion = (bf16[256,256]{1,0:T(8,128)(2,1)S(1)}, bf16[256,256]{1,0:T(8,128)(2,1)S(1)}) fusion(bf16[512,2048]{1,0:T(8,128)(2,1)} %head_hbm.5, s32[]{:T(128)S(6)} %select_n.103), kind=kLoop, calls=%fused_computation.43 | loop fusion | bytes 524292 | tf_op jit(solution)/shard_map/dynamic_slice | solution.py:422
  10.2 3.0 %collective-permute-start.6 = (bf16[256,256]{1,0:T(8,128)(2,1)S(1)}, bf16[256,256]{1,0:T(8,128)(2,1)S(1)}, u32[]{:S(2)}, u32[]{:S(2)}) collective-permute-start(bf16[256,256]{1,0:T(8,128)(2,1)S(1)} %get-tuple-element.44), channel_id=1, source_target_pairs={{0,8},{2,10},{4,12},{6,14},{8,0},{10,2},{12,4},{14,6},{1,9},{3,11}... | collective-permute-start | bytes 393224 | tf_op jit(solution)/shard_map/ppermute | solution.py:423
  13.4 2.5 %all-to-all-done = s32[8,2,128]{2,1,0:T(2,128)S(1)} async-done(((s32[8,2,128]{2,1,0:T(2,128)}), s32[8,2,128]{2,1,0:T(2,128)S(1)}, u32[]{:S(2)}, u32[]{:S(2)}) %all-to-all-start) | async-done | bytes 8224 | tf_op jit(solution)/shard_map/all_to_all | solution.py:391
  15.9 3.8 %pick.1 = bf16[768,1536]{1,0:T(8,128)(2,1)} custom-call(s32[16,128]{1,0:T(8,128)S(1)} %bitcast.36, bf16[512,2048]{1,0:T(8,128)(2,1)} %head_hbm.5), custom_call_target="tpu_custom_call" | custom-call | tf_op jit(solution)/shard_map/pick/pallas_call | solution.py:278
  19.8 3.8 %all-to-all-start.1 = ((bf16[8,96,1536]{2,1,0:T(8,128)(2,1)}), bf16[8,96,1536]{2,1,0:T(8,128)(2,1)S(1)}, u32[]{:S(2)}, u32[]{:S(2)}) async-start(bf16[8,96,1536]{2,1,0:T(8,128)(2,1)} %bitcast.40), calls=%async_computation.1 | async-start | bytes 4718592 | tf_op jit(solution)/shard_map/all_to_all | solution.py:391
  23.9 1.9 %fusion = f32[3,128]{1,0:T(4,128)S(1)} fusion(bf16[128,3,2048]{2,0,1:T(8,128)(2,1)} %param.8), kind=kLoop, calls=%fused_computation.2 | loop fusion | flops 2358912 | bytes 1574400 | tf_op jit(solution)/shard_map/reduce_sum | solution.py:466
  26.4 0.6 collective-permute-done
  27.1 1.6 %collective-permute-start.2 = (bf16[256,256]{1,0:T(8,128)(2,1)S(1)}, bf16[256,256]{1,0:T(8,128)(2,1)S(1)}, u32[]{:S(2)}, u32[]{:S(2)}) collective-permute-start(bf16[256,256]{1,0:T(8,128)(2,1)S(1)} %collective-permute-done.1.near_hbm), channel_id=1, source_target_pairs={{0,16},{16,0},{1,17},{17,1},{2,18},{18,2},{3,19},{19,3},{4,20},{20... | collective-permute-start | bytes 393224 | tf_op jit(solution)/shard_map/ppermute | solution.py:450
  29.1 0.6 collective-permute-start.7
  29.7 3.8 %collective-permute-done.2.far_hbm = bf16[256,256]{1,0:T(8,128)(2,1)S(1)} collective-permute-done((bf16[256,256]{1,0:T(8,128)(2,1)S(1)}, bf16[256,256]{1,0:T(8,128)(2,1)S(1)}, u32[]{:S(2)}, u32[]{:S(2)}) %collective-permute-start.2) | collective-permute-done | bytes 131104 | tf_op jit(solution)/shard_map/ppermute | solution.py:450
  33.5 0.6 copy-done.4
  34.1 1.5 %pick_early.2 = (bf16[192,256]{1,0:T(8,128)(2,1)S(1)}, bf16[192,256]{1,0:T(8,128)(2,1)S(1)}, bf16[192,256]{1,0:T(8,128)(2,1)S(1)}, bf16[192,256]{1,0:T(8,128)(2,1)S(1)}) custom-call(s32[8,128]{1,0:T(8,128)S(1)} %add_select_fusion.4.asked_ref, bf16[512,2048]{1,0:T(8,128)(2,1)} %head_hbm.5, bf16[256,256]{1,0:T(8,128)(2,1)} %copy-done.2, bf16[256,256]{1,0:T(8,128)(2,1)} %copy-done.4), custom_call_target="tpu_custom_call" | custom-call | tf_op jit(solution)/shard_map/pick_early/pallas_call | solution.py:297
  35.6 2.0 %collective-permute-start.3 = (bf16[192,256]{1,0:T(8,128)(2,1)S(1)}, bf16[192,256]{1,0:T(8,128)(2,1)S(1)}, u32[]{:S(2)}, u32[]{:S(2)}) collective-permute-start(bf16[192,256]{1,0:T(8,128)(2,1)S(1)} %get-tuple-element.31), channel_id=1, source_target_pairs={{0,2},{2,0},{4,6},{6,4},{8,10},{10,8},{12,14},{14,12},{1,3},{3,1},... | collective-permute-start | bytes 294920 | tf_op jit(solution)/shard_map/ppermute | solution.py:454
  37.7 8.6 %collective-permute-start.4 = (bf16[192,256]{1,0:T(8,128)(2,1)S(1)}, bf16[192,256]{1,0:T(8,128)(2,1)S(1)}, u32[]{:S(2)}, u32[]{:S(2)}) collective-permute-start(bf16[192,256]{1,0:T(8,128)(2,1)S(1)} %get-tuple-element.32), channel_id=1, source_target_pairs={{0,4},{2,6},{4,0},{6,2},{8,12},{10,14},{12,8},{14,10},{1,5},{3,7},... | collective-permute-start | bytes 294920 | tf_op jit(solution)/shard_map/ppermute | solution.py:454
  46.4 0.7 copy-done.3
  47.0 2.1 %pick_early.3 = (bf16[192,256]{1,0:T(8,128)(2,1)S(1)}, bf16[192,256]{1,0:T(8,128)(2,1)}, bf16[192,256]{1,0:T(8,128)(2,1)}, bf16[192,256]{1,0:T(8,128)(2,1)S(1)}) custom-call(s32[8,128]{1,0:T(8,128)S(1)} %add_select_fusion.4.asked_ref, bf16[512,2048]{1,0:T(8,128)(2,1)} %head_hbm.5, bf16[256,256]{1,0:T(8,128)(2,1)} %copy-done.1, bf16[256,256]{1,0:T(8,128)(2,1)} %copy-done.3), custom_call_target="tpu_custom_call" | custom-call | tf_op jit(solution)/shard_map/pick_early/pallas_call | solution.py:297
  49.1 1.6 %collective-permute-start.8 = (bf16[192,256]{1,0:T(8,128)(2,1)}, bf16[192,256]{1,0:T(8,128)(2,1)S(1)}, u32[]{:S(2)}, u32[]{:S(2)}) collective-permute-start(bf16[192,256]{1,0:T(8,128)(2,1)} %get-tuple-element.36), channel_id=1, source_target_pairs={{0,2},{2,0},{4,6},{6,4},{8,10},{10,8},{12,14},{14,12},{1,3},{3,1},... | collective-permute-start | bytes 294920 | tf_op jit(solution)/shard_map/ppermute | solution.py:454
  50.7 1.9 %collective-permute-start.9 = (bf16[192,256]{1,0:T(8,128)(2,1)}, bf16[192,256]{1,0:T(8,128)(2,1)S(1)}, u32[]{:S(2)}, u32[]{:S(2)}) collective-permute-start(bf16[192,256]{1,0:T(8,128)(2,1)} %get-tuple-element.37), channel_id=1, source_target_pairs={{0,4},{2,6},{4,0},{6,2},{8,12},{10,14},{12,8},{14,10},{1,5},{3,7},... | collective-permute-start | bytes 294920 | tf_op jit(solution)/shard_map/ppermute | solution.py:454
  52.7 1.1 %pad_maximum_fusion.mixed_hbm = bf16[256,2048]{1,0:T(8,128)(2,1)} fusion(bf16[128,2048]{1,0:T(8,128)(2,1)S(1)} %get-tuple-element.47, bf16[128,2048]{1,0:T(8,128)(2,1)S(1)} %get-tuple-element.46), kind=kLoop, calls=%fused_computation.8 | loop fusion | flops 2097152 | bytes 2097152 | tf_op jit(solution)/shard_map/concatenate | solution.py:471
  53.9 11.2 %collective-permute-done.4.refs_2_ = bf16[192,256]{1,0:T(8,128)(2,1)S(1)} collective-permute-done((bf16[192,256]{1,0:T(8,128)(2,1)S(1)}, bf16[192,256]{1,0:T(8,128)(2,1)S(1)}, u32[]{:S(2)}, u32[]{:S(2)}) %collective-permute-start.4) | collective-permute-done | bytes 98336 | tf_op jit(solution)/shard_map/ppermute | solution.py:454
  65.1 1.8 %collective-permute-done.5.refs_3_ = bf16[192,256]{1,0:T(8,128)(2,1)S(1)} collective-permute-done((bf16[192,256]{1,0:T(8,128)(2,1)S(1)}, bf16[192,256]{1,0:T(8,128)(2,1)S(1)}, u32[]{:S(2)}, u32[]{:S(2)}) %collective-permute-start.5) | collective-permute-done | bytes 98336 | tf_op jit(solution)/shard_map/ppermute | solution.py:454
  66.9 1.2 %collective-permute-done.9.refs_6_ = bf16[192,256]{1,0:T(8,128)(2,1)S(1)} collective-permute-done((bf16[192,256]{1,0:T(8,128)(2,1)}, bf16[192,256]{1,0:T(8,128)(2,1)S(1)}, u32[]{:S(2)}, u32[]{:S(2)}) %collective-permute-start.9) | collective-permute-done | bytes 98336 | tf_op jit(solution)/shard_map/ppermute | solution.py:454
  68.1 0.9 collective-permute-done.10.refs_7_
  69.1 7.0 %all-to-all-done.1 = bf16[8,96,1536]{2,1,0:T(8,128)(2,1)S(1)} async-done(((bf16[8,96,1536]{2,1,0:T(8,128)(2,1)}), bf16[8,96,1536]{2,1,0:T(8,128)(2,1)S(1)}, u32[]{:S(2)}, u32[]{:S(2)}) %all-to-all-start.1) | async-done | bytes 2359328 | tf_op jit(solution)/shard_map/all_to_all | solution.py:391
  76.1 2.4 %score.1 = (f32[8,128]{1,0:T(8,128)S(1)}, bf16[768,128]{1,0:T(8,128)(2,1)S(1)}, bf16[768,128]{1,0:T(8,128)(2,1)S(1)}) custom-call(f32[40,128]{1,0:T(8,128)S(1)} %pad.9.pack_ref, bf16[256,2048]{1,0:T(8,128)(2,1)} %pad_maximum_fusion.mixed_hbm, bf16[768,1536]{1,0:T(8,128)(2,1)S(1)} %bitcast.34, bf16[192,256]{1,0:T(8,128)(2,1)S(1)} %get-tuple-element.30.refs_0_, ...), custom_call_target="tpu_custom_call" | custom-call | tf_op jit(solution)/shard_map/score/pallas_call | solution.py:315
  78.6 1.2 %collective-permute-done.11.other_ref = f32[8,128]{1,0:T(8,128)S(1)} collective-permute-done((f32[8,128]{1,0:T(8,128)S(1)}, f32[8,128]{1,0:T(8,128)S(1)}, u32[]{:S(2)}, u32[]{:S(2)}) %collective-permute-start.11) | collective-permute-done | bytes 4128 | tf_op jit(solution)/shard_map/ppermute | solution.py:387
  79.7 2.2 %gradient.1 = bf16[8,64,128]{2,1,0:T(8,128)(2,1)S(1)} custom-call(f32[8,128]{1,0:T(8,128)S(1)} %get-tuple-element.39.own_ref, f32[8,128]{1,0:T(8,128)S(1)} %collective-permute-done.11.other_ref, f32[40,128]{1,0:T(8,128)S(1)} %pad.9.pack_ref, bf16[768,128]{1,0:T(8,128)(2,1)S(1)} %get-tuple-element.40.late_mask_ref, ...), custom_call_target="tpu_custom_call" | custom-call | tf_op jit(solution)/shard_map/gradient/pallas_call | solution.py:335
  81.9 13.3 %all_to_all.15.parts_ref = bf16[8,64,128]{2,1,0:T(8,128)(2,1)S(1)} all-to-all(bf16[8,64,128]{2,1,0:T(8,128)(2,1)S(1)} %gradient.1), channel_id=1, replica_groups=mesh['groups'=2,'dp'=8,'mp'=2] {'dp'}, dimensions={0} | all-to-all | bytes 262144 | tf_op jit(solution)/shard_map/all_to_all | solution.py:391
  95.3 0.6 add_up.1
  (67 shorter events, 1.9 us)
Async XLA Ops:
  2.0 13.9 %all-to-all-start = ((s32[8,2,128]{2,1,0:T(2,128)}), s32[8,2,128]{2,1,0:T(2,128)S(1)}, u32[]{:S(2)}, u32[]{:S(2)}) async-start(s32[8,2,128]{2,1,0:T(2,128)} %copy.12), calls=%async_computation | async-start | bytes 16384 | tf_op jit(solution)/shard_map/all_to_all | solution.py:391
  10.2 18.9 %collective-permute-start.6 = (bf16[256,256]{1,0:T(8,128)(2,1)S(1)}, bf16[256,256]{1,0:T(8,128)(2,1)S(1)}, u32[]{:S(2)}, u32[]{:S(2)}) collective-permute-start(bf16[256,256]{1,0:T(8,128)(2,1)S(1)} %get-tuple-element.44), channel_id=1, source_target_pairs={{0,8},{2,10},{4,12},{6,14},{8,0},{10,2},{12,4},{14,6},{1,9},{3,11}... | collective-permute-start | bytes 393224 | tf_op jit(solution)/shard_map/ppermute | solution.py:423
  13.2 13.8 %collective-permute-start.1 = (bf16[256,256]{1,0:T(8,128)(2,1)S(1)}, bf16[256,256]{1,0:T(8,128)(2,1)S(1)}, u32[]{:S(2)}, u32[]{:S(2)}) collective-permute-start(bf16[256,256]{1,0:T(8,128)(2,1)S(1)} %get-tuple-element.45), channel_id=1, source_target_pairs={{0,8},{2,10},{4,12},{6,14},{8,0},{10,2},{12,4},{14,6},{1,9},{3,11}... | collective-permute-start | bytes 393224 | tf_op jit(solution)/shard_map/ppermute | solution.py:423
  19.7 4.0 %copy-start.8 = (s32[1,4]{1,0:T(1,128)S(1)}, s32[1,4]{1,0:T(1,128)}, u32[]{:S(2)}) copy-start(s32[1,4]{1,0:T(1,128)} %param.13) | copy-start | bytes 52
  19.7 4.2 %copy-start.6 = (bf16[128,4]{0,1:T(4,128)(2,1)S(1)}, bf16[128,4]{0,1:T(4,128)(2,1)}, u32[]{:S(2)}) copy-start(bf16[128,4]{0,1:T(4,128)(2,1)} %param.12) | copy-start | bytes 3076
  19.7 6.2 %copy-start.9 = (s32[128,1]{0,1:T(1,128)S(1)}, s32[128,1]{0,1:T(1,128)}, u32[]{:S(2)}) copy-start(s32[128,1]{0,1:T(1,128)} %param.9) | copy-start | bytes 1540
  19.7 6.7 %copy-start.7 = (s32[128,4]{0,1:T(4,128)S(1)}, s32[128,4]{0,1:T(4,128)}, u32[]{:S(2)}) copy-start(s32[128,4]{0,1:T(4,128)} %param.10) | copy-start | bytes 6148
  19.8 8.9 %copy-start.5 = (f32[3,2048]{1,0:T(4,128)S(1)}, f32[3,2048]{1,0:T(4,128)}, u32[]{:S(2)}) copy-start(f32[3,2048]{1,0:T(4,128)} %param.14) | copy-start | bytes 73732
  19.8 56.3 %all-to-all-start.1 = ((bf16[8,96,1536]{2,1,0:T(8,128)(2,1)}), bf16[8,96,1536]{2,1,0:T(8,128)(2,1)S(1)}, u32[]{:S(2)}, u32[]{:S(2)}) async-start(bf16[8,96,1536]{2,1,0:T(8,128)(2,1)} %bitcast.40), calls=%async_computation.1 | async-start | bytes 4718592 | tf_op jit(solution)/shard_map/all_to_all | solution.py:391
  23.9 4.8 %copy-start = (bf16[128,3,2048]{2,0,1:T(8,128)(2,1)S(1)}, bf16[128,3,2048]{2,0,1:T(8,128)(2,1)}, u32[]{:S(2)}) copy-start(bf16[128,3,2048]{2,0,1:T(8,128)(2,1)} %param.8) | copy-start | bytes 4718596
  25.8 1.2 %collective-permute-start = (f32[3,128]{1,0:T(4,128)S(1)}, f32[3,128]{1,0:T(4,128)S(1)}, u32[]{:S(2)}, u32[]{:S(2)}) collective-permute-start(f32[3,128]{1,0:T(4,128)S(1)} %fusion), channel_id=1, source_target_pairs={{0,1},{1,0},{2,3},{3,2},{4,5},{5,4},{6,7},{7,6},{8,9},{9,8},{10,11... | collective-permute-start | bytes 4616 | tf_op jit(solution)/shard_map/ppermute | solution.py:387
  27.1 6.4 %copy-start.2 = (bf16[256,256]{1,0:T(8,128)(2,1)}, bf16[256,256]{1,0:T(8,128)(2,1)S(1)}, u32[]{:S(2)}) copy-start(bf16[256,256]{1,0:T(8,128)(2,1)S(1)} %collective-permute-done.1.near_hbm) | copy-start | bytes 393220
  27.1 6.4 %collective-permute-start.2 = (bf16[256,256]{1,0:T(8,128)(2,1)S(1)}, bf16[256,256]{1,0:T(8,128)(2,1)S(1)}, u32[]{:S(2)}, u32[]{:S(2)}) collective-permute-start(bf16[256,256]{1,0:T(8,128)(2,1)S(1)} %collective-permute-done.1.near_hbm), channel_id=1, source_target_pairs={{0,16},{16,0},{1,17},{17,1},{2,18},{18,2},{3,19},{19,3},{4,20},{20... | collective-permute-start | bytes 393224 | tf_op jit(solution)/shard_map/ppermute | solution.py:450
  29.1 17.2 %copy-start.1 = (bf16[256,256]{1,0:T(8,128)(2,1)}, bf16[256,256]{1,0:T(8,128)(2,1)S(1)}, u32[]{:S(2)}) copy-start(bf16[256,256]{1,0:T(8,128)(2,1)S(1)} %collective-permute-done.6.near_hbm) | copy-start | bytes 393220
  29.1 17.2 %collective-permute-start.7 = (bf16[256,256]{1,0:T(8,128)(2,1)S(1)}, bf16[256,256]{1,0:T(8,128)(2,1)S(1)}, u32[]{:S(2)}, u32[]{:S(2)}) collective-permute-start(bf16[256,256]{1,0:T(8,128)(2,1)S(1)} %collective-permute-done.6.near_hbm), channel_id=1, source_target_pairs={{0,16},{16,0},{1,17},{17,1},{2,18},{18,2},{3,19},{19,3},{4,20},{20... | collective-permute-start | bytes 393224 | tf_op jit(solution)/shard_map/ppermute | solution.py:450
  33.5 0.6 copy-start.4
  35.6 17.1 %collective-permute-start.3 = (bf16[192,256]{1,0:T(8,128)(2,1)S(1)}, bf16[192,256]{1,0:T(8,128)(2,1)S(1)}, u32[]{:S(2)}, u32[]{:S(2)}) collective-permute-start(bf16[192,256]{1,0:T(8,128)(2,1)S(1)} %get-tuple-element.31), channel_id=1, source_target_pairs={{0,2},{2,0},{4,6},{6,4},{8,10},{10,8},{12,14},{14,12},{1,3},{3,1},... | collective-permute-start | bytes 294920 | tf_op jit(solution)/shard_map/ppermute | solution.py:454
  37.7 27.4 %collective-permute-start.4 = (bf16[192,256]{1,0:T(8,128)(2,1)S(1)}, bf16[192,256]{1,0:T(8,128)(2,1)S(1)}, u32[]{:S(2)}, u32[]{:S(2)}) collective-permute-start(bf16[192,256]{1,0:T(8,128)(2,1)S(1)} %get-tuple-element.32), channel_id=1, source_target_pairs={{0,4},{2,6},{4,0},{6,2},{8,12},{10,14},{12,8},{14,10},{1,5},{3,7},... | collective-permute-start | bytes 294920 | tf_op jit(solution)/shard_map/ppermute | solution.py:454
  46.3 20.6 %collective-permute-start.5 = (bf16[192,256]{1,0:T(8,128)(2,1)S(1)}, bf16[192,256]{1,0:T(8,128)(2,1)S(1)}, u32[]{:S(2)}, u32[]{:S(2)}) collective-permute-start(bf16[192,256]{1,0:T(8,128)(2,1)S(1)} %get-tuple-element.33), channel_id=1, source_target_pairs={{0,6},{2,4},{4,2},{6,0},{8,14},{10,12},{12,10},{14,8},{1,7},{3,5},... | collective-permute-start | bytes 294920 | tf_op jit(solution)/shard_map/ppermute | solution.py:454
  46.4 0.7 copy-start.3
  49.1 17.8 %collective-permute-start.8 = (bf16[192,256]{1,0:T(8,128)(2,1)}, bf16[192,256]{1,0:T(8,128)(2,1)S(1)}, u32[]{:S(2)}, u32[]{:S(2)}) collective-permute-start(bf16[192,256]{1,0:T(8,128)(2,1)} %get-tuple-element.36), channel_id=1, source_target_pairs={{0,2},{2,0},{4,6},{6,4},{8,10},{10,8},{12,14},{14,12},{1,3},{3,1},... | collective-permute-start | bytes 294920 | tf_op jit(solution)/shard_map/ppermute | solution.py:454
  50.7 17.4 %collective-permute-start.9 = (bf16[192,256]{1,0:T(8,128)(2,1)}, bf16[192,256]{1,0:T(8,128)(2,1)S(1)}, u32[]{:S(2)}, u32[]{:S(2)}) collective-permute-start(bf16[192,256]{1,0:T(8,128)(2,1)} %get-tuple-element.37), channel_id=1, source_target_pairs={{0,4},{2,6},{4,0},{6,2},{8,12},{10,14},{12,8},{14,10},{1,5},{3,7},... | collective-permute-start | bytes 294920 | tf_op jit(solution)/shard_map/ppermute | solution.py:454
  52.7 16.4 %collective-permute-start.10 = (bf16[192,256]{1,0:T(8,128)(2,1)S(1)}, bf16[192,256]{1,0:T(8,128)(2,1)S(1)}, u32[]{:S(2)}, u32[]{:S(2)}) collective-permute-start(bf16[192,256]{1,0:T(8,128)(2,1)S(1)} %get-tuple-element.38), channel_id=1, source_target_pairs={{0,6},{2,4},{4,2},{6,0},{8,14},{10,12},{12,10},{14,8},{1,7},{3,5},... | collective-permute-start | bytes 294920 | tf_op jit(solution)/shard_map/ppermute | solution.py:454
  78.5 1.2 %collective-permute-start.11 = (f32[8,128]{1,0:T(8,128)S(1)}, f32[8,128]{1,0:T(8,128)S(1)}, u32[]{:S(2)}, u32[]{:S(2)}) collective-permute-start(f32[8,128]{1,0:T(8,128)S(1)} %get-tuple-element.39.own_ref), channel_id=1, source_target_pairs={{0,1},{1,0},{2,3},{3,2},{4,5},{5,4},{6,7},{7,6},{8,9},{9,8},{10,11... | collective-permute-start | bytes 12296 | tf_op jit(solution)/shard_map/ppermute | solution.py:387

commit v4 on v3

--- a/solution.py
+++ b/solution.py
@@ -11,8 +11,8 @@
 HIGHEST = lax.Precision.HIGHEST
 F32 = jnp.float32
 BF16 = jnp.bfloat16
-VMEM_LIMIT = 40 * 1024 * 1024
-CHUNKS = (256, 256)
+VMEM_LIMIT = 16 * 1024 * 1024
+CHUNKS = (384, 256)
 
 
 def iota(shape, axis):
@@ -167,8 +167,7 @@
 def grad_kernel(
     own_ref, other_ref, pack_ref, late_mask_ref, early_mask_ref, late_ref, *refs, top, used, parts
 ):
-    *early_refs, hidden_hbm, out_ref, hidden_ref, grad_ref, sems = refs
-    arrivals = fetch(hidden_hbm, hidden_ref, sems)
+    *early_refs, hidden_ref, out_ref, grad_ref = refs
     layers, rows, features = hidden_ref.shape
     shards = own_ref.shape[0]
     lines = grad_ref.shape[0]
@@ -208,8 +207,6 @@
     sources = [([late_ref], [spread_out(late_mask_ref[...], by_shard)], 0)]
     for group, start in chunks_of(early_refs, parts, late):
         sources.append((group, part, start))
-    for copy in arrivals:
-        copy.wait()
     for rows_refs, grads, start in sources:
         for cut in pieces(rows_refs[0].shape[1]):
             carried = sum(
@@ -331,20 +328,17 @@
 
 
 def gradient(own, other, pack, masks, late, early, hidden, lines, total_lines, top, used, parts):
-    count = len(pieces(hidden.shape[2]))
     return pl.pallas_call(
         functools.partial(grad_kernel, top=top, used=used, parts=parts),
-        in_specs=[VMEM] * (6 + len(early)) + [HBM],
+        in_specs=[VMEM] * (7 + len(early)),
         out_specs=VMEM,
         out_shape=jax.ShapeDtypeStruct((own.shape[0], total_lines, 128), BF16),
         scratch_shapes=[
-            pltpu.VMEM(hidden.shape, BF16),
             pltpu.VMEM((lines, 128), F32),
-            pltpu.SemaphoreType.DMA((count,)),
         ],
         compiler_params=params(),
         name="gradient",
-    )(own, other, pack, *masks, late, *early, in_hbm(hidden))
+    )(own, other, pack, *masks, late, *early, hidden)
 
 
 def after(value, first):
@@ -426,13 +420,11 @@
 
     shard = candidate_shard.T
     offset = candidate_offset.T
-    number = jnp.arange(peers, dtype=jnp.int32)[:, None]
-    asked = jnp.max(
-        jnp.where(shard[:, None, :] == number[None], offset[:, None, :], -1), axis=0
-    )
-    partner = jnp.concatenate([asked[half:], asked[:half]], axis=0)
-    partner = jnp.where(partner >= 0, (partner + group * part) % count, -1)
-    wanted = exchange(jnp.stack([asked, partner], axis=1)).reshape(2 * peers, rows)
+    line = jnp.arange(2 * peers, dtype=jnp.int32)[:, None]
+    number = (line // 2 + line % 2 * half) % peers
+    placed = (offset[:, None, :] + line[None] % 2 * (group * part)) % count
+    message = jnp.max(jnp.where(shard[:, None, :] == number[None], placed, -1), axis=0)
+    wanted = exchange(message.reshape(peers, 2, rows)).reshape(2 * peers, rows)
 
     picked = pick(wanted, draft_head, spread, late)
     rows_late = exchange(picked.reshape(peers, spread, late)).reshape(peers * spread, late)
@@ -458,8 +450,10 @@
             rows_here = [rows_here.reshape(peers * spread, -1)]
         rows_early += rows_here
 
-    hidden, row_owner, shard, target_logits, lengths, layer_mix = after(
-        (hidden, row_owner, shard, target_logits, lengths, layer_mix), picked
+    hidden, layer_mix = after((hidden, layer_mix), picked)
+    number = jnp.arange(peers, dtype=jnp.int32)[:, None]
+    asked = jnp.max(
+        jnp.where(shard[:, None, :] == number[None], offset[:, None, :], -1), axis=0
     )
     tokens = hidden.transpose(1, 0, 2)
     wide = tokens.astype(F32)

time: 96.4 us -> 93.4 us (0.969)
  starting transfers between devices: 30.5 us -> 26 us
  other arithmetic: 5.1 us -> 9.04 us
  blocking collectives: 13.3 us -> 10.8 us
    ppermute x6, starting transfers between devices: 14.1 us -> 7.22 us  [local(): lax.ppermute(rows_here[i], 'dp', [(j, j ^ i) for j in range(peers)])]
    all_to_all x2, waiting for transfers between devices: 9.53 us -> 4.04 us  [exchange(): lax.all_to_all(value, 'dp', split_axis=0, concat_axis=0, tiled=True, axis...]
    ppermute x6, waiting for transfers between devices: 15.2 us -> 20.1 us  [local(): lax.ppermute(rows_here[i], 'dp', [(j, j ^ i) for j in range(peers)])]
    all_to_all x1, blocking collectives: 13.3 us -> 10.8 us  [exchange(): lax.all_to_all(value, 'dp', split_axis=0, concat_axis=0, tiled=True, axis...]
    all_to_all x2, starting transfers between devices: 11 us -> 13.4 us  [exchange(): lax.all_to_all(value, 'dp', split_axis=0, concat_axis=0, tiled=True, axis...]
    reduce_max x0 -> x1, other arithmetic: none -> 1.39 us  [local(): jnp.max(jnp.where(shard[:, None, :] == number[None], placed, -1), axis=0)]
    pallas_call x1, Pallas kernels: 2.18 us -> 1.04 us  [gradient(): pl.pallas_call(functools.partial(grad_kernel, top=top, used=used, parts=p...]
  transfers between devices with their start and end apart: 14 -> 14, of which waited for: 9 -> 8; matrix products, arithmetic and copies ran while one was open for 6% -> 10% of each run, Pallas kernels for 8% -> 9%
where the time goes in v4:
time: 93.4 us; the launch traced here: 92.8 us
  waiting for transfers between devices  30.1 us (32%)
  starting transfers between devices  26 us (28%)
  Pallas kernels  12.4 us (13%)
  blocking collectives  10.8 us (12%)
  other arithmetic  9.04 us (10%)
  local copies, waits for them, and re-layouts  3.48 us (4%)
  between operations  1 us (1%)
    ppermute x6, waiting for transfers between devices, local(): lax.ppermute(rows_here[i], 'dp', [(j, j ^ i) for j in range(peers)])  20.1 us
    all_to_all x2, starting transfers between devices, exchange(): lax.all_to_all(value, 'dp', split_axis=0, concat_axis=0, tiled=True, axis...  13.4 us
    all_to_all x1, blocking collectives, exchange(): lax.all_to_all(value, 'dp', split_axis=0, concat_axis=0, tiled=True, axis...  10.8 us
    ppermute x6, starting transfers between devices, local(): lax.ppermute(rows_here[i], 'dp', [(j, j ^ i) for j in range(peers)])  7.22 us
    pallas_call x2, Pallas kernels, pick_early(): pl.pallas_call(functools.partial(early_kernel, spread=spread, start=start...  4.46 us
    all_to_all x2, waiting for transfers between devices, exchange(): lax.all_to_all(value, 'dp', split_axis=0, concat_axis=0, tiled=True, axis...  4.04 us
    ppermute x2, waiting for transfers between devices, local(): far = lax.ppermute(near, 'groups', [(0, 1), (1, 0)])  3.77 us
    pallas_call x1, Pallas kernels, pick(): pl.pallas_call(functools.partial(pick_kernel, spread=spread), in_specs=[V...  3.67 us
  transfers between devices with their start and end apart: 14, of which 8 were waited for; matrix products, arithmetic and copies ran while one was open for 10% of the time, Pallas kernels for 9%

profile of v4, /device:TPU:0, one launch (start us, length us, event | category | flops | bytes accessed | tf_op | source)
XLA Modules:
  0.0 92.8 jit_solution(4163049949878725107)
XLA Ops:
  0.7 1.4 %fusion.6 = s32[16,128]{1,0:T(8,128)} fusion(s32[16]{0:T(128)S(1)} %broadcast_multiply_fusion, s32[4,128]{1,0:T(4,128)} %bitcast.40, s32[4,128]{1,0:T(4,128)} %bitcast.38, s32[16]{0:T(128)S(1)} %and_select_fusion), kind=kLoop, calls=%fused_computation.18 | loop fusion | flops 120832 | bytes 12416 | tf_op jit(solution)/shard_map/reduce_max | solution.py:426
  2.1 7.3 %all-to-all-start = ((s32[8,2,128]{2,1,0:T(2,128)}), s32[8,2,128]{2,1,0:T(2,128)S(1)}, u32[]{:S(2)}, u32[]{:S(2)}) async-start(s32[8,2,128]{2,1,0:T(2,128)} %bitcast.10), calls=%async_computation | async-start | bytes 16384 | tf_op jit(solution)/shard_map/all_to_all | solution.py:385
  9.3 0.9 constant_dynamic-slice_fusion
  10.2 3.0 %collective-permute-start.6 = (bf16[256,256]{1,0:T(8,128)(2,1)S(1)}, bf16[256,256]{1,0:T(8,128)(2,1)S(1)}, u32[]{:S(2)}, u32[]{:S(2)}) collective-permute-start(bf16[256,256]{1,0:T(8,128)(2,1)S(1)} %constant_dynamic-slice_fusion), channel_id=1, source_target_pairs={{0,8},{2,10},{4,12},{6,14},{8,0},{10,2},{12,4},{14,6},{1,9},{3,11}... | collective-permute-start | bytes 393224 | tf_op jit(solution)/shard_map/ppermute | solution.py:417
  13.2 0.9 %constant_dynamic-slice_fusion.1 = bf16[256,384]{1,0:T(8,128)(2,1)S(1)} fusion(bf16[512,2048]{1,0:T(8,128)(2,1)} %head_hbm.5, s32[]{:T(128)S(6)} %select_n.135), kind=kLoop, calls=%fused_computation.53 | loop fusion | bytes 393220 | tf_op jit(solution)/shard_map/dynamic_slice | solution.py:416
  14.2 0.7 select_reduce_fusion
  15.0 0.8 reduce-window.7
  15.8 0.7 reduce_max.33
  16.5 0.7 fusion.8
  18.1 3.7 %pick.1 = bf16[768,1408]{1,0:T(8,128)(2,1)} custom-call(s32[16,128]{1,0:T(8,128)S(1)} %bitcast.34, bf16[512,2048]{1,0:T(8,128)(2,1)} %head_hbm.5), custom_call_target="tpu_custom_call" | custom-call | tf_op jit(solution)/shard_map/pick/pallas_call | solution.py:275
  21.8 6.1 %all-to-all-start.1 = ((bf16[8,96,1408]{2,1,0:T(8,128)(2,1)}), bf16[8,96,1408]{2,1,0:T(8,128)(2,1)S(1)}, u32[]{:S(2)}, u32[]{:S(2)}) async-start(bf16[8,96,1408]{2,1,0:T(8,128)(2,1)} %bitcast.37), calls=%async_computation.1 | async-start | bytes 4325376 | tf_op jit(solution)/shard_map/all_to_all | solution.py:385
  28.5 1.8 %fusion = f32[3,128]{1,0:T(4,128)S(1)} fusion(bf16[128,3,2048]{2,0,1:T(8,128)(2,1)} %param.8), kind=kLoop, calls=%fused_computation.2 | loop fusion | flops 2358912 | bytes 1574400 | tf_op jit(solution)/shard_map/reduce_sum | solution.py:460
  30.4 1.1 %collective-permute-done = f32[3,128]{1,0:T(4,128)S(1)} collective-permute-done((f32[3,128]{1,0:T(4,128)S(1)}, f32[3,128]{1,0:T(4,128)S(1)}, u32[]{:S(2)}, u32[]{:S(2)}) %collective-permute-start) | collective-permute-done | bytes 1568 | tf_op jit(solution)/shard_map/ppermute | solution.py:381
  31.5 1.6 %collective-permute-start.7 = (bf16[256,256]{1,0:T(8,128)(2,1)S(1)}, bf16[256,256]{1,0:T(8,128)(2,1)S(1)}, u32[]{:S(2)}, u32[]{:S(2)}) collective-permute-start(bf16[256,256]{1,0:T(8,128)(2,1)S(1)} %collective-permute-done.6.near_hbm), channel_id=1, source_target_pairs={{0,16},{16,0},{1,17},{17,1},{2,18},{18,2},{3,19},{19,3},{4,20},{20... | collective-permute-start | bytes 393224 | tf_op jit(solution)/shard_map/ppermute | solution.py:442
  34.2 3.8 %collective-permute-done.7.far_hbm = bf16[256,256]{1,0:T(8,128)(2,1)S(1)} collective-permute-done((bf16[256,256]{1,0:T(8,128)(2,1)S(1)}, bf16[256,256]{1,0:T(8,128)(2,1)S(1)}, u32[]{:S(2)}, u32[]{:S(2)}) %collective-permute-start.7) | collective-permute-done | bytes 131104 | tf_op jit(solution)/shard_map/ppermute | solution.py:442
  38.6 2.1 %pick_early.3 = (bf16[192,256]{1,0:T(8,128)(2,1)S(1)}, bf16[192,256]{1,0:T(8,128)(2,1)S(1)}, bf16[192,256]{1,0:T(8,128)(2,1)}, bf16[192,256]{1,0:T(8,128)(2,1)}) custom-call(s32[8,128]{1,0:T(8,128)S(1)} %add_select_fusion.5.asked_ref, bf16[512,2048]{1,0:T(8,128)(2,1)} %head_hbm.5, bf16[256,256]{1,0:T(8,128)(2,1)} %copy-done.4, bf16[256,256]{1,0:T(8,128)(2,1)} %copy-done.5), custom_call_target="tpu_custom_call" | custom-call | tf_op jit(solution)/shard_map/pick_early/pallas_call | solution.py:294
  40.7 2.1 %collective-permute-start.8 = (bf16[192,256]{1,0:T(8,128)(2,1)S(1)}, bf16[192,256]{1,0:T(8,128)(2,1)S(1)}, u32[]{:S(2)}, u32[]{:S(2)}) collective-permute-start(bf16[192,256]{1,0:T(8,128)(2,1)S(1)} %get-tuple-element.28), channel_id=1, source_target_pairs={{0,2},{2,0},{4,6},{6,4},{8,10},{10,8},{12,14},{14,12},{1,3},{3,1},... | collective-permute-start | bytes 294920 | tf_op jit(solution)/shard_map/ppermute | solution.py:446
  42.9 1.5 %collective-permute-start.9 = (bf16[192,256]{1,0:T(8,128)(2,1)}, bf16[192,256]{1,0:T(8,128)(2,1)S(1)}, u32[]{:S(2)}, u32[]{:S(2)}) collective-permute-start(bf16[192,256]{1,0:T(8,128)(2,1)} %get-tuple-element.29), channel_id=1, source_target_pairs={{0,4},{2,6},{4,0},{6,2},{8,12},{10,14},{12,8},{14,10},{1,5},{3,7},... | collective-permute-start | bytes 294920 | tf_op jit(solution)/shard_map/ppermute | solution.py:446
  44.5 0.7 copy-done.3
  45.2 2.4 %pick_early.2 = (bf16[192,384]{1,0:T(8,128)(2,1)S(1)}, bf16[192,384]{1,0:T(8,128)(2,1)}, bf16[192,384]{1,0:T(8,128)(2,1)S(1)}, bf16[192,384]{1,0:T(8,128)(2,1)S(1)}) custom-call(s32[8,128]{1,0:T(8,128)S(1)} %add_select_fusion.5.asked_ref, bf16[512,2048]{1,0:T(8,128)(2,1)} %head_hbm.5, bf16[256,384]{1,0:T(8,128)(2,1)} %copy-done.2, bf16[256,384]{1,0:T(8,128)(2,1)} %copy-done.3), custom_call_target="tpu_custom_call" | custom-call | tf_op jit(solution)/shard_map/pick_early/pallas_call | solution.py:294
  47.6 2.0 %collective-permute-start.3 = (bf16[192,384]{1,0:T(8,128)(2,1)}, bf16[192,384]{1,0:T(8,128)(2,1)S(1)}, u32[]{:S(2)}, u32[]{:S(2)}) collective-permute-start(bf16[192,384]{1,0:T(8,128)(2,1)} %get-tuple-element.23), channel_id=1, source_target_pairs={{0,2},{2,0},{4,6},{6,4},{8,10},{10,8},{12,14},{14,12},{1,3},{3,1},... | collective-permute-start | bytes 442376 | tf_op jit(solution)/shard_map/ppermute | solution.py:446
  49.6 1.5 %collective-permute-start.4 = (bf16[192,384]{1,0:T(8,128)(2,1)S(1)}, bf16[192,384]{1,0:T(8,128)(2,1)S(1)}, u32[]{:S(2)}, u32[]{:S(2)}) collective-permute-start(bf16[192,384]{1,0:T(8,128)(2,1)S(1)} %get-tuple-element.24), channel_id=1, source_target_pairs={{0,4},{2,6},{4,0},{6,2},{8,12},{10,14},{12,8},{14,10},{1,5},{3,7},... | collective-permute-start | bytes 442376 | tf_op jit(solution)/shard_map/ppermute | solution.py:446
  51.2 1.1 %pad_maximum_fusion.mixed_hbm = bf16[256,2048]{1,0:T(8,128)(2,1)} fusion(bf16[128,2048]{1,0:T(8,128)(2,1)S(1)} %get-tuple-element.37, bf16[128,2048]{1,0:T(8,128)(2,1)S(1)} %get-tuple-element.36), kind=kLoop, calls=%fused_computation.8 | loop fusion | flops 2097152 | bytes 2097152 | tf_op jit(solution)/shard_map/concatenate | solution.py:465
  52.4 14.0 %collective-permute-done.9.refs_6_ = bf16[192,256]{1,0:T(8,128)(2,1)S(1)} collective-permute-done((bf16[192,256]{1,0:T(8,128)(2,1)}, bf16[192,256]{1,0:T(8,128)(2,1)S(1)}, u32[]{:S(2)}, u32[]{:S(2)}) %collective-permute-start.9) | collective-permute-done | bytes 98336 | tf_op jit(solution)/shard_map/ppermute | solution.py:446
  66.4 2.1 %collective-permute-done.10.refs_7_ = bf16[192,256]{1,0:T(8,128)(2,1)S(1)} collective-permute-done((bf16[192,256]{1,0:T(8,128)(2,1)}, bf16[192,256]{1,0:T(8,128)(2,1)S(1)}, u32[]{:S(2)}, u32[]{:S(2)}) %collective-permute-start.10) | collective-permute-done | bytes 98336 | tf_op jit(solution)/shard_map/ppermute | solution.py:446
  68.5 2.4 %collective-permute-done.4.refs_2_ = bf16[192,384]{1,0:T(8,128)(2,1)S(1)} collective-permute-done((bf16[192,384]{1,0:T(8,128)(2,1)S(1)}, bf16[192,384]{1,0:T(8,128)(2,1)S(1)}, u32[]{:S(2)}, u32[]{:S(2)}) %collective-permute-start.4) | collective-permute-done | bytes 147488 | tf_op jit(solution)/shard_map/ppermute | solution.py:446
  70.8 1.6 %collective-permute-done.5.refs_3_ = bf16[192,384]{1,0:T(8,128)(2,1)S(1)} collective-permute-done((bf16[192,384]{1,0:T(8,128)(2,1)S(1)}, bf16[192,384]{1,0:T(8,128)(2,1)S(1)}, u32[]{:S(2)}, u32[]{:S(2)}) %collective-permute-start.5) | collective-permute-done | bytes 147488 | tf_op jit(solution)/shard_map/ppermute | solution.py:446
  72.4 4.0 %all-to-all-done.1 = bf16[8,96,1408]{2,1,0:T(8,128)(2,1)S(1)} async-done(((bf16[8,96,1408]{2,1,0:T(8,128)(2,1)}), bf16[8,96,1408]{2,1,0:T(8,128)(2,1)S(1)}, u32[]{:S(2)}, u32[]{:S(2)}) %all-to-all-start.1) | async-done | bytes 2162720 | tf_op jit(solution)/shard_map/all_to_all | solution.py:385
  76.5 2.6 %score.1 = (f32[8,128]{1,0:T(8,128)S(1)}, bf16[768,128]{1,0:T(8,128)(2,1)S(1)}, bf16[768,128]{1,0:T(8,128)(2,1)S(1)}) custom-call(f32[40,128]{1,0:T(8,128)S(1)} %pad.9.pack_ref, bf16[256,2048]{1,0:T(8,128)(2,1)} %pad_maximum_fusion.mixed_hbm, bf16[768,1408]{1,0:T(8,128)(2,1)S(1)} %bitcast.31, bf16[192,384]{1,0:T(8,128)(2,1)S(1)} %get-tuple-element.22.refs_0_, ...), custom_call_target="tpu_custom_call" | custom-call | tf_op jit(solution)/shard_map/score/pallas_call | solution.py:312
  79.2 1.2 %collective-permute-done.11.other_ref = f32[8,128]{1,0:T(8,128)S(1)} collective-permute-done((f32[8,128]{1,0:T(8,128)S(1)}, f32[8,128]{1,0:T(8,128)S(1)}, u32[]{:S(2)}, u32[]{:S(2)}) %collective-permute-start.11) | collective-permute-done | bytes 4128 | tf_op jit(solution)/shard_map/ppermute | solution.py:381
  80.3 1.0 %gradient.1 = bf16[8,64,128]{2,1,0:T(8,128)(2,1)S(1)} custom-call(f32[8,128]{1,0:T(8,128)S(1)} %get-tuple-element.31.own_ref, f32[8,128]{1,0:T(8,128)S(1)} %collective-permute-done.11.other_ref, f32[40,128]{1,0:T(8,128)S(1)} %pad.9.pack_ref, bf16[768,128]{1,0:T(8,128)(2,1)S(1)} %get-tuple-element.32.late_mask_ref, ...), custom_call_target="tpu_custom_call" | custom-call | tf_op jit(solution)/shard_map/gradient/pallas_call | solution.py:331
  81.4 10.8 %all_to_all.15.parts_ref = bf16[8,64,128]{2,1,0:T(8,128)(2,1)S(1)} all-to-all(bf16[8,64,128]{2,1,0:T(8,128)(2,1)S(1)} %gradient.1), channel_id=1, replica_groups=mesh['groups'=2,'dp'=8,'mp'=2] {'dp'}, dimensions={0} | all-to-all | bytes 262144 | tf_op jit(solution)/shard_map/all_to_all | solution.py:385
  (69 shorter events, 4.4 us)
Async XLA Ops:
  2.1 16.0 %all-to-all-start = ((s32[8,2,128]{2,1,0:T(2,128)}), s32[8,2,128]{2,1,0:T(2,128)S(1)}, u32[]{:S(2)}, u32[]{:S(2)}) async-start(s32[8,2,128]{2,1,0:T(2,128)} %bitcast.10), calls=%async_computation | async-start | bytes 16384 | tf_op jit(solution)/shard_map/all_to_all | solution.py:385
  10.2 21.3 %collective-permute-start.6 = (bf16[256,256]{1,0:T(8,128)(2,1)S(1)}, bf16[256,256]{1,0:T(8,128)(2,1)S(1)}, u32[]{:S(2)}, u32[]{:S(2)}) collective-permute-start(bf16[256,256]{1,0:T(8,128)(2,1)S(1)} %constant_dynamic-slice_fusion), channel_id=1, source_target_pairs={{0,8},{2,10},{4,12},{6,14},{8,0},{10,2},{12,4},{14,6},{1,9},{3,11}... | collective-permute-start | bytes 393224 | tf_op jit(solution)/shard_map/ppermute | solution.py:417
  14.2 19.4 %collective-permute-start.1 = (bf16[256,384]{1,0:T(8,128)(2,1)S(1)}, bf16[256,384]{1,0:T(8,128)(2,1)S(1)}, u32[]{:S(2)}, u32[]{:S(2)}) collective-permute-start(bf16[256,384]{1,0:T(8,128)(2,1)S(1)} %constant_dynamic-slice_fusion.1), channel_id=1, source_target_pairs={{0,8},{2,10},{4,12},{6,14},{8,0},{10,2},{12,4},{14,6},{1,9},{3,11}... | collective-permute-start | bytes 589832 | tf_op jit(solution)/shard_map/ppermute | solution.py:417
  21.7 6.3 %copy-start.10 = (s32[128,1]{0,1:T(1,128)S(1)}, s32[128,1]{0,1:T(1,128)}, u32[]{:S(2)}) copy-start(s32[128,1]{0,1:T(1,128)} %param.9) | copy-start | bytes 1540
  21.8 6.5 %copy-start.9 = (s32[1,4]{1,0:T(1,128)S(1)}, s32[1,4]{1,0:T(1,128)}, u32[]{:S(2)}) copy-start(s32[1,4]{1,0:T(1,128)} %param.13) | copy-start | bytes 52
  21.8 6.6 %copy-start.7 = (s32[128,4]{0,1:T(4,128)S(1)}, s32[128,4]{0,1:T(4,128)}, u32[]{:S(2)}) copy-start(s32[128,4]{0,1:T(4,128)} %param.10) | copy-start | bytes 6148
  21.8 6.7 %copy-start.8 = (bf16[128,4]{0,1:T(4,128)(2,1)S(1)}, bf16[128,4]{0,1:T(4,128)(2,1)}, u32[]{:S(2)}) copy-start(bf16[128,4]{0,1:T(4,128)(2,1)} %param.12) | copy-start | bytes 3076
  21.8 11.3 %copy-start.6 = (f32[3,2048]{1,0:T(4,128)S(1)}, f32[3,2048]{1,0:T(4,128)}, u32[]{:S(2)}) copy-start(f32[3,2048]{1,0:T(4,128)} %param.14) | copy-start | bytes 73732
  21.8 54.6 %all-to-all-start.1 = ((bf16[8,96,1408]{2,1,0:T(8,128)(2,1)}), bf16[8,96,1408]{2,1,0:T(8,128)(2,1)S(1)}, u32[]{:S(2)}, u32[]{:S(2)}) async-start(bf16[8,96,1408]{2,1,0:T(8,128)(2,1)} %bitcast.37), calls=%async_computation.1 | async-start | bytes 4325376 | tf_op jit(solution)/shard_map/all_to_all | solution.py:385
  28.0 5.1 %copy-start = (bf16[128,3,2048]{2,0,1:T(8,128)(2,1)S(1)}, bf16[128,3,2048]{2,0,1:T(8,128)(2,1)}, u32[]{:S(2)}) copy-start(bf16[128,3,2048]{2,0,1:T(8,128)(2,1)} %param.8) | copy-start | bytes 4718596
  30.3 1.2 %collective-permute-start = (f32[3,128]{1,0:T(4,128)S(1)}, f32[3,128]{1,0:T(4,128)S(1)}, u32[]{:S(2)}, u32[]{:S(2)}) collective-permute-start(f32[3,128]{1,0:T(4,128)S(1)} %fusion), channel_id=1, source_target_pairs={{0,1},{1,0},{2,3},{3,2},{4,5},{5,4},{6,7},{7,6},{8,9},{9,8},{10,11... | collective-permute-start | bytes 4616 | tf_op jit(solution)/shard_map/ppermute | solution.py:381
  31.5 6.4 %copy-start.4 = (bf16[256,256]{1,0:T(8,128)(2,1)}, bf16[256,256]{1,0:T(8,128)(2,1)S(1)}, u32[]{:S(2)}) copy-start(bf16[256,256]{1,0:T(8,128)(2,1)S(1)} %collective-permute-done.6.near_hbm) | copy-start | bytes 393220
  31.5 6.4 %collective-permute-start.7 = (bf16[256,256]{1,0:T(8,128)(2,1)S(1)}, bf16[256,256]{1,0:T(8,128)(2,1)S(1)}, u32[]{:S(2)}, u32[]{:S(2)}) collective-permute-start(bf16[256,256]{1,0:T(8,128)(2,1)S(1)} %collective-permute-done.6.near_hbm), channel_id=1, source_target_pairs={{0,16},{16,0},{1,17},{17,1},{2,18},{18,2},{3,19},{19,3},{4,20},{20... | collective-permute-start | bytes 393224 | tf_op jit(solution)/shard_map/ppermute | solution.py:442
  33.6 9.3 %copy-start.2 = (bf16[256,384]{1,0:T(8,128)(2,1)}, bf16[256,384]{1,0:T(8,128)(2,1)S(1)}, u32[]{:S(2)}) copy-start(bf16[256,384]{1,0:T(8,128)(2,1)S(1)} %collective-permute-done.1.near_hbm) | copy-start | bytes 589828
  33.6 11.0 %collective-permute-start.2 = (bf16[256,384]{1,0:T(8,128)(2,1)S(1)}, bf16[256,384]{1,0:T(8,128)(2,1)S(1)}, u32[]{:S(2)}, u32[]{:S(2)}) collective-permute-start(bf16[256,384]{1,0:T(8,128)(2,1)S(1)} %collective-permute-done.1.near_hbm), channel_id=1, source_target_pairs={{0,16},{16,0},{1,17},{17,1},{2,18},{18,2},{3,19},{19,3},{4,20},{20... | collective-permute-start | bytes 589832 | tf_op jit(solution)/shard_map/ppermute | solution.py:442
  37.9 0.7 copy-start.5
  40.7 10.4 %collective-permute-start.8 = (bf16[192,256]{1,0:T(8,128)(2,1)S(1)}, bf16[192,256]{1,0:T(8,128)(2,1)S(1)}, u32[]{:S(2)}, u32[]{:S(2)}) collective-permute-start(bf16[192,256]{1,0:T(8,128)(2,1)S(1)} %get-tuple-element.28), channel_id=1, source_target_pairs={{0,2},{2,0},{4,6},{6,4},{8,10},{10,8},{12,14},{14,12},{1,3},{3,1},... | collective-permute-start | bytes 294920 | tf_op jit(solution)/shard_map/ppermute | solution.py:446
  42.9 23.4 %collective-permute-start.9 = (bf16[192,256]{1,0:T(8,128)(2,1)}, bf16[192,256]{1,0:T(8,128)(2,1)S(1)}, u32[]{:S(2)}, u32[]{:S(2)}) collective-permute-start(bf16[192,256]{1,0:T(8,128)(2,1)} %get-tuple-element.29), channel_id=1, source_target_pairs={{0,4},{2,6},{4,0},{6,2},{8,12},{10,14},{12,8},{14,10},{1,5},{3,7},... | collective-permute-start | bytes 294920 | tf_op jit(solution)/shard_map/ppermute | solution.py:446
  44.5 24.0 %collective-permute-start.10 = (bf16[192,256]{1,0:T(8,128)(2,1)}, bf16[192,256]{1,0:T(8,128)(2,1)S(1)}, u32[]{:S(2)}, u32[]{:S(2)}) collective-permute-start(bf16[192,256]{1,0:T(8,128)(2,1)} %get-tuple-element.30), channel_id=1, source_target_pairs={{0,6},{2,4},{4,2},{6,0},{8,14},{10,12},{12,10},{14,8},{1,7},{3,5},... | collective-permute-start | bytes 294920 | tf_op jit(solution)/shard_map/ppermute | solution.py:446
  44.5 0.7 copy-start.3
  47.6 20.9 %collective-permute-start.3 = (bf16[192,384]{1,0:T(8,128)(2,1)}, bf16[192,384]{1,0:T(8,128)(2,1)S(1)}, u32[]{:S(2)}, u32[]{:S(2)}) collective-permute-start(bf16[192,384]{1,0:T(8,128)(2,1)} %get-tuple-element.23), channel_id=1, source_target_pairs={{0,2},{2,0},{4,6},{6,4},{8,10},{10,8},{12,14},{14,12},{1,3},{3,1},... | collective-permute-start | bytes 442376 | tf_op jit(solution)/shard_map/ppermute | solution.py:446
  49.6 21.2 %collective-permute-start.4 = (bf16[192,384]{1,0:T(8,128)(2,1)S(1)}, bf16[192,384]{1,0:T(8,128)(2,1)S(1)}, u32[]{:S(2)}, u32[]{:S(2)}) collective-permute-start(bf16[192,384]{1,0:T(8,128)(2,1)S(1)} %get-tuple-element.24), channel_id=1, source_target_pairs={{0,4},{2,6},{4,0},{6,2},{8,12},{10,14},{12,8},{14,10},{1,5},{3,7},... | collective-permute-start | bytes 442376 | tf_op jit(solution)/shard_map/ppermute | solution.py:446
  51.1 21.3 %collective-permute-start.5 = (bf16[192,384]{1,0:T(8,128)(2,1)S(1)}, bf16[192,384]{1,0:T(8,128)(2,1)S(1)}, u32[]{:S(2)}, u32[]{:S(2)}) collective-permute-start(bf16[192,384]{1,0:T(8,128)(2,1)S(1)} %get-tuple-element.25), channel_id=1, source_target_pairs={{0,6},{2,4},{4,2},{6,0},{8,14},{10,12},{12,10},{14,8},{1,7},{3,5},... | collective-permute-start | bytes 442376 | tf_op jit(solution)/shard_map/ppermute | solution.py:446
  76.4 3.9 %copy-start.1 = (bf16[128,3,2048]{2,0,1:T(8,128)(2,1)S(1)}, bf16[128,3,2048]{2,0,1:T(8,128)(2,1)}, u32[]{:S(2)}) copy-start(bf16[128,3,2048]{2,0,1:T(8,128)(2,1)} %param.8) | copy-start | bytes 4718596
  79.1 1.2 %collective-permute-start.11 = (f32[8,128]{1,0:T(8,128)S(1)}, f32[8,128]{1,0:T(8,128)S(1)}, u32[]{:S(2)}, u32[]{:S(2)}) collective-permute-start(f32[8,128]{1,0:T(8,128)S(1)} %get-tuple-element.31.own_ref), channel_id=1, source_target_pairs={{0,1},{1,0},{2,3},{3,2},{4,5},{5,4},{6,7},{7,6},{8,9},{9,8},{10,11... | collective-permute-start | bytes 12296 | tf_op jit(solution)/shard_map/ppermute | solution.py:381

commit v5 on v4

--- a/solution.py
+++ b/solution.py
@@ -12,7 +12,7 @@
 F32 = jnp.float32
 BF16 = jnp.bfloat16
 VMEM_LIMIT = 16 * 1024 * 1024
-CHUNKS = (384, 256)
+CHUNKS = (512, 128)
 
 
 def iota(shape, axis):
@@ -74,28 +74,39 @@
         copy.wait()
 
 
-def early_kernel(asked_ref, head_hbm, near_hbm, far_hbm, *refs, spread, start):
-    *out_refs, own_ref, other_ref, sems = refs
+def early_kernel(asked_ref, head_hbm, near_ref, far_ref, *refs, spread, start):
+    *out_refs, own_ref, sent_ref, sems = refs
     count, wide = own_ref.shape
+    copy = pltpu.make_async_copy(head_hbm.at[:, pl.ds(start, wide)], own_ref, sems.at[0])
+    copy.start()
+    peers = asked_ref.shape[0] // 2
+    hot = [hot_rows(every_other(asked_ref, i), spread, count) for i in range(2)]
+    other = sum(
+        jnp.dot(
+            hot[1][:, j * count // 2 : (j + 1) * count // 2],
+            ref[...],
+            preferred_element_type=F32,
+        )
+        for j, ref in enumerate((near_ref, far_ref))
+    )
+    copy.wait()
+    own = jnp.dot(hot[0], own_ref[...], preferred_element_type=F32)
+    each = 2 * peers * spread // len(out_refs)
+    targets = [out_refs[0]] + [sent_ref.at[i] for i in range(len(out_refs) - 1)]
+    for i, picked in enumerate((own.astype(BF16), other.astype(BF16))):
+        for peer in range(peers):
+            first = (2 * peer + i) * spread
+            targets[first // each][first % each : first % each + spread, :] = picked[
+                peer * spread : (peer + 1) * spread
+            ]
     copies = [
-        pltpu.make_async_copy(head_hbm.at[:, pl.ds(start, wide)], own_ref, sems.at[0]),
-        pltpu.make_async_copy(near_hbm, other_ref.at[: count // 2, :], sems.at[1]),
-        pltpu.make_async_copy(far_hbm, other_ref.at[count // 2 :, :], sems.at[2]),
+        pltpu.make_async_copy(sent_ref.at[i], out_ref, sems.at[1 + i])
+        for i, out_ref in enumerate(out_refs[1:])
     ]
     for copy in copies:
         copy.start()
-    peers = asked_ref.shape[0] // 2
-    hot = [hot_rows(every_other(asked_ref, i), spread, count) for i in range(2)]
     for copy in copies:
         copy.wait()
-    each = 2 * peers * spread // len(out_refs)
-    for i, table in enumerate((own_ref, other_ref)):
-        picked = jnp.dot(hot[i], table[...], preferred_element_type=F32).astype(BF16)
-        for peer in range(peers):
-            first = (2 * peer + i) * spread
-            out_refs[first // each][first % each : first % each + spread, :] = picked[
-                peer * spread : (peer + 1) * spread
-            ]
 
 
 def swapped(value, flags):
@@ -293,17 +304,18 @@
     slots = asked.shape[0] * spread
     return pl.pallas_call(
         functools.partial(early_kernel, spread=spread, start=start),
-        in_specs=[VMEM, HBM, HBM, HBM],
-        out_specs=[VMEM] * count,
-        out_shape=[jax.ShapeDtypeStruct((slots // count, wide), BF16)] * count,
+        in_specs=[VMEM, HBM, VMEM, VMEM],
+        out_specs=[VMEM] + [HBM] * (count - 1),
+        out_shape=[jax.ShapeDtypeStruct((slots // count, wide), BF16)]
+        + [pltpu.HBM((slots // count, wide), BF16)] * (count - 1),
         scratch_shapes=[
             pltpu.VMEM((rows, wide), BF16),
-            pltpu.VMEM((rows, wide), BF16),
-            pltpu.SemaphoreType.DMA((3,)),
+            pltpu.VMEM((max(1, count - 1), slots // count, wide), BF16),
+            pltpu.SemaphoreType.DMA((count,)),
         ],
         compiler_params=params(),
         name="pick_early",
-    )(asked, in_hbm(head), in_hbm(near), in_hbm(far))
+    )(asked, in_hbm(head), near, far)
 
 
 def score(pack, mixed, late, early, shards, used, parts):

time: 93.4 us -> 93.3 us (level)
  local copies, waits for them, and re-layouts: 3.48 us -> 2.08 us
    ppermute x2, waiting for transfers between devices: 3.77 us -> 6.23 us  [local(): far = lax.ppermute(near, 'groups', [(0, 1), (1, 0)])]
    ppermute x6, waiting for transfers between devices: 20.1 us -> 18.2 us  [local(): lax.ppermute(rows_here[i], 'dp', [(j, j ^ i) for j in range(peers)])]
    unnamed x22 -> x14, local copies, waits for them, and re-layouts: 1.4 us -> 0.04 us
    ppermute x2, starting transfers between devices: 2.16 us -> 3.1 us  [local(): far = lax.ppermute(near, 'groups', [(0, 1), (1, 0)])]
  transfers between devices with their start and end apart: 14 -> 14, of which waited for: 8 -> 9; matrix products, arithmetic and copies ran while one was open for 10% -> 10% of each run, Pallas kernels for 9% -> 9%
where the time goes in v5:
time: 93.3 us; the launch traced here: 92.7 us
  waiting for transfers between devices  30.6 us (33%)
  starting transfers between devices  26.8 us (29%)
  Pallas kernels  12.3 us (13%)
  blocking collectives  10.8 us (12%)
  other arithmetic  9.07 us (10%)
  local copies, waits for them, and re-layouts  2.08 us (2%)
  between operations  0.98 us (1%)
    ppermute x6, waiting for transfers between devices, local(): lax.ppermute(rows_here[i], 'dp', [(j, j ^ i) for j in range(peers)])  18.2 us
    all_to_all x2, starting transfers between devices, exchange(): lax.all_to_all(value, 'dp', split_axis=0, concat_axis=0, tiled=True, axis...  13.4 us
    all_to_all x1, blocking collectives, exchange(): lax.all_to_all(value, 'dp', split_axis=0, concat_axis=0, tiled=True, axis...  10.8 us
    ppermute x6, starting transfers between devices, local(): lax.ppermute(rows_here[i], 'dp', [(j, j ^ i) for j in range(peers)])  7.23 us
    ppermute x2, waiting for transfers between devices, local(): far = lax.ppermute(near, 'groups', [(0, 1), (1, 0)])  6.23 us
    pallas_call x2, Pallas kernels, pick_early(): pl.pallas_call(functools.partial(early_kernel, spread=spread, start=start...  4.38 us
    all_to_all x2, waiting for transfers between devices, exchange(): lax.all_to_all(value, 'dp', split_axis=0, concat_axis=0, tiled=True, axis...  3.93 us
    pallas_call x1, Pallas kernels, pick(): pl.pallas_call(functools.partial(pick_kernel, spread=spread), in_specs=[V...  3.68 us
  transfers between devices with their start and end apart: 14, of which 9 were waited for; matrix products, arithmetic and copies ran while one was open for 10% of the time, Pallas kernels for 9%

profile of v5, /device:TPU:0, one launch (start us, length us, event | category | flops | bytes accessed | tf_op | source)
XLA Modules:
  0.0 92.7 jit_solution(654323315084674740)
XLA Ops:
  0.7 1.4 %fusion.6 = s32[16,128]{1,0:T(8,128)} fusion(s32[16]{0:T(128)S(1)} %broadcast_multiply_fusion, s32[4,128]{1,0:T(4,128)} %bitcast.40, s32[4,128]{1,0:T(4,128)} %bitcast.38, s32[16]{0:T(128)S(1)} %and_select_fusion), kind=kLoop, calls=%fused_computation.18 | loop fusion | flops 120832 | bytes 12416 | tf_op jit(solution)/shard_map/reduce_max | solution.py:438
  2.1 7.3 %all-to-all-start = ((s32[8,2,128]{2,1,0:T(2,128)}), s32[8,2,128]{2,1,0:T(2,128)S(1)}, u32[]{:S(2)}, u32[]{:S(2)}) async-start(s32[8,2,128]{2,1,0:T(2,128)} %bitcast.10), calls=%async_computation | async-start | bytes 16384 | tf_op jit(solution)/shard_map/all_to_all | solution.py:397
  9.3 0.8 constant_dynamic-slice_fusion
  10.1 2.9 %collective-permute-start.6 = (bf16[256,128]{1,0:T(8,128)(2,1)S(1)}, bf16[256,128]{1,0:T(8,128)(2,1)S(1)}, u32[]{:S(2)}, u32[]{:S(2)}) collective-permute-start(bf16[256,128]{1,0:T(8,128)(2,1)S(1)} %constant_dynamic-slice_fusion), channel_id=1, source_target_pairs={{0,8},{2,10},{4,12},{6,14},{8,0},{10,2},{12,4},{14,6},{1,9},{3,11}... | collective-permute-start | bytes 196616 | tf_op jit(solution)/shard_map/ppermute | solution.py:429
  13.1 1.0 %constant_dynamic-slice_fusion.1 = bf16[256,512]{1,0:T(8,128)(2,1)S(1)} fusion(bf16[512,2048]{1,0:T(8,128)(2,1)} %head_hbm.5, s32[]{:T(128)S(6)} %select_n.135), kind=kLoop, calls=%fused_computation.53 | loop fusion | bytes 524292 | tf_op jit(solution)/shard_map/dynamic_slice | solution.py:428
  14.1 0.7 select_reduce_fusion
  14.8 0.8 reduce-window.7
  15.7 0.7 reduce_max.33
  17.9 3.7 %pick.1 = bf16[768,1408]{1,0:T(8,128)(2,1)} custom-call(s32[16,128]{1,0:T(8,128)S(1)} %bitcast.34, bf16[512,2048]{1,0:T(8,128)(2,1)} %head_hbm.5), custom_call_target="tpu_custom_call" | custom-call | tf_op jit(solution)/shard_map/pick/pallas_call | solution.py:286
  21.7 6.1 %all-to-all-start.1 = ((bf16[8,96,1408]{2,1,0:T(8,128)(2,1)}), bf16[8,96,1408]{2,1,0:T(8,128)(2,1)S(1)}, u32[]{:S(2)}, u32[]{:S(2)}) async-start(bf16[8,96,1408]{2,1,0:T(8,128)(2,1)} %bitcast.37), calls=%async_computation.1 | async-start | bytes 4325376 | tf_op jit(solution)/shard_map/all_to_all | solution.py:397
  28.3 1.8 %fusion = f32[3,128]{1,0:T(4,128)S(1)} fusion(bf16[128,3,2048]{2,0,1:T(8,128)(2,1)} %param.8), kind=kLoop, calls=%fused_computation.2 | loop fusion | flops 2358912 | bytes 1574400 | tf_op jit(solution)/shard_map/reduce_sum | solution.py:472
  30.3 1.1 %collective-permute-done = f32[3,128]{1,0:T(4,128)S(1)} collective-permute-done((f32[3,128]{1,0:T(4,128)S(1)}, f32[3,128]{1,0:T(4,128)S(1)}, u32[]{:S(2)}, u32[]{:S(2)}) %collective-permute-start) | collective-permute-done | bytes 1568 | tf_op jit(solution)/shard_map/ppermute | solution.py:393
  31.4 1.6 %collective-permute-start.7 = (bf16[256,128]{1,0:T(8,128)(2,1)S(1)}, bf16[256,128]{1,0:T(8,128)(2,1)S(1)}, u32[]{:S(2)}, u32[]{:S(2)}) collective-permute-start(bf16[256,128]{1,0:T(8,128)(2,1)S(1)} %collective-permute-done.6.near_ref), channel_id=1, source_target_pairs={{0,16},{16,0},{1,17},{17,1},{2,18},{18,2},{3,19},{19,3},{4,20},{20... | collective-permute-start | bytes 196616 | tf_op jit(solution)/shard_map/ppermute | solution.py:454
  33.4 2.3 %collective-permute-done.7.far_ref = bf16[256,128]{1,0:T(8,128)(2,1)S(1)} collective-permute-done((bf16[256,128]{1,0:T(8,128)(2,1)S(1)}, bf16[256,128]{1,0:T(8,128)(2,1)S(1)}, u32[]{:S(2)}, u32[]{:S(2)}) %collective-permute-start.7) | collective-permute-done | bytes 65568 | tf_op jit(solution)/shard_map/ppermute | solution.py:454
  35.7 2.0 %pick_early.3 = (bf16[192,128]{1,0:T(8,128)(2,1)S(1)}, bf16[192,128]{1,0:T(8,128)(2,1)}, bf16[192,128]{1,0:T(8,128)(2,1)}, bf16[192,128]{1,0:T(8,128)(2,1)}) custom-call(s32[8,128]{1,0:T(8,128)S(1)} %add_select_fusion.5.asked_ref, bf16[512,2048]{1,0:T(8,128)(2,1)} %head_hbm.5, bf16[256,128]{1,0:T(8,128)(2,1)S(1)} %collective-permute-done.6.near_ref, ...), custom_call_target="tpu_custom_call" | custom-call | tf_op jit(solution)/shard_map/pick_early/pallas_call | solution.py:305
  37.7 2.1 %collective-permute-start.8 = (bf16[192,128]{1,0:T(8,128)(2,1)}, bf16[192,128]{1,0:T(8,128)(2,1)S(1)}, u32[]{:S(2)}, u32[]{:S(2)}) collective-permute-start(bf16[192,128]{1,0:T(8,128)(2,1)} %get-tuple-element.28), channel_id=1, source_target_pairs={{0,2},{2,0},{4,6},{6,4},{8,10},{10,8},{12,14},{14,12},{1,3},{3,1},... | collective-permute-start | bytes 147464 | tf_op jit(solution)/shard_map/ppermute | solution.py:458
  39.8 1.5 %collective-permute-start.2 = (bf16[256,512]{1,0:T(8,128)(2,1)S(1)}, bf16[256,512]{1,0:T(8,128)(2,1)S(1)}, u32[]{:S(2)}, u32[]{:S(2)}) collective-permute-start(bf16[256,512]{1,0:T(8,128)(2,1)S(1)} %collective-permute-done.1.near_ref), channel_id=1, source_target_pairs={{0,16},{16,0},{1,17},{17,1},{2,18},{18,2},{3,19},{19,3},{4,20},{20... | collective-permute-start | bytes 786440 | tf_op jit(solution)/shard_map/ppermute | solution.py:454
  41.4 1.5 %collective-permute-start.9 = (bf16[192,128]{1,0:T(8,128)(2,1)}, bf16[192,128]{1,0:T(8,128)(2,1)S(1)}, u32[]{:S(2)}, u32[]{:S(2)}) collective-permute-start(bf16[192,128]{1,0:T(8,128)(2,1)} %get-tuple-element.29), channel_id=1, source_target_pairs={{0,4},{2,6},{4,0},{6,2},{8,12},{10,14},{12,8},{14,10},{1,5},{3,7},... | collective-permute-start | bytes 147464 | tf_op jit(solution)/shard_map/ppermute | solution.py:458
  43.1 3.9 %collective-permute-done.2.far_ref = bf16[256,512]{1,0:T(8,128)(2,1)S(1)} collective-permute-done((bf16[256,512]{1,0:T(8,128)(2,1)S(1)}, bf16[256,512]{1,0:T(8,128)(2,1)S(1)}, u32[]{:S(2)}, u32[]{:S(2)}) %collective-permute-start.2) | collective-permute-done | bytes 262176 | tf_op jit(solution)/shard_map/ppermute | solution.py:454
  47.0 2.4 %pick_early.2 = (bf16[192,512]{1,0:T(8,128)(2,1)S(1)}, bf16[192,512]{1,0:T(8,128)(2,1)}, bf16[192,512]{1,0:T(8,128)(2,1)}, bf16[192,512]{1,0:T(8,128)(2,1)}) custom-call(s32[8,128]{1,0:T(8,128)S(1)} %add_select_fusion.5.asked_ref, bf16[512,2048]{1,0:T(8,128)(2,1)} %head_hbm.5, bf16[256,512]{1,0:T(8,128)(2,1)S(1)} %collective-permute-done.1.near_ref, ...), custom_call_target="tpu_custom_call" | custom-call | tf_op jit(solution)/shard_map/pick_early/pallas_call | solution.py:305
  49.9 1.7 %collective-permute-start.4 = (bf16[192,512]{1,0:T(8,128)(2,1)}, bf16[192,512]{1,0:T(8,128)(2,1)S(1)}, u32[]{:S(2)}, u32[]{:S(2)}) collective-permute-start(bf16[192,512]{1,0:T(8,128)(2,1)} %get-tuple-element.24), channel_id=1, source_target_pairs={{0,4},{2,6},{4,0},{6,2},{8,12},{10,14},{12,8},{14,10},{1,5},{3,7},... | collective-permute-start | bytes 589832 | tf_op jit(solution)/shard_map/ppermute | solution.py:458
  51.5 1.5 %collective-permute-start.5 = (bf16[192,512]{1,0:T(8,128)(2,1)}, bf16[192,512]{1,0:T(8,128)(2,1)S(1)}, u32[]{:S(2)}, u32[]{:S(2)}) collective-permute-start(bf16[192,512]{1,0:T(8,128)(2,1)} %get-tuple-element.25), channel_id=1, source_target_pairs={{0,6},{2,4},{4,2},{6,0},{8,14},{10,12},{12,10},{14,8},{1,7},{3,5},... | collective-permute-start | bytes 589832 | tf_op jit(solution)/shard_map/ppermute | solution.py:458
  53.0 1.1 %pad_maximum_fusion.mixed_hbm = bf16[256,2048]{1,0:T(8,128)(2,1)} fusion(bf16[128,2048]{1,0:T(8,128)(2,1)S(1)} %get-tuple-element.37, bf16[128,2048]{1,0:T(8,128)(2,1)S(1)} %get-tuple-element.36), kind=kLoop, calls=%fused_computation.8 | loop fusion | flops 2097152 | bytes 2097152 | tf_op jit(solution)/shard_map/concatenate | solution.py:477
  54.2 11.0 %collective-permute-done.9.refs_6_ = bf16[192,128]{1,0:T(8,128)(2,1)S(1)} collective-permute-done((bf16[192,128]{1,0:T(8,128)(2,1)}, bf16[192,128]{1,0:T(8,128)(2,1)S(1)}, u32[]{:S(2)}, u32[]{:S(2)}) %collective-permute-start.9) | collective-permute-done | bytes 49184 | tf_op jit(solution)/shard_map/ppermute | solution.py:458
  65.2 1.1 %collective-permute-done.10.refs_7_ = bf16[192,128]{1,0:T(8,128)(2,1)S(1)} collective-permute-done((bf16[192,128]{1,0:T(8,128)(2,1)}, bf16[192,128]{1,0:T(8,128)(2,1)S(1)}, u32[]{:S(2)}, u32[]{:S(2)}) %collective-permute-start.10) | collective-permute-done | bytes 49184 | tf_op jit(solution)/shard_map/ppermute | solution.py:458
  66.3 4.0 %collective-permute-done.4.refs_2_ = bf16[192,512]{1,0:T(8,128)(2,1)S(1)} collective-permute-done((bf16[192,512]{1,0:T(8,128)(2,1)}, bf16[192,512]{1,0:T(8,128)(2,1)S(1)}, u32[]{:S(2)}, u32[]{:S(2)}) %collective-permute-start.4) | collective-permute-done | bytes 196640 | tf_op jit(solution)/shard_map/ppermute | solution.py:458
  70.3 2.1 %collective-permute-done.5.refs_3_ = bf16[192,512]{1,0:T(8,128)(2,1)S(1)} collective-permute-done((bf16[192,512]{1,0:T(8,128)(2,1)}, bf16[192,512]{1,0:T(8,128)(2,1)S(1)}, u32[]{:S(2)}, u32[]{:S(2)}) %collective-permute-start.5) | collective-permute-done | bytes 196640 | tf_op jit(solution)/shard_map/ppermute | solution.py:458
  72.4 3.9 %all-to-all-done.1 = bf16[8,96,1408]{2,1,0:T(8,128)(2,1)S(1)} async-done(((bf16[8,96,1408]{2,1,0:T(8,128)(2,1)}), bf16[8,96,1408]{2,1,0:T(8,128)(2,1)S(1)}, u32[]{:S(2)}, u32[]{:S(2)}) %all-to-all-start.1) | async-done | bytes 2162720 | tf_op jit(solution)/shard_map/all_to_all | solution.py:397
  76.3 2.6 %score.1 = (f32[8,128]{1,0:T(8,128)S(1)}, bf16[768,128]{1,0:T(8,128)(2,1)S(1)}, bf16[768,128]{1,0:T(8,128)(2,1)S(1)}) custom-call(f32[40,128]{1,0:T(8,128)S(1)} %pad.9.pack_ref, bf16[256,2048]{1,0:T(8,128)(2,1)} %pad_maximum_fusion.mixed_hbm, bf16[768,1408]{1,0:T(8,128)(2,1)S(1)} %bitcast.31, bf16[192,512]{1,0:T(8,128)(2,1)S(1)} %get-tuple-element.22.refs_0_, ...), custom_call_target="tpu_custom_call" | custom-call | tf_op jit(solution)/shard_map/score/pallas_call | solution.py:324
  79.0 1.2 %collective-permute-done.11.other_ref = f32[8,128]{1,0:T(8,128)S(1)} collective-permute-done((f32[8,128]{1,0:T(8,128)S(1)}, f32[8,128]{1,0:T(8,128)S(1)}, u32[]{:S(2)}, u32[]{:S(2)}) %collective-permute-start.11) | collective-permute-done | bytes 4128 | tf_op jit(solution)/shard_map/ppermute | solution.py:393
  80.2 1.0 %gradient.1 = bf16[8,64,128]{2,1,0:T(8,128)(2,1)S(1)} custom-call(f32[8,128]{1,0:T(8,128)S(1)} %get-tuple-element.31.own_ref, f32[8,128]{1,0:T(8,128)S(1)} %collective-permute-done.11.other_ref, f32[40,128]{1,0:T(8,128)S(1)} %pad.9.pack_ref, bf16[768,128]{1,0:T(8,128)(2,1)S(1)} %get-tuple-element.32.late_mask_ref, ...), custom_call_target="tpu_custom_call" | custom-call | tf_op jit(solution)/shard_map/gradient/pallas_call | solution.py:343
  81.2 10.8 %all_to_all.15.parts_ref = bf16[8,64,128]{2,1,0:T(8,128)(2,1)S(1)} all-to-all(bf16[8,64,128]{2,1,0:T(8,128)(2,1)S(1)} %gradient.1), channel_id=1, replica_groups=mesh['groups'=2,'dp'=8,'mp'=2] {'dp'}, dimensions={0} | all-to-all | bytes 262144 | tf_op jit(solution)/shard_map/all_to_all | solution.py:397
  (61 shorter events, 4.2 us)
Async XLA Ops:
  2.1 15.9 %all-to-all-start = ((s32[8,2,128]{2,1,0:T(2,128)}), s32[8,2,128]{2,1,0:T(2,128)S(1)}, u32[]{:S(2)}, u32[]{:S(2)}) async-start(s32[8,2,128]{2,1,0:T(2,128)} %bitcast.10), calls=%async_computation | async-start | bytes 16384 | tf_op jit(solution)/shard_map/all_to_all | solution.py:397
  10.1 21.2 %collective-permute-start.6 = (bf16[256,128]{1,0:T(8,128)(2,1)S(1)}, bf16[256,128]{1,0:T(8,128)(2,1)S(1)}, u32[]{:S(2)}, u32[]{:S(2)}) collective-permute-start(bf16[256,128]{1,0:T(8,128)(2,1)S(1)} %constant_dynamic-slice_fusion), channel_id=1, source_target_pairs={{0,8},{2,10},{4,12},{6,14},{8,0},{10,2},{12,4},{14,6},{1,9},{3,11}... | collective-permute-start | bytes 196616 | tf_op jit(solution)/shard_map/ppermute | solution.py:429
  14.0 25.7 %collective-permute-start.1 = (bf16[256,512]{1,0:T(8,128)(2,1)S(1)}, bf16[256,512]{1,0:T(8,128)(2,1)S(1)}, u32[]{:S(2)}, u32[]{:S(2)}) collective-permute-start(bf16[256,512]{1,0:T(8,128)(2,1)S(1)} %constant_dynamic-slice_fusion.1), channel_id=1, source_target_pairs={{0,8},{2,10},{4,12},{6,14},{8,0},{10,2},{12,4},{14,6},{1,9},{3,11}... | collective-permute-start | bytes 786440 | tf_op jit(solution)/shard_map/ppermute | solution.py:429
  21.6 6.3 %copy-start.6 = (s32[128,1]{0,1:T(1,128)S(1)}, s32[128,1]{0,1:T(1,128)}, u32[]{:S(2)}) copy-start(s32[128,1]{0,1:T(1,128)} %param.9) | copy-start | bytes 1540
  21.6 6.5 %copy-start.5 = (s32[1,4]{1,0:T(1,128)S(1)}, s32[1,4]{1,0:T(1,128)}, u32[]{:S(2)}) copy-start(s32[1,4]{1,0:T(1,128)} %param.13) | copy-start | bytes 52
  21.7 6.6 %copy-start.3 = (s32[128,4]{0,1:T(4,128)S(1)}, s32[128,4]{0,1:T(4,128)}, u32[]{:S(2)}) copy-start(s32[128,4]{0,1:T(4,128)} %param.10) | copy-start | bytes 6148
  21.7 6.7 %copy-start.4 = (bf16[128,4]{0,1:T(4,128)(2,1)S(1)}, bf16[128,4]{0,1:T(4,128)(2,1)}, u32[]{:S(2)}) copy-start(bf16[128,4]{0,1:T(4,128)(2,1)} %param.12) | copy-start | bytes 3076
  21.7 11.3 %copy-start.2 = (f32[3,2048]{1,0:T(4,128)S(1)}, f32[3,2048]{1,0:T(4,128)}, u32[]{:S(2)}) copy-start(f32[3,2048]{1,0:T(4,128)} %param.14) | copy-start | bytes 73732
  21.7 54.7 %all-to-all-start.1 = ((bf16[8,96,1408]{2,1,0:T(8,128)(2,1)}), bf16[8,96,1408]{2,1,0:T(8,128)(2,1)S(1)}, u32[]{:S(2)}, u32[]{:S(2)}) async-start(bf16[8,96,1408]{2,1,0:T(8,128)(2,1)} %bitcast.37), calls=%async_computation.1 | async-start | bytes 4325376 | tf_op jit(solution)/shard_map/all_to_all | solution.py:397
  27.9 5.1 %copy-start = (bf16[128,3,2048]{2,0,1:T(8,128)(2,1)S(1)}, bf16[128,3,2048]{2,0,1:T(8,128)(2,1)}, u32[]{:S(2)}) copy-start(bf16[128,3,2048]{2,0,1:T(8,128)(2,1)} %param.8) | copy-start | bytes 4718596
  30.2 1.2 %collective-permute-start = (f32[3,128]{1,0:T(4,128)S(1)}, f32[3,128]{1,0:T(4,128)S(1)}, u32[]{:S(2)}, u32[]{:S(2)}) collective-permute-start(f32[3,128]{1,0:T(4,128)S(1)} %fusion), channel_id=1, source_target_pairs={{0,1},{1,0},{2,3},{3,2},{4,5},{5,4},{6,7},{7,6},{8,9},{9,8},{10,11... | collective-permute-start | bytes 4616 | tf_op jit(solution)/shard_map/ppermute | solution.py:393
  31.4 4.3 %collective-permute-start.7 = (bf16[256,128]{1,0:T(8,128)(2,1)S(1)}, bf16[256,128]{1,0:T(8,128)(2,1)S(1)}, u32[]{:S(2)}, u32[]{:S(2)}) collective-permute-start(bf16[256,128]{1,0:T(8,128)(2,1)S(1)} %collective-permute-done.6.near_ref), channel_id=1, source_target_pairs={{0,16},{16,0},{1,17},{17,1},{2,18},{18,2},{3,19},{19,3},{4,20},{20... | collective-permute-start | bytes 196616 | tf_op jit(solution)/shard_map/ppermute | solution.py:454
  37.7 13.8 %collective-permute-start.8 = (bf16[192,128]{1,0:T(8,128)(2,1)}, bf16[192,128]{1,0:T(8,128)(2,1)S(1)}, u32[]{:S(2)}, u32[]{:S(2)}) collective-permute-start(bf16[192,128]{1,0:T(8,128)(2,1)} %get-tuple-element.28), channel_id=1, source_target_pairs={{0,2},{2,0},{4,6},{6,4},{8,10},{10,8},{12,14},{14,12},{1,3},{3,1},... | collective-permute-start | bytes 147464 | tf_op jit(solution)/shard_map/ppermute | solution.py:458
  39.8 7.2 %collective-permute-start.2 = (bf16[256,512]{1,0:T(8,128)(2,1)S(1)}, bf16[256,512]{1,0:T(8,128)(2,1)S(1)}, u32[]{:S(2)}, u32[]{:S(2)}) collective-permute-start(bf16[256,512]{1,0:T(8,128)(2,1)S(1)} %collective-permute-done.1.near_ref), channel_id=1, source_target_pairs={{0,16},{16,0},{1,17},{17,1},{2,18},{18,2},{3,19},{19,3},{4,20},{20... | collective-permute-start | bytes 786440 | tf_op jit(solution)/shard_map/ppermute | solution.py:454
  41.4 23.8 %collective-permute-start.9 = (bf16[192,128]{1,0:T(8,128)(2,1)}, bf16[192,128]{1,0:T(8,128)(2,1)S(1)}, u32[]{:S(2)}, u32[]{:S(2)}) collective-permute-start(bf16[192,128]{1,0:T(8,128)(2,1)} %get-tuple-element.29), channel_id=1, source_target_pairs={{0,4},{2,6},{4,0},{6,2},{8,12},{10,14},{12,8},{14,10},{1,5},{3,7},... | collective-permute-start | bytes 147464 | tf_op jit(solution)/shard_map/ppermute | solution.py:458
  43.0 23.3 %collective-permute-start.10 = (bf16[192,128]{1,0:T(8,128)(2,1)}, bf16[192,128]{1,0:T(8,128)(2,1)S(1)}, u32[]{:S(2)}, u32[]{:S(2)}) collective-permute-start(bf16[192,128]{1,0:T(8,128)(2,1)} %get-tuple-element.30), channel_id=1, source_target_pairs={{0,6},{2,4},{4,2},{6,0},{8,14},{10,12},{12,10},{14,8},{1,7},{3,5},... | collective-permute-start | bytes 147464 | tf_op jit(solution)/shard_map/ppermute | solution.py:458
  49.4 16.8 %collective-permute-start.3 = (bf16[192,512]{1,0:T(8,128)(2,1)}, bf16[192,512]{1,0:T(8,128)(2,1)S(1)}, u32[]{:S(2)}, u32[]{:S(2)}) collective-permute-start(bf16[192,512]{1,0:T(8,128)(2,1)} %get-tuple-element.23), channel_id=1, source_target_pairs={{0,2},{2,0},{4,6},{6,4},{8,10},{10,8},{12,14},{14,12},{1,3},{3,1},... | collective-permute-start | bytes 589832 | tf_op jit(solution)/shard_map/ppermute | solution.py:458
  49.9 20.4 %collective-permute-start.4 = (bf16[192,512]{1,0:T(8,128)(2,1)}, bf16[192,512]{1,0:T(8,128)(2,1)S(1)}, u32[]{:S(2)}, u32[]{:S(2)}) collective-permute-start(bf16[192,512]{1,0:T(8,128)(2,1)} %get-tuple-element.24), channel_id=1, source_target_pairs={{0,4},{2,6},{4,0},{6,2},{8,12},{10,14},{12,8},{14,10},{1,5},{3,7},... | collective-permute-start | bytes 589832 | tf_op jit(solution)/shard_map/ppermute | solution.py:458
  51.5 20.9 %collective-permute-start.5 = (bf16[192,512]{1,0:T(8,128)(2,1)}, bf16[192,512]{1,0:T(8,128)(2,1)S(1)}, u32[]{:S(2)}, u32[]{:S(2)}) collective-permute-start(bf16[192,512]{1,0:T(8,128)(2,1)} %get-tuple-element.25), channel_id=1, source_target_pairs={{0,6},{2,4},{4,2},{6,0},{8,14},{10,12},{12,10},{14,8},{1,7},{3,5},... | collective-permute-start | bytes 589832 | tf_op jit(solution)/shard_map/ppermute | solution.py:458
  76.3 3.9 %copy-start.1 = (bf16[128,3,2048]{2,0,1:T(8,128)(2,1)S(1)}, bf16[128,3,2048]{2,0,1:T(8,128)(2,1)}, u32[]{:S(2)}) copy-start(bf16[128,3,2048]{2,0,1:T(8,128)(2,1)} %param.8) | copy-start | bytes 4718596
  79.0 1.2 %collective-permute-start.11 = (f32[8,128]{1,0:T(8,128)S(1)}, f32[8,128]{1,0:T(8,128)S(1)}, u32[]{:S(2)}, u32[]{:S(2)}) collective-permute-start(f32[8,128]{1,0:T(8,128)S(1)} %get-tuple-element.31.own_ref), channel_id=1, source_target_pairs={{0,1},{1,0},{2,3},{3,2},{4,5},{5,4},{6,7},{7,6},{8,9},{9,8},{10,11... | collective-permute-start | bytes 12296 | tf_op jit(solution)/shard_map/ppermute | solution.py:393

commit v6 on v5

--- a/solution.py
+++ b/solution.py
@@ -12,7 +12,7 @@
 F32 = jnp.float32
 BF16 = jnp.bfloat16
 VMEM_LIMIT = 16 * 1024 * 1024
-CHUNKS = (512, 128)
+CHUNKS = (256, 384)
 
 
 def iota(shape, axis):
@@ -71,6 +71,44 @@
         copy.start()
         departures.append(copy)
     for copy in departures:
+        copy.wait()
+
+
+def begin_kernel(
+    group_ref, shard_hbm, offset_hbm, head_hbm, message_hbm, *refs, peers, starts
+):
+    *out_refs, shard_ref, offset_ref, message_ref, sems = refs
+    small = [
+        pltpu.make_async_copy(shard_hbm, shard_ref, sems.at[0]),
+        pltpu.make_async_copy(offset_hbm, offset_ref, sems.at[1]),
+    ]
+    large = []
+    part = out_refs[0].shape[0]
+    shift = group_ref[0] * part
+    for i, out_ref in enumerate(out_refs):
+        rows = pl.ds(pl.multiple_of(shift, part), part)
+        source = head_hbm.at[rows, pl.ds(starts[i], out_ref.shape[1])]
+        large.append(pltpu.make_async_copy(source, out_ref, sems.at[3 + i]))
+    for copy in small + large:
+        copy.start()
+    for copy in small:
+        copy.wait()
+    shard, offset = shard_ref[...], offset_ref[...]
+    count = head_hbm.shape[0]
+    other = offset + shift
+    other = jnp.where(other >= count, other - count, other)
+    line = iota(message_ref.shape, 0)
+    number = line // 2 + jnp.where(line % 2 == 0, 0, peers // 2)
+    number = jnp.where(number >= peers, number - peers, number)
+    message = jnp.full(message_ref.shape, -1, jnp.int32)
+    for k in range(shard.shape[0]):
+        asked = jnp.where(line % 2 == 0, offset[k : k + 1], other[k : k + 1])
+        message = jnp.where(shard[k : k + 1] == number, asked, message)
+    message_ref[...] = message
+    copy = pltpu.make_async_copy(message_ref, message_hbm, sems.at[2])
+    copy.start()
+    copy.wait()
+    for copy in large:
         copy.wait()
 
 
@@ -299,6 +337,25 @@
     )(asked, in_hbm(head))
 
 
+def begin(group, shard, offset, head, peers, part, starts, wides):
+    rows = shard.shape[1]
+    return pl.pallas_call(
+        functools.partial(begin_kernel, peers=peers, starts=starts),
+        in_specs=[pl.BlockSpec(memory_space=pltpu.SMEM), HBM, HBM, HBM],
+        out_specs=[HBM] + [VMEM] * len(wides),
+        out_shape=[pltpu.HBM((2 * peers, rows), jnp.int32)]
+        + [jax.ShapeDtypeStruct((part, wide), BF16) for wide in wides],
+        scratch_shapes=[
+            pltpu.VMEM(shard.shape, jnp.int32),
+            pltpu.VMEM(shard.shape, jnp.int32),
+            pltpu.VMEM((2 * peers, rows), jnp.int32),
+            pltpu.SemaphoreType.DMA((3 + len(wides),)),
+        ],
+        compiler_params=params(),
+        name="begin",
+    )(group.reshape(1), in_hbm(shard), in_hbm(offset), in_hbm(head))
+
+
 def pick_early(asked, head, near, far, spread, start, count):
     rows, wide = head.shape[0], near.shape[1]
     slots = asked.shape[0] * spread
@@ -422,20 +479,12 @@
 
     count = draft_head.shape[0]
     part = count // 2
-    chunks, start = [], late
-    for wide in CHUNKS:
-        wide = wide * features // 2048
-        near = lax.dynamic_slice(draft_head, (group * part, start), (part, wide))
-        near = lax.ppermute(near, "dp", [(i, (i + half) % peers) for i in range(peers)])
-        chunks.append((start, near))
-        start += wide
-
-    shard = candidate_shard.T
-    offset = candidate_offset.T
-    line = jnp.arange(2 * peers, dtype=jnp.int32)[:, None]
-    number = (line // 2 + line % 2 * half) % peers
-    placed = (offset[:, None, :] + line[None] % 2 * (group * part)) % count
-    message = jnp.max(jnp.where(shard[:, None, :] == number[None], placed, -1), axis=0)
+    wides = [wide * features // 2048 for wide in CHUNKS]
+    starts = [late + sum(wides[:i]) for i in range(len(wides))]
+    shard, offset = candidate_shard.T, candidate_offset.T
+    message, *slices = begin(group, shard, offset, draft_head, peers, part, starts, wides)
+    across = [(i, (i + half) % peers) for i in range(peers)]
+    chunks = [(start, lax.ppermute(near, "dp", across)) for start, near in zip(starts, slices)]
     wanted = exchange(message.reshape(peers, 2, rows)).reshape(2 * peers, rows)
 
     picked = pick(wanted, draft_head, spread, late)
@@ -462,7 +511,6 @@
             rows_here = [rows_here.reshape(peers * spread, -1)]
         rows_early += rows_here
 
-    hidden, layer_mix = after((hidden, layer_mix), picked)
     number = jnp.arange(peers, dtype=jnp.int32)[:, None]
     asked = jnp.max(
         jnp.where(shard[:, None, :] == number[None], offset[:, None, :], -1), axis=0

time: 93.3 us -> 92.5 us (level)
  other arithmetic: 9.07 us -> 4.35 us
  waiting for transfers between devices: 30.6 us -> 34.9 us
  local copies, waits for them, and re-layouts: 2.08 us -> 0.26 us
  blocking collectives: 10.8 us -> 12.6 us
  starting transfers between devices: 26.8 us -> 25.1 us
  Pallas kernels: 12.3 us -> 13.8 us
    all_to_all x2, waiting for transfers between devices: 3.93 us -> 11 us  [exchange(): lax.all_to_all(value, 'dp', split_axis=0, concat_axis=0, tiled=True, axis...]
    ppermute x2, waiting for transfers between devices: 6.23 us -> 2.87 us  [local(): far = lax.ppermute(near, 'groups', [(0, 1), (1, 0)])]
    all_to_all x2, starting transfers between devices: 13.4 us -> 10.9 us  [exchange(): lax.all_to_all(value, 'dp', split_axis=0, concat_axis=0, tiled=True, axis...]
    dynamic_slice x2 -> x0, local copies, waits for them, and re-layouts: 1.81 us -> none  [local(): near = lax.dynamic_slice(draft_head, (group * part, start), (part, wide))]
    all_to_all x1, blocking collectives: 10.8 us -> 12.6 us  [exchange(): lax.all_to_all(value, 'dp', split_axis=0, concat_axis=0, tiled=True, axis...]
    ppermute x6, starting transfers between devices: 7.23 us -> 8.94 us  [local(): lax.ppermute(rows_here[i], 'dp', [(j, j ^ i) for j in range(peers)])]
    ppermute x6, waiting for transfers between devices: 18.2 us -> 19.8 us  [local(): lax.ppermute(rows_here[i], 'dp', [(j, j ^ i) for j in range(peers)])]
    reduce_sum x1, other arithmetic: 0.45 us -> 1.95 us  [local(): mixed = jnp.sum(wide * layer_mix[:, None, :] * inverse[:, :, None], axis=0)]
  transfers between devices with their start and end apart: 14 -> 14, of which waited for: 9 -> 8; matrix products, arithmetic and copies ran while one was open for 10% -> 5% of each run, Pallas kernels for 9% -> 9%
where the time goes in v6:
time: 92.5 us; the launch traced here: 92 us
  waiting for transfers between devices  34.9 us (38%)
  starting transfers between devices  25.1 us (27%)
  Pallas kernels  13.8 us (15%)
  blocking collectives  12.6 us (14%)
  other arithmetic  4.35 us (5%)
  between operations  1.02 us (1%)
    ppermute x6, waiting for transfers between devices, local(): lax.ppermute(rows_here[i], 'dp', [(j, j ^ i) for j in range(peers)])  19.8 us
    all_to_all x1, blocking collectives, exchange(): lax.all_to_all(value, 'dp', split_axis=0, concat_axis=0, tiled=True, axis...  12.6 us
    all_to_all x2, waiting for transfers between devices, exchange(): lax.all_to_all(value, 'dp', split_axis=0, concat_axis=0, tiled=True, axis...  11 us
    all_to_all x2, starting transfers between devices, exchange(): lax.all_to_all(value, 'dp', split_axis=0, concat_axis=0, tiled=True, axis...  10.9 us
    ppermute x6, starting transfers between devices, local(): lax.ppermute(rows_here[i], 'dp', [(j, j ^ i) for j in range(peers)])  8.94 us
    pallas_call x2, Pallas kernels, pick_early(): pl.pallas_call(functools.partial(early_kernel, spread=spread, start=start...  4.39 us
    pallas_call x1, Pallas kernels, pick(): pl.pallas_call(functools.partial(pick_kernel, spread=spread), in_specs=[V...  3.69 us
    ppermute x2, starting transfers between devices, local(): lax.ppermute(near, 'dp', across)  2.97 us
  transfers between devices with their start and end apart: 14, of which 8 were waited for; matrix products, arithmetic and copies ran while one was open for 5% of the time, Pallas kernels for 9%

profile of v6, /device:TPU:0, one launch (start us, length us, event | category | flops | bytes accessed | tf_op | source)
XLA Modules:
  0.0 92.0 jit_solution(13184863985825097326)
XLA Ops:
  0.7 1.5 %begin.1 = (s32[16,128]{1,0:T(8,128)}, bf16[256,256]{1,0:T(8,128)(2,1)S(1)}, bf16[256,384]{1,0:T(8,128)(2,1)S(1)}) custom-call(s32[1]{0:T(128)} %bitcast.11.group_ref, s32[4,128]{1,0:T(4,128)} %bitcast.39, s32[4,128]{1,0:T(4,128)} %bitcast.41, bf16[512,2048]{1,0:T(8,128)(2,1)} %head_hbm.7), custom_call_target="tpu_custom_call" | custom-call | tf_op jit(solution)/shard_map/begin/pallas_call | solution.py:342
  2.2 7.3 %all-to-all-start = ((s32[8,2,128]{2,1,0:T(2,128)}), s32[8,2,128]{2,1,0:T(2,128)S(1)}, u32[]{:S(2)}, u32[]{:S(2)}) async-start(s32[8,2,128]{2,1,0:T(2,128)} %bitcast.43), calls=%async_computation | async-start | bytes 16384 | tf_op jit(solution)/shard_map/all_to_all | solution.py:454
  9.4 2.9 %collective-permute-start.6 = (bf16[256,384]{1,0:T(8,128)(2,1)S(1)}, bf16[256,384]{1,0:T(8,128)(2,1)S(1)}, u32[]{:S(2)}, u32[]{:S(2)}) collective-permute-start(bf16[256,384]{1,0:T(8,128)(2,1)S(1)} %get-tuple-element.27), channel_id=1, source_target_pairs={{0,8},{2,10},{4,12},{6,14},{8,0},{10,2},{12,4},{14,6},{1,9},{3,11}... | collective-permute-start | bytes 589832 | tf_op jit(solution)/shard_map/ppermute | solution.py:487
  12.4 0.4 fusion
  12.9 0.2 reduce-window.7
  13.1 0.1 fusion.8
  13.3 0.2 convert_reduce_fusion
  13.7 8.1 %all-to-all-done = s32[8,2,128]{2,1,0:T(2,128)S(1)} async-done(((s32[8,2,128]{2,1,0:T(2,128)}), s32[8,2,128]{2,1,0:T(2,128)S(1)}, u32[]{:S(2)}, u32[]{:S(2)}) %all-to-all-start) | async-done | bytes 8224 | tf_op jit(solution)/shard_map/all_to_all | solution.py:454
  21.8 3.7 %pick.1 = bf16[768,1408]{1,0:T(8,128)(2,1)} custom-call(s32[16,128]{1,0:T(8,128)S(1)} %bitcast.35, bf16[512,2048]{1,0:T(8,128)(2,1)} %head_hbm.7), custom_call_target="tpu_custom_call" | custom-call | tf_op jit(solution)/shard_map/pick/pallas_call | solution.py:324
  25.5 3.6 %all-to-all-start.1 = ((bf16[8,96,1408]{2,1,0:T(8,128)(2,1)}), bf16[8,96,1408]{2,1,0:T(8,128)(2,1)S(1)}, u32[]{:S(2)}, u32[]{:S(2)}) async-start(bf16[8,96,1408]{2,1,0:T(8,128)(2,1)} %bitcast.38), calls=%async_computation.1 | async-start | bytes 4325376 | tf_op jit(solution)/shard_map/all_to_all | solution.py:454
  29.3 2.0 %fusion.2 = f32[128,2048]{1,0:T(8,128)S(1)} fusion(f32[3,128]{1,0:T(4,128)S(1)} %add_rsqrt_fusion, f32[3,2048]{1,0:T(4,128)S(1)} %copy-done.2, bf16[128,3,2048]{2,0,1:T(8,128)(2,1)} %param.8), kind=kLoop, calls=%fused_computation.4 | loop fusion | flops 2883584 | bytes 2647552 | tf_op jit(solution)/shard_map/reduce_sum | solution.py:523
  31.3 1.6 %collective-permute-start.2 = (bf16[256,256]{1,0:T(8,128)(2,1)S(1)}, bf16[256,256]{1,0:T(8,128)(2,1)S(1)}, u32[]{:S(2)}, u32[]{:S(2)}) collective-permute-start(bf16[256,256]{1,0:T(8,128)(2,1)S(1)} %collective-permute-done.1.near_ref), channel_id=1, source_target_pairs={{0,16},{16,0},{1,17},{17,1},{2,18},{18,2},{3,19},{19,3},{4,20},{20... | collective-permute-start | bytes 393224 | tf_op jit(solution)/shard_map/ppermute | solution.py:503
  32.9 0.6 collective-permute-start.7
  33.5 2.9 %collective-permute-done.2.far_ref = bf16[256,256]{1,0:T(8,128)(2,1)S(1)} collective-permute-done((bf16[256,256]{1,0:T(8,128)(2,1)S(1)}, bf16[256,256]{1,0:T(8,128)(2,1)S(1)}, u32[]{:S(2)}, u32[]{:S(2)}) %collective-permute-start.2) | collective-permute-done | bytes 131104 | tf_op jit(solution)/shard_map/ppermute | solution.py:503
  36.4 2.0 %pick_early.2 = (bf16[192,256]{1,0:T(8,128)(2,1)S(1)}, bf16[192,256]{1,0:T(8,128)(2,1)}, bf16[192,256]{1,0:T(8,128)(2,1)}, bf16[192,256]{1,0:T(8,128)(2,1)}) custom-call(s32[8,128]{1,0:T(8,128)S(1)} %add_select_fusion.3.asked_ref, bf16[512,2048]{1,0:T(8,128)(2,1)} %head_hbm.7, bf16[256,256]{1,0:T(8,128)(2,1)S(1)} %collective-permute-done.1.near_ref, ...), custom_call_target="tpu_custom_call" | custom-call | tf_op jit(solution)/shard_map/pick_early/pallas_call | solution.py:362
  38.4 2.0 %collective-permute-start.3 = (bf16[192,256]{1,0:T(8,128)(2,1)}, bf16[192,256]{1,0:T(8,128)(2,1)S(1)}, u32[]{:S(2)}, u32[]{:S(2)}) collective-permute-start(bf16[192,256]{1,0:T(8,128)(2,1)} %get-tuple-element.24), channel_id=1, source_target_pairs={{0,2},{2,0},{4,6},{6,4},{8,10},{10,8},{12,14},{14,12},{1,3},{3,1},... | collective-permute-start | bytes 294920 | tf_op jit(solution)/shard_map/ppermute | solution.py:507
  40.4 0.2 reduce-precision_convert_fusion
  40.6 3.3 %collective-permute-start.4 = (bf16[192,256]{1,0:T(8,128)(2,1)}, bf16[192,256]{1,0:T(8,128)(2,1)S(1)}, u32[]{:S(2)}, u32[]{:S(2)}) collective-permute-start(bf16[192,256]{1,0:T(8,128)(2,1)} %get-tuple-element.25), channel_id=1, source_target_pairs={{0,4},{2,6},{4,0},{6,2},{8,12},{10,14},{12,8},{14,10},{1,5},{3,7},... | collective-permute-start | bytes 294920 | tf_op jit(solution)/shard_map/ppermute | solution.py:507
  43.9 2.3 %pick_early.3 = (bf16[192,384]{1,0:T(8,128)(2,1)S(1)}, bf16[192,384]{1,0:T(8,128)(2,1)}, bf16[192,384]{1,0:T(8,128)(2,1)}, bf16[192,384]{1,0:T(8,128)(2,1)}) custom-call(s32[8,128]{1,0:T(8,128)S(1)} %add_select_fusion.3.asked_ref, bf16[512,2048]{1,0:T(8,128)(2,1)} %head_hbm.7, bf16[256,384]{1,0:T(8,128)(2,1)S(1)} %collective-permute-done.6.near_ref, ...), custom_call_target="tpu_custom_call" | custom-call | tf_op jit(solution)/shard_map/pick_early/pallas_call | solution.py:362
  46.3 3.0 %collective-permute-start.10 = (bf16[192,384]{1,0:T(8,128)(2,1)}, bf16[192,384]{1,0:T(8,128)(2,1)S(1)}, u32[]{:S(2)}, u32[]{:S(2)}) collective-permute-start(bf16[192,384]{1,0:T(8,128)(2,1)} %get-tuple-element.32), channel_id=1, source_target_pairs={{0,6},{2,4},{4,2},{6,0},{8,14},{10,12},{12,10},{14,8},{1,7},{3,5},... | collective-permute-start | bytes 442376 | tf_op jit(solution)/shard_map/ppermute | solution.py:507
  49.3 0.6 collective-permute-start.9
  49.9 1.1 %pad_maximum_fusion.mixed_hbm = bf16[256,2048]{1,0:T(8,128)(2,1)} fusion(bf16[128,2048]{1,0:T(8,128)(2,1)S(1)} %get-tuple-element.39, bf16[128,2048]{1,0:T(8,128)(2,1)S(1)} %get-tuple-element.38), kind=kLoop, calls=%fused_computation.8 | loop fusion | flops 2097152 | bytes 2097152 | tf_op jit(solution)/shard_map/concatenate | solution.py:525
  51.1 15.6 %collective-permute-done.4.refs_2_ = bf16[192,256]{1,0:T(8,128)(2,1)S(1)} collective-permute-done((bf16[192,256]{1,0:T(8,128)(2,1)}, bf16[192,256]{1,0:T(8,128)(2,1)S(1)}, u32[]{:S(2)}, u32[]{:S(2)}) %collective-permute-start.4) | collective-permute-done | bytes 98336 | tf_op jit(solution)/shard_map/ppermute | solution.py:507
  66.7 1.1 %collective-permute-done.5.refs_3_ = bf16[192,256]{1,0:T(8,128)(2,1)S(1)} collective-permute-done((bf16[192,256]{1,0:T(8,128)(2,1)}, bf16[192,256]{1,0:T(8,128)(2,1)S(1)}, u32[]{:S(2)}, u32[]{:S(2)}) %collective-permute-start.5) | collective-permute-done | bytes 98336 | tf_op jit(solution)/shard_map/ppermute | solution.py:507
  67.7 1.6 %collective-permute-done.10.refs_7_ = bf16[192,384]{1,0:T(8,128)(2,1)S(1)} collective-permute-done((bf16[192,384]{1,0:T(8,128)(2,1)}, bf16[192,384]{1,0:T(8,128)(2,1)S(1)}, u32[]{:S(2)}, u32[]{:S(2)}) %collective-permute-start.10) | collective-permute-done | bytes 147488 | tf_op jit(solution)/shard_map/ppermute | solution.py:507
  69.3 1.6 %collective-permute-done.9.refs_6_ = bf16[192,384]{1,0:T(8,128)(2,1)S(1)} collective-permute-done((bf16[192,384]{1,0:T(8,128)(2,1)}, bf16[192,384]{1,0:T(8,128)(2,1)S(1)}, u32[]{:S(2)}, u32[]{:S(2)}) %collective-permute-start.9) | collective-permute-done | bytes 147488 | tf_op jit(solution)/shard_map/ppermute | solution.py:507
  70.9 3.0 %all-to-all-done.1 = bf16[8,96,1408]{2,1,0:T(8,128)(2,1)S(1)} async-done(((bf16[8,96,1408]{2,1,0:T(8,128)(2,1)}), bf16[8,96,1408]{2,1,0:T(8,128)(2,1)S(1)}, u32[]{:S(2)}, u32[]{:S(2)}) %all-to-all-start.1) | async-done | bytes 2162720 | tf_op jit(solution)/shard_map/all_to_all | solution.py:454
  73.9 2.6 %score.1 = (f32[8,128]{1,0:T(8,128)S(1)}, bf16[768,128]{1,0:T(8,128)(2,1)S(1)}, bf16[768,128]{1,0:T(8,128)(2,1)S(1)}) custom-call(f32[40,128]{1,0:T(8,128)S(1)} %pad.9.pack_ref, bf16[256,2048]{1,0:T(8,128)(2,1)} %pad_maximum_fusion.mixed_hbm, bf16[768,1408]{1,0:T(8,128)(2,1)S(1)} %bitcast.32, bf16[192,256]{1,0:T(8,128)(2,1)S(1)} %get-tuple-element.23.refs_0_, ...), custom_call_target="tpu_custom_call" | custom-call | tf_op jit(solution)/shard_map/score/pallas_call | solution.py:381
  76.6 1.2 %collective-permute-done.11.other_ref = f32[8,128]{1,0:T(8,128)S(1)} collective-permute-done((f32[8,128]{1,0:T(8,128)S(1)}, f32[8,128]{1,0:T(8,128)S(1)}, u32[]{:S(2)}, u32[]{:S(2)}) %collective-permute-start.11) | collective-permute-done | bytes 4128 | tf_op jit(solution)/shard_map/ppermute | solution.py:450
  77.7 1.0 %gradient.1 = bf16[8,64,128]{2,1,0:T(8,128)(2,1)S(1)} custom-call(f32[8,128]{1,0:T(8,128)S(1)} %get-tuple-element.33.own_ref, f32[8,128]{1,0:T(8,128)S(1)} %collective-permute-done.11.other_ref, f32[40,128]{1,0:T(8,128)S(1)} %pad.9.pack_ref, bf16[768,128]{1,0:T(8,128)(2,1)S(1)} %get-tuple-element.34.late_mask_ref, ...), custom_call_target="tpu_custom_call" | custom-call | tf_op jit(solution)/shard_map/gradient/pallas_call | solution.py:400
  78.8 12.6 %all_to_all.15.parts_ref = bf16[8,64,128]{2,1,0:T(8,128)(2,1)S(1)} all-to-all(bf16[8,64,128]{2,1,0:T(8,128)(2,1)S(1)} %gradient.1), channel_id=1, replica_groups=mesh['groups'=2,'dp'=8,'mp'=2] {'dp'}, dimensions={0} | all-to-all | bytes 262144 | tf_op jit(solution)/shard_map/all_to_all | solution.py:454
  91.3 0.6 add_up.1
  (59 shorter events, 0.8 us)
Async XLA Ops:
  0.6 12.2 %copy-start.3 = (s32[128,4]{0,1:T(4,128)S(1)}, s32[128,4]{0,1:T(4,128)}, u32[]{:S(2)}) copy-start(s32[128,4]{0,1:T(4,128)} %param.10) | copy-start | bytes 6148
  0.6 12.2 %copy-start.5 = (s32[128,4]{0,1:T(4,128)S(1)}, s32[128,4]{0,1:T(4,128)}, u32[]{:S(2)}) copy-start(s32[128,4]{0,1:T(4,128)} %param.11) | copy-start | bytes 6148
  0.7 11.8 %copy-start = (bf16[128,3,2048]{2,0,1:T(8,128)(2,1)S(1)}, bf16[128,3,2048]{2,0,1:T(8,128)(2,1)}, u32[]{:S(2)}) copy-start(bf16[128,3,2048]{2,0,1:T(8,128)(2,1)} %param.8) | copy-start | bytes 4718596
  0.7 12.3 %copy-start.6 = (s32[1,4]{1,0:T(1,128)S(1)}, s32[1,4]{1,0:T(1,128)}, u32[]{:S(2)}) copy-start(s32[1,4]{1,0:T(1,128)} %param.13) | copy-start | bytes 52
  0.7 12.6 %copy-start.7 = (s32[128,1]{0,1:T(1,128)S(1)}, s32[128,1]{0,1:T(1,128)}, u32[]{:S(2)}) copy-start(s32[128,1]{0,1:T(1,128)} %param.9) | copy-start | bytes 1540
  0.7 12.8 %copy-start.4 = (bf16[128,4]{0,1:T(4,128)(2,1)S(1)}, bf16[128,4]{0,1:T(4,128)(2,1)}, u32[]{:S(2)}) copy-start(bf16[128,4]{0,1:T(4,128)(2,1)} %param.12) | copy-start | bytes 3076
  2.2 19.6 %all-to-all-start = ((s32[8,2,128]{2,1,0:T(2,128)}), s32[8,2,128]{2,1,0:T(2,128)S(1)}, u32[]{:S(2)}, u32[]{:S(2)}) async-start(s32[8,2,128]{2,1,0:T(2,128)} %bitcast.43), calls=%async_computation | async-start | bytes 16384 | tf_op jit(solution)/shard_map/all_to_all | solution.py:454
  9.4 23.5 %collective-permute-start.6 = (bf16[256,384]{1,0:T(8,128)(2,1)S(1)}, bf16[256,384]{1,0:T(8,128)(2,1)S(1)}, u32[]{:S(2)}, u32[]{:S(2)}) collective-permute-start(bf16[256,384]{1,0:T(8,128)(2,1)S(1)} %get-tuple-element.27), channel_id=1, source_target_pairs={{0,8},{2,10},{4,12},{6,14},{8,0},{10,2},{12,4},{14,6},{1,9},{3,11}... | collective-permute-start | bytes 589832 | tf_op jit(solution)/shard_map/ppermute | solution.py:487
  12.4 19.0 %collective-permute-start.1 = (bf16[256,256]{1,0:T(8,128)(2,1)S(1)}, bf16[256,256]{1,0:T(8,128)(2,1)S(1)}, u32[]{:S(2)}, u32[]{:S(2)}) collective-permute-start(bf16[256,256]{1,0:T(8,128)(2,1)S(1)} %get-tuple-element.21), channel_id=1, source_target_pairs={{0,8},{2,10},{4,12},{6,14},{8,0},{10,2},{12,4},{14,6},{1,9},{3,11}... | collective-permute-start | bytes 393224 | tf_op jit(solution)/shard_map/ppermute | solution.py:487
  12.8 16.5 %collective-permute-start = (f32[3,128]{1,0:T(4,128)S(1)}, f32[3,128]{1,0:T(4,128)S(1)}, u32[]{:S(2)}, u32[]{:S(2)}) collective-permute-start(f32[3,128]{1,0:T(4,128)S(1)} %fusion), channel_id=1, source_target_pairs={{0,1},{1,0},{2,3},{3,2},{4,5},{5,4},{6,7},{7,6},{8,9},{9,8},{10,11... | collective-permute-start | bytes 4616 | tf_op jit(solution)/shard_map/ppermute | solution.py:450
  25.5 3.8 %copy-start.2 = (f32[3,2048]{1,0:T(4,128)S(1)}, f32[3,2048]{1,0:T(4,128)}, u32[]{:S(2)}) copy-start(f32[3,2048]{1,0:T(4,128)} %param.14) | copy-start | bytes 73732
  25.5 48.4 %all-to-all-start.1 = ((bf16[8,96,1408]{2,1,0:T(8,128)(2,1)}), bf16[8,96,1408]{2,1,0:T(8,128)(2,1)S(1)}, u32[]{:S(2)}, u32[]{:S(2)}) async-start(bf16[8,96,1408]{2,1,0:T(8,128)(2,1)} %bitcast.38), calls=%async_computation.1 | async-start | bytes 4325376 | tf_op jit(solution)/shard_map/all_to_all | solution.py:454
  31.3 5.0 %collective-permute-start.2 = (bf16[256,256]{1,0:T(8,128)(2,1)S(1)}, bf16[256,256]{1,0:T(8,128)(2,1)S(1)}, u32[]{:S(2)}, u32[]{:S(2)}) collective-permute-start(bf16[256,256]{1,0:T(8,128)(2,1)S(1)} %collective-permute-done.1.near_ref), channel_id=1, source_target_pairs={{0,16},{16,0},{1,17},{17,1},{2,18},{18,2},{3,19},{19,3},{4,20},{20... | collective-permute-start | bytes 393224 | tf_op jit(solution)/shard_map/ppermute | solution.py:503
  32.9 11.0 %collective-permute-start.7 = (bf16[256,384]{1,0:T(8,128)(2,1)S(1)}, bf16[256,384]{1,0:T(8,128)(2,1)S(1)}, u32[]{:S(2)}, u32[]{:S(2)}) collective-permute-start(bf16[256,384]{1,0:T(8,128)(2,1)S(1)} %collective-permute-done.6.near_ref), channel_id=1, source_target_pairs={{0,16},{16,0},{1,17},{17,1},{2,18},{18,2},{3,19},{19,3},{4,20},{20... | collective-permute-start | bytes 589832 | tf_op jit(solution)/shard_map/ppermute | solution.py:503
  38.4 10.8 %collective-permute-start.3 = (bf16[192,256]{1,0:T(8,128)(2,1)}, bf16[192,256]{1,0:T(8,128)(2,1)S(1)}, u32[]{:S(2)}, u32[]{:S(2)}) collective-permute-start(bf16[192,256]{1,0:T(8,128)(2,1)} %get-tuple-element.24), channel_id=1, source_target_pairs={{0,2},{2,0},{4,6},{6,4},{8,10},{10,8},{12,14},{14,12},{1,3},{3,1},... | collective-permute-start | bytes 294920 | tf_op jit(solution)/shard_map/ppermute | solution.py:507
  40.6 26.1 %collective-permute-start.4 = (bf16[192,256]{1,0:T(8,128)(2,1)}, bf16[192,256]{1,0:T(8,128)(2,1)S(1)}, u32[]{:S(2)}, u32[]{:S(2)}) collective-permute-start(bf16[192,256]{1,0:T(8,128)(2,1)} %get-tuple-element.25), channel_id=1, source_target_pairs={{0,4},{2,6},{4,0},{6,2},{8,12},{10,14},{12,8},{14,10},{1,5},{3,7},... | collective-permute-start | bytes 294920 | tf_op jit(solution)/shard_map/ppermute | solution.py:507
  43.9 23.8 %collective-permute-start.5 = (bf16[192,256]{1,0:T(8,128)(2,1)}, bf16[192,256]{1,0:T(8,128)(2,1)S(1)}, u32[]{:S(2)}, u32[]{:S(2)}) collective-permute-start(bf16[192,256]{1,0:T(8,128)(2,1)} %get-tuple-element.26), channel_id=1, source_target_pairs={{0,6},{2,4},{4,2},{6,0},{8,14},{10,12},{12,10},{14,8},{1,7},{3,5},... | collective-permute-start | bytes 294920 | tf_op jit(solution)/shard_map/ppermute | solution.py:507
  46.3 23.1 %collective-permute-start.10 = (bf16[192,384]{1,0:T(8,128)(2,1)}, bf16[192,384]{1,0:T(8,128)(2,1)S(1)}, u32[]{:S(2)}, u32[]{:S(2)}) collective-permute-start(bf16[192,384]{1,0:T(8,128)(2,1)} %get-tuple-element.32), channel_id=1, source_target_pairs={{0,6},{2,4},{4,2},{6,0},{8,14},{10,12},{12,10},{14,8},{1,7},{3,5},... | collective-permute-start | bytes 442376 | tf_op jit(solution)/shard_map/ppermute | solution.py:507
  49.2 20.1 %collective-permute-start.8 = (bf16[192,384]{1,0:T(8,128)(2,1)}, bf16[192,384]{1,0:T(8,128)(2,1)S(1)}, u32[]{:S(2)}, u32[]{:S(2)}) collective-permute-start(bf16[192,384]{1,0:T(8,128)(2,1)} %get-tuple-element.30), channel_id=1, source_target_pairs={{0,2},{2,0},{4,6},{6,4},{8,10},{10,8},{12,14},{14,12},{1,3},{3,1},... | collective-permute-start | bytes 442376 | tf_op jit(solution)/shard_map/ppermute | solution.py:507
  49.3 21.6 %collective-permute-start.9 = (bf16[192,384]{1,0:T(8,128)(2,1)}, bf16[192,384]{1,0:T(8,128)(2,1)S(1)}, u32[]{:S(2)}, u32[]{:S(2)}) collective-permute-start(bf16[192,384]{1,0:T(8,128)(2,1)} %get-tuple-element.31), channel_id=1, source_target_pairs={{0,4},{2,6},{4,0},{6,2},{8,12},{10,14},{12,8},{14,10},{1,5},{3,7},... | collective-permute-start | bytes 442376 | tf_op jit(solution)/shard_map/ppermute | solution.py:507
  73.9 3.9 %copy-start.1 = (bf16[128,3,2048]{2,0,1:T(8,128)(2,1)S(1)}, bf16[128,3,2048]{2,0,1:T(8,128)(2,1)}, u32[]{:S(2)}) copy-start(bf16[128,3,2048]{2,0,1:T(8,128)(2,1)} %param.8) | copy-start | bytes 4718596
  76.5 1.2 %collective-permute-start.11 = (f32[8,128]{1,0:T(8,128)S(1)}, f32[8,128]{1,0:T(8,128)S(1)}, u32[]{:S(2)}, u32[]{:S(2)}) collective-permute-start(f32[8,128]{1,0:T(8,128)S(1)} %get-tuple-element.33.own_ref), channel_id=1, source_target_pairs={{0,1},{1,0},{2,3},{3,2},{4,5},{5,4},{6,7},{7,6},{8,9},{9,8},{10,11... | collective-permute-start | bytes 12296 | tf_op jit(solution)/shard_map/ppermute | solution.py:450

commit v7 on v6

--- a/solution.py
+++ b/solution.py
@@ -12,7 +12,7 @@
 F32 = jnp.float32
 BF16 = jnp.bfloat16
 VMEM_LIMIT = 16 * 1024 * 1024
-CHUNKS = (256, 384)
+CHUNKS = (384, 256)
 
 
 def iota(shape, axis):
@@ -182,39 +182,45 @@
         start += refs[i].shape[1]
 
 
-def score_kernel(pack_ref, mixed_hbm, late_ref, *refs, used, parts):
-    *early_refs, out_ref, late_mask_ref, early_mask_ref, mixed_ref, sems = refs
-    arrivals = fetch(mixed_hbm, mixed_ref, sems)
-    shards, rows = out_ref.shape
-    spread = late_ref.shape[0] // shards
-    late = late_ref.shape[1]
-    late_mask = slot_mask(pack_ref[:shards, :], spread).astype(F32)
-    early_mask = slot_mask(pack_ref[shards : 2 * shards, :], spread).astype(F32)
-    late_mask_ref[...] = late_mask.reshape(late_mask_ref.shape).astype(BF16)
-    early_mask_ref[...] = early_mask.reshape(early_mask_ref.shape).astype(BF16)
-    flags = flags_of(pack_ref, shards, used)
-    for copy in arrivals:
-        copy.wait()
-
-    def scored(rows_ref, mixed, mask):
-        score = lax.dot_general(
-            rows_ref[...], mixed, (((1,), (1,)), ((), ())), preferred_element_type=F32
-        )
-        score = (score[:, :rows] + score[:, rows:]).reshape(mask.shape)
-        return jnp.sum(score * mask, axis=1)
-
-    total = scored(late_ref, mixed_ref[:, :late], late_mask)
-    for group, start in chunks_of(early_refs, parts, late):
-        lines, each = [], shards // parts
+def slot_sums(fetched, mixed, mask):
+    rows = mask.shape[2]
+    score = lax.dot_general(
+        fetched, mixed, (((1,), (1,)), ((), ())), preferred_element_type=F32
+    )
+    score = (score[:, :rows] + score[:, rows:]).reshape(mask.shape)
+    return jnp.sum(score * mask, axis=1)
+
+
+def early_score_kernel(pack_ref, mixed_hbm, *refs, used, parts):
+    *early_refs, out_ref, mixed_ref, sem = refs
+    shards = out_ref.shape[0]
+    wide = mixed_ref.shape[1]
+    late = mixed_hbm.shape[1] - wide
+    copy = pltpu.make_async_copy(mixed_hbm.at[:, pl.ds(late, wide)], mixed_ref, sem)
+    copy.start()
+    each = shards // parts
+    mask = slot_mask(pack_ref[shards : 2 * shards, :], early_refs[0].shape[0] // each).astype(F32)
+    copy.wait()
+    lines = [0.0] * parts
+    for group, start in chunks_of(early_refs, parts, 0):
         for i, early_ref in enumerate(group):
             mixed = mixed_ref[:, pl.ds(start, early_ref.shape[1])]
-            lines.append(scored(early_ref, mixed, early_mask[i * each : (i + 1) * each]))
-        total = total + from_pairs(jnp.concatenate(lines, axis=0), flags)
-    out_ref[...] = total
+            lines[i] += slot_sums(early_ref[...], mixed, mask[i * each : (i + 1) * each])
+    out_ref[...] = from_pairs(jnp.concatenate(lines, axis=0), flags_of(pack_ref, shards, used))
+
+
+def score_kernel(pack_ref, early_ref, mixed_hbm, late_ref, out_ref, mask_ref, mixed_ref, sem):
+    shards = out_ref.shape[0]
+    copy = pltpu.make_async_copy(mixed_hbm.at[:, pl.ds(0, late_ref.shape[1])], mixed_ref, sem)
+    copy.start()
+    mask = slot_mask(pack_ref[:shards, :], late_ref.shape[0] // shards).astype(F32)
+    mask_ref[...] = mask.reshape(mask_ref.shape).astype(BF16)
+    copy.wait()
+    out_ref[...] = slot_sums(late_ref[...], mixed_ref[...], mask) + early_ref[...]
 
 
 def grad_kernel(
-    own_ref, other_ref, pack_ref, late_mask_ref, early_mask_ref, late_ref, *refs, top, used, parts
+    own_ref, other_ref, pack_ref, late_mask_ref, late_ref, *refs, top, used, parts
 ):
     *early_refs, hidden_ref, out_ref, grad_ref = refs
     layers, rows, features = hidden_ref.shape
@@ -250,7 +256,9 @@
 
     late = late_ref.shape[1]
     pairs = to_pairs(by_shard, flags)
-    part = spread_out(early_mask_ref[...], pairs)
+    spread = late_mask_ref.shape[0] // shards
+    early_mask = slot_mask(pack_ref[shards : 2 * shards, :], spread)
+    part = spread_out(early_mask, pairs)
     each = part.shape[0] // parts
     part = [part[i * each : (i + 1) * each] for i in range(parts)]
     sources = [([late_ref], [spread_out(late_mask_ref[...], by_shard)], 0)]
@@ -375,31 +383,43 @@
     )(asked, in_hbm(head), near, far)
 
 
-def score(pack, mixed, late, early, shards, used, parts):
+def score_early(pack, mixed, early, shards, used, parts):
     rows = pack.shape[1]
-    slots = sum(array.shape[0] for array in early[:parts])
-    return pl.pallas_call(
-        functools.partial(score_kernel, used=used, parts=parts),
-        in_specs=[VMEM, HBM, VMEM] + [VMEM] * len(early),
-        out_specs=[VMEM] * 3,
+    wide = sum(array.shape[1] for array in early[::parts])
+    return pl.pallas_call(
+        functools.partial(early_score_kernel, used=used, parts=parts),
+        in_specs=[VMEM, HBM] + [VMEM] * len(early),
+        out_specs=VMEM,
+        out_shape=jax.ShapeDtypeStruct((shards, rows), F32),
+        scratch_shapes=[pltpu.VMEM((mixed.shape[0], wide), BF16), pltpu.SemaphoreType.DMA(())],
+        compiler_params=params(),
+        name="score_early",
+    )(pack, in_hbm(mixed), *early)
+
+
+def score(pack, early, mixed, late, shards):
+    rows = pack.shape[1]
+    return pl.pallas_call(
+        score_kernel,
+        in_specs=[VMEM, VMEM, HBM, VMEM],
+        out_specs=[VMEM] * 2,
         out_shape=[
             jax.ShapeDtypeStruct((shards, rows), F32),
             jax.ShapeDtypeStruct((late.shape[0], rows), BF16),
-            jax.ShapeDtypeStruct((slots, rows), BF16),
         ],
         scratch_shapes=[
-            pltpu.VMEM(mixed.shape, BF16),
-            pltpu.SemaphoreType.DMA((len(pieces(mixed.shape[1])),)),
+            pltpu.VMEM((mixed.shape[0], late.shape[1]), BF16),
+            pltpu.SemaphoreType.DMA(()),
         ],
         compiler_params=params(),
         name="score",
-    )(pack, in_hbm(mixed), late, *early)
-
-
-def gradient(own, other, pack, masks, late, early, hidden, lines, total_lines, top, used, parts):
+    )(pack, early, in_hbm(mixed), late)
+
+
+def gradient(own, other, pack, mask, late, early, hidden, lines, total_lines, top, used, parts):
     return pl.pallas_call(
         functools.partial(grad_kernel, top=top, used=used, parts=parts),
-        in_specs=[VMEM] * (7 + len(early)),
+        in_specs=[VMEM] * (6 + len(early)),
         out_specs=VMEM,
         out_shape=jax.ShapeDtypeStruct((own.shape[0], total_lines, 128), BF16),
         scratch_shapes=[
@@ -407,7 +427,7 @@
         ],
         compiler_params=params(),
         name="gradient",
-    )(own, other, pack, *masks, late, *early, hidden)
+    )(own, other, pack, mask, late, *early, hidden)
 
 
 def after(value, first):
@@ -511,6 +531,7 @@
             rows_here = [rows_here.reshape(peers * spread, -1)]
         rows_early += rows_here
 
+    hidden, layer_mix = after((hidden, layer_mix), picked)
     number = jnp.arange(peers, dtype=jnp.int32)[:, None]
     asked = jnp.max(
         jnp.where(shard[:, None, :] == number[None], offset[:, None, :], -1), axis=0
@@ -539,10 +560,11 @@
     slots = peers * capacity
     lines = layers * features // 128
     total_lines = lines + 2 * top * slots // 128
-    own, *masks = score(pack, mixed, rows_late, rows_early, peers, used, parts)
+    early = score_early(pack, mixed, rows_early, peers, used, parts)
+    own, mask = score(pack, early, mixed, rows_late, peers)
     other = swap_cores(own)
     sent = gradient(
-        own, other, pack, masks, rows_late, rows_early, tokens, lines, total_lines, top, used, parts
+        own, other, pack, mask, rows_late, rows_early, tokens, lines, total_lines, top, used, parts
     )
     grad, logp = add_up(exchange(sent), layers, features, top, slots)
     return (logp.T[None], grad)

time: 92.5 us -> 93.4 us (level)
  waiting for transfers between devices: 34.9 us -> 29.1 us
  starting transfers between devices: 25.1 us -> 28.3 us
  blocking collectives: 12.6 us -> 14.5 us
    all_to_all x2, waiting for transfers between devices: 11 us -> 5.79 us  [exchange(): lax.all_to_all(value, 'dp', split_axis=0, concat_axis=0, tiled=True, axis...]
    ppermute x6, starting transfers between devices: 8.94 us -> 12 us  [local(): lax.ppermute(rows_here[i], 'dp', [(j, j ^ i) for j in range(peers)])]
    ppermute x6, waiting for transfers between devices: 19.8 us -> 17.3 us  [local(): lax.ppermute(rows_here[i], 'dp', [(j, j ^ i) for j in range(peers)])]
    all_to_all x1, blocking collectives: 12.6 us -> 14.5 us  [exchange(): lax.all_to_all(value, 'dp', split_axis=0, concat_axis=0, tiled=True, axis...]
    reduce_sum x1, other arithmetic: 1.95 us -> 0.45 us  [local(): mixed = jnp.sum(wide * layer_mix[:, None, :] * inverse[:, :, None], axis=0)]
    reduce_sum x1, other arithmetic: 0.38 us -> 1.83 us  [local(): squares = jnp.sum(wide * wide, axis=2)]
    ppermute x2, waiting for transfers between devices: 1.16 us -> 2.21 us  [swap_cores(): return lax.ppermute(value, 'mp', [(i, i ^ 1) for i in range(size)])]
    pallas_call x1 -> x2, Pallas kernels: 2.64 us -> 3.67 us  [the longest x1 2.07 us: score(): pl.pallas_call(score_kernel, in_specs=[VMEM, VMEM, HBM, VMEM], out_specs=...]
  transfers between devices with their start and end apart: 14 -> 14, of which waited for: 8 -> 9; matrix products, arithmetic and copies ran while one was open for 5% -> 6% of each run, Pallas kernels for 9% -> 10%
where the time goes in v7:
time: 93.4 us; the launch traced here: 92.8 us
  waiting for transfers between devices  29.1 us (31%)
  starting transfers between devices  28.3 us (30%)
  Pallas kernels  14.7 us (16%)
  blocking collectives  14.5 us (16%)
  other arithmetic  4.98 us (5%)
  between operations  1 us (1%)
    ppermute x6, waiting for transfers between devices, local(): lax.ppermute(rows_here[i], 'dp', [(j, j ^ i) for j in range(peers)])  17.3 us
    all_to_all x1, blocking collectives, exchange(): lax.all_to_all(value, 'dp', split_axis=0, concat_axis=0, tiled=True, axis...  14.5 us
    ppermute x6, starting transfers between devices, local(): lax.ppermute(rows_here[i], 'dp', [(j, j ^ i) for j in range(peers)])  12 us
    all_to_all x2, starting transfers between devices, exchange(): lax.all_to_all(value, 'dp', split_axis=0, concat_axis=0, tiled=True, axis...  11 us
    all_to_all x2, waiting for transfers between devices, exchange(): lax.all_to_all(value, 'dp', split_axis=0, concat_axis=0, tiled=True, axis...  5.79 us
    pallas_call x2, Pallas kernels, pick_early(): pl.pallas_call(functools.partial(early_kernel, spread=spread, start=start...  4.38 us
    ppermute x2, waiting for transfers between devices, local(): far = lax.ppermute(near, 'groups', [(0, 1), (1, 0)])  3.79 us
    pallas_call x1, Pallas kernels, pick(): pl.pallas_call(functools.partial(pick_kernel, spread=spread), in_specs=[V...  3.67 us
  transfers between devices with their start and end apart: 14, of which 9 were waited for; matrix products, arithmetic and copies ran while one was open for 6% of the time, Pallas kernels for 10%

profile of v7, /device:TPU:0, one launch (start us, length us, event | category | flops | bytes accessed | tf_op | source)
XLA Modules:
  0.0 92.8 jit_solution(3845845657543680349)
XLA Ops:
  0.7 1.4 %begin.1 = (s32[16,128]{1,0:T(8,128)}, bf16[256,384]{1,0:T(8,128)(2,1)S(1)}, bf16[256,256]{1,0:T(8,128)(2,1)S(1)}) custom-call(s32[1]{0:T(128)} %bitcast.10.group_ref, s32[4,128]{1,0:T(4,128)} %bitcast.39, s32[4,128]{1,0:T(4,128)} %bitcast.41, bf16[512,2048]{1,0:T(8,128)(2,1)} %head_hbm.7), custom_call_target="tpu_custom_call" | custom-call | tf_op jit(solution)/shard_map/begin/pallas_call | solution.py:350
  2.0 7.3 %all-to-all-start = ((s32[8,2,128]{2,1,0:T(2,128)}), s32[8,2,128]{2,1,0:T(2,128)S(1)}, u32[]{:S(2)}, u32[]{:S(2)}) async-start(s32[8,2,128]{2,1,0:T(2,128)} %bitcast.43), calls=%async_computation | async-start | bytes 16384 | tf_op jit(solution)/shard_map/all_to_all | solution.py:474
  9.3 2.9 %collective-permute-start.6 = (bf16[256,256]{1,0:T(8,128)(2,1)S(1)}, bf16[256,256]{1,0:T(8,128)(2,1)S(1)}, u32[]{:S(2)}, u32[]{:S(2)}) collective-permute-start(bf16[256,256]{1,0:T(8,128)(2,1)S(1)} %get-tuple-element.30), channel_id=1, source_target_pairs={{0,8},{2,10},{4,12},{6,14},{8,0},{10,2},{12,4},{14,6},{1,9},{3,11}... | collective-permute-start | bytes 393224 | tf_op jit(solution)/shard_map/ppermute | solution.py:507
  12.3 0.7 select_reduce_fusion
  13.0 0.2 reduce-window.7
  13.4 2.6 %all-to-all-done = s32[8,2,128]{2,1,0:T(2,128)S(1)} async-done(((s32[8,2,128]{2,1,0:T(2,128)}), s32[8,2,128]{2,1,0:T(2,128)S(1)}, u32[]{:S(2)}, u32[]{:S(2)}) %all-to-all-start) | async-done | bytes 8224 | tf_op jit(solution)/shard_map/all_to_all | solution.py:474
  16.0 3.7 %pick.1 = bf16[768,1408]{1,0:T(8,128)(2,1)} custom-call(s32[16,128]{1,0:T(8,128)S(1)} %bitcast.35, bf16[512,2048]{1,0:T(8,128)(2,1)} %head_hbm.7), custom_call_target="tpu_custom_call" | custom-call | tf_op jit(solution)/shard_map/pick/pallas_call | solution.py:332
  19.7 3.7 %all-to-all-start.1 = ((bf16[8,96,1408]{2,1,0:T(8,128)(2,1)}), bf16[8,96,1408]{2,1,0:T(8,128)(2,1)S(1)}, u32[]{:S(2)}, u32[]{:S(2)}) async-start(bf16[8,96,1408]{2,1,0:T(8,128)(2,1)} %bitcast.38), calls=%async_computation.1 | async-start | bytes 4325376 | tf_op jit(solution)/shard_map/all_to_all | solution.py:474
  24.0 1.8 %fusion = f32[3,128]{1,0:T(4,128)S(1)} fusion(bf16[128,3,2048]{2,0,1:T(8,128)(2,1)} %param.8), kind=kLoop, calls=%fused_computation.2 | loop fusion | flops 2358912 | bytes 1574400 | tf_op jit(solution)/shard_map/reduce_sum | solution.py:541
  26.0 1.1 %collective-permute-done = f32[3,128]{1,0:T(4,128)S(1)} collective-permute-done((f32[3,128]{1,0:T(4,128)S(1)}, f32[3,128]{1,0:T(4,128)S(1)}, u32[]{:S(2)}, u32[]{:S(2)}) %collective-permute-start) | collective-permute-done | bytes 1568 | tf_op jit(solution)/shard_map/ppermute | solution.py:470
  27.0 1.6 %collective-permute-start.7 = (bf16[256,256]{1,0:T(8,128)(2,1)S(1)}, bf16[256,256]{1,0:T(8,128)(2,1)S(1)}, u32[]{:S(2)}, u32[]{:S(2)}) collective-permute-start(bf16[256,256]{1,0:T(8,128)(2,1)S(1)} %collective-permute-done.6.near_ref), channel_id=1, source_target_pairs={{0,16},{16,0},{1,17},{17,1},{2,18},{18,2},{3,19},{19,3},{4,20},{20... | collective-permute-start | bytes 393224 | tf_op jit(solution)/shard_map/ppermute | solution.py:523
  28.6 0.4 fusion.2
  29.1 0.6 collective-permute-start.2
  29.7 3.8 %collective-permute-done.7.far_ref = bf16[256,256]{1,0:T(8,128)(2,1)S(1)} collective-permute-done((bf16[256,256]{1,0:T(8,128)(2,1)S(1)}, bf16[256,256]{1,0:T(8,128)(2,1)S(1)}, u32[]{:S(2)}, u32[]{:S(2)}) %collective-permute-start.7) | collective-permute-done | bytes 131104 | tf_op jit(solution)/shard_map/ppermute | solution.py:523
  33.4 2.1 %pick_early.3 = (bf16[192,256]{1,0:T(8,128)(2,1)S(1)}, bf16[192,256]{1,0:T(8,128)(2,1)}, bf16[192,256]{1,0:T(8,128)(2,1)}, bf16[192,256]{1,0:T(8,128)(2,1)}) custom-call(s32[8,128]{1,0:T(8,128)S(1)} %add_select_fusion.3.asked_ref, bf16[512,2048]{1,0:T(8,128)(2,1)} %head_hbm.7, bf16[256,256]{1,0:T(8,128)(2,1)S(1)} %collective-permute-done.6.near_ref, ...), custom_call_target="tpu_custom_call" | custom-call | tf_op jit(solution)/shard_map/pick_early/pallas_call | solution.py:370
  35.5 2.0 %collective-permute-start.8 = (bf16[192,256]{1,0:T(8,128)(2,1)}, bf16[192,256]{1,0:T(8,128)(2,1)S(1)}, u32[]{:S(2)}, u32[]{:S(2)}) collective-permute-start(bf16[192,256]{1,0:T(8,128)(2,1)} %get-tuple-element.33), channel_id=1, source_target_pairs={{0,2},{2,0},{4,6},{6,4},{8,10},{10,8},{12,14},{14,12},{1,3},{3,1},... | collective-permute-start | bytes 294920 | tf_op jit(solution)/shard_map/ppermute | solution.py:527
  37.7 6.4 %collective-permute-start.9 = (bf16[192,256]{1,0:T(8,128)(2,1)}, bf16[192,256]{1,0:T(8,128)(2,1)S(1)}, u32[]{:S(2)}, u32[]{:S(2)}) collective-permute-start(bf16[192,256]{1,0:T(8,128)(2,1)} %get-tuple-element.34), channel_id=1, source_target_pairs={{0,4},{2,6},{4,0},{6,2},{8,12},{10,14},{12,8},{14,10},{1,5},{3,7},... | collective-permute-start | bytes 294920 | tf_op jit(solution)/shard_map/ppermute | solution.py:527
  44.1 2.3 %pick_early.2 = (bf16[192,384]{1,0:T(8,128)(2,1)S(1)}, bf16[192,384]{1,0:T(8,128)(2,1)}, bf16[192,384]{1,0:T(8,128)(2,1)}, bf16[192,384]{1,0:T(8,128)(2,1)}) custom-call(s32[8,128]{1,0:T(8,128)S(1)} %add_select_fusion.3.asked_ref, bf16[512,2048]{1,0:T(8,128)(2,1)} %head_hbm.7, bf16[256,384]{1,0:T(8,128)(2,1)S(1)} %collective-permute-done.1.near_ref, ...), custom_call_target="tpu_custom_call" | custom-call | tf_op jit(solution)/shard_map/pick_early/pallas_call | solution.py:370
  46.5 1.6 %collective-permute-start.3 = (bf16[192,384]{1,0:T(8,128)(2,1)}, bf16[192,384]{1,0:T(8,128)(2,1)S(1)}, u32[]{:S(2)}, u32[]{:S(2)}) collective-permute-start(bf16[192,384]{1,0:T(8,128)(2,1)} %get-tuple-element.27), channel_id=1, source_target_pairs={{0,2},{2,0},{4,6},{6,4},{8,10},{10,8},{12,14},{14,12},{1,3},{3,1},... | collective-permute-start | bytes 442376 | tf_op jit(solution)/shard_map/ppermute | solution.py:527
  48.1 1.9 %collective-permute-start.4 = (bf16[192,384]{1,0:T(8,128)(2,1)}, bf16[192,384]{1,0:T(8,128)(2,1)S(1)}, u32[]{:S(2)}, u32[]{:S(2)}) collective-permute-start(bf16[192,384]{1,0:T(8,128)(2,1)} %get-tuple-element.28), channel_id=1, source_target_pairs={{0,4},{2,6},{4,0},{6,2},{8,12},{10,14},{12,8},{14,10},{1,5},{3,7},... | collective-permute-start | bytes 442376 | tf_op jit(solution)/shard_map/ppermute | solution.py:527
  50.0 1.1 %pad_maximum_fusion.mixed_hbm = bf16[256,2048]{1,0:T(8,128)(2,1)} fusion(bf16[128,2048]{1,0:T(8,128)(2,1)S(1)} %get-tuple-element.41, bf16[128,2048]{1,0:T(8,128)(2,1)S(1)} %get-tuple-element.40), kind=kLoop, calls=%fused_computation.8 | loop fusion | flops 2097152 | bytes 2097152 | tf_op jit(solution)/shard_map/concatenate | solution.py:546
  51.2 11.3 %collective-permute-done.9.refs_6_ = bf16[192,256]{1,0:T(8,128)(2,1)S(1)} collective-permute-done((bf16[192,256]{1,0:T(8,128)(2,1)}, bf16[192,256]{1,0:T(8,128)(2,1)S(1)}, u32[]{:S(2)}, u32[]{:S(2)}) %collective-permute-start.9) | collective-permute-done | bytes 98336 | tf_op jit(solution)/shard_map/ppermute | solution.py:527
  62.5 2.1 %collective-permute-done.10.refs_7_ = bf16[192,256]{1,0:T(8,128)(2,1)S(1)} collective-permute-done((bf16[192,256]{1,0:T(8,128)(2,1)}, bf16[192,256]{1,0:T(8,128)(2,1)S(1)}, u32[]{:S(2)}, u32[]{:S(2)}) %collective-permute-start.10) | collective-permute-done | bytes 98336 | tf_op jit(solution)/shard_map/ppermute | solution.py:527
  64.6 2.3 %collective-permute-done.4.refs_2_ = bf16[192,384]{1,0:T(8,128)(2,1)S(1)} collective-permute-done((bf16[192,384]{1,0:T(8,128)(2,1)}, bf16[192,384]{1,0:T(8,128)(2,1)S(1)}, u32[]{:S(2)}, u32[]{:S(2)}) %collective-permute-start.4) | collective-permute-done | bytes 147488 | tf_op jit(solution)/shard_map/ppermute | solution.py:527
  66.9 1.6 %collective-permute-done.5.refs_3_ = bf16[192,384]{1,0:T(8,128)(2,1)S(1)} collective-permute-done((bf16[192,384]{1,0:T(8,128)(2,1)}, bf16[192,384]{1,0:T(8,128)(2,1)S(1)}, u32[]{:S(2)}, u32[]{:S(2)}) %collective-permute-start.5) | collective-permute-done | bytes 147488 | tf_op jit(solution)/shard_map/ppermute | solution.py:527
  68.5 1.6 %score_early.1.early_ref = f32[8,128]{1,0:T(8,128)S(1)} custom-call(f32[40,128]{1,0:T(8,128)S(1)} %pad.9.pack_ref, bf16[256,2048]{1,0:T(8,128)(2,1)} %pad_maximum_fusion.mixed_hbm, bf16[192,384]{1,0:T(8,128)(2,1)S(1)} %get-tuple-element.26.refs_0_, bf16[192,384]{1,0:T(8,128)(2,1)S(1)} %collective-permute-done.3.refs_1_, ...), custom_call_target="tpu_custom_call" | custom-call | tf_op jit(solution)/shard_map/score_early/pallas_call | solution.py:389
  70.1 3.2 %all-to-all-done.1 = bf16[8,96,1408]{2,1,0:T(8,128)(2,1)S(1)} async-done(((bf16[8,96,1408]{2,1,0:T(8,128)(2,1)}), bf16[8,96,1408]{2,1,0:T(8,128)(2,1)S(1)}, u32[]{:S(2)}, u32[]{:S(2)}) %all-to-all-start.1) | async-done | bytes 2162720 | tf_op jit(solution)/shard_map/all_to_all | solution.py:474
  73.4 2.1 %score.1 = (f32[8,128]{1,0:T(8,128)S(1)}, bf16[768,128]{1,0:T(8,128)(2,1)S(1)}) custom-call(f32[40,128]{1,0:T(8,128)S(1)} %pad.9.pack_ref, f32[8,128]{1,0:T(8,128)S(1)} %score_early.1.early_ref, bf16[256,2048]{1,0:T(8,128)(2,1)} %pad_maximum_fusion.mixed_hbm, bf16[768,1408]{1,0:T(8,128)(2,1)S(1)} %bitcast.32), custom_call_target="tpu_custom_call" | custom-call | tf_op jit(solution)/shard_map/score/pallas_call | solution.py:402
  75.5 1.2 %collective-permute-done.11.other_ref = f32[8,128]{1,0:T(8,128)S(1)} collective-permute-done((f32[8,128]{1,0:T(8,128)S(1)}, f32[8,128]{1,0:T(8,128)S(1)}, u32[]{:S(2)}, u32[]{:S(2)}) %collective-permute-start.11) | collective-permute-done | bytes 4128 | tf_op jit(solution)/shard_map/ppermute | solution.py:470
  76.7 1.0 %gradient.1 = bf16[8,64,128]{2,1,0:T(8,128)(2,1)S(1)} custom-call(f32[8,128]{1,0:T(8,128)S(1)} %get-tuple-element.36.own_ref, f32[8,128]{1,0:T(8,128)S(1)} %collective-permute-done.11.other_ref, f32[40,128]{1,0:T(8,128)S(1)} %pad.9.pack_ref, bf16[768,128]{1,0:T(8,128)(2,1)S(1)} %get-tuple-element.37.late_mask_ref, bf16[768,1408]{1,0:T(8,128)(2,1)S(1)} %bitcast.33, ...), custom_call_target="tpu_custom_call" | custom-call | tf_op jit(solution)/shard_map/gradient/pallas_call | solution.py:420
  77.7 14.5 %all_to_all.15.parts_ref = bf16[8,64,128]{2,1,0:T(8,128)(2,1)S(1)} all-to-all(bf16[8,64,128]{2,1,0:T(8,128)(2,1)S(1)} %gradient.1), channel_id=1, replica_groups=mesh['groups'=2,'dp'=8,'mp'=2] {'dp'}, dimensions={0} | all-to-all | bytes 262144 | tf_op jit(solution)/shard_map/all_to_all | solution.py:474
  92.2 0.6 add_up.1
  (58 shorter events, 1.2 us)
Async XLA Ops:
  0.6 12.3 %copy-start.5 = (s32[1,4]{1,0:T(1,128)S(1)}, s32[1,4]{1,0:T(1,128)}, u32[]{:S(2)}) copy-start(s32[1,4]{1,0:T(1,128)} %param.13) | copy-start | bytes 52
  0.6 12.5 %copy-start.4 = (bf16[128,4]{0,1:T(4,128)(2,1)S(1)}, bf16[128,4]{0,1:T(4,128)(2,1)}, u32[]{:S(2)}) copy-start(bf16[128,4]{0,1:T(4,128)(2,1)} %param.12) | copy-start | bytes 3076
  2.0 14.0 %all-to-all-start = ((s32[8,2,128]{2,1,0:T(2,128)}), s32[8,2,128]{2,1,0:T(2,128)S(1)}, u32[]{:S(2)}, u32[]{:S(2)}) async-start(s32[8,2,128]{2,1,0:T(2,128)} %bitcast.43), calls=%async_computation | async-start | bytes 16384 | tf_op jit(solution)/shard_map/all_to_all | solution.py:474
  9.3 17.7 %collective-permute-start.6 = (bf16[256,256]{1,0:T(8,128)(2,1)S(1)}, bf16[256,256]{1,0:T(8,128)(2,1)S(1)}, u32[]{:S(2)}, u32[]{:S(2)}) collective-permute-start(bf16[256,256]{1,0:T(8,128)(2,1)S(1)} %get-tuple-element.30), channel_id=1, source_target_pairs={{0,8},{2,10},{4,12},{6,14},{8,0},{10,2},{12,4},{14,6},{1,9},{3,11}... | collective-permute-start | bytes 393224 | tf_op jit(solution)/shard_map/ppermute | solution.py:507
  12.2 16.9 %collective-permute-start.1 = (bf16[256,384]{1,0:T(8,128)(2,1)S(1)}, bf16[256,384]{1,0:T(8,128)(2,1)S(1)}, u32[]{:S(2)}, u32[]{:S(2)}) collective-permute-start(bf16[256,384]{1,0:T(8,128)(2,1)S(1)} %get-tuple-element.24), channel_id=1, source_target_pairs={{0,8},{2,10},{4,12},{6,14},{8,0},{10,2},{12,4},{14,6},{1,9},{3,11}... | collective-permute-start | bytes 589832 | tf_op jit(solution)/shard_map/ppermute | solution.py:507
  19.7 3.9 %copy-start.6 = (s32[128,1]{0,1:T(1,128)S(1)}, s32[128,1]{0,1:T(1,128)}, u32[]{:S(2)}) copy-start(s32[128,1]{0,1:T(1,128)} %param.9) | copy-start | bytes 1540
  19.7 4.3 %copy-start.3 = (s32[128,4]{0,1:T(4,128)S(1)}, s32[128,4]{0,1:T(4,128)}, u32[]{:S(2)}) copy-start(s32[128,4]{0,1:T(4,128)} %param.10) | copy-start | bytes 6148
  19.7 8.9 %copy-start.2 = (f32[3,2048]{1,0:T(4,128)S(1)}, f32[3,2048]{1,0:T(4,128)}, u32[]{:S(2)}) copy-start(f32[3,2048]{1,0:T(4,128)} %param.14) | copy-start | bytes 73732
  19.7 53.7 %all-to-all-start.1 = ((bf16[8,96,1408]{2,1,0:T(8,128)(2,1)}), bf16[8,96,1408]{2,1,0:T(8,128)(2,1)S(1)}, u32[]{:S(2)}, u32[]{:S(2)}) async-start(bf16[8,96,1408]{2,1,0:T(8,128)(2,1)} %bitcast.38), calls=%async_computation.1 | async-start | bytes 4325376 | tf_op jit(solution)/shard_map/all_to_all | solution.py:474
  23.5 5.1 %copy-start = (bf16[128,3,2048]{2,0,1:T(8,128)(2,1)S(1)}, bf16[128,3,2048]{2,0,1:T(8,128)(2,1)}, u32[]{:S(2)}) copy-start(bf16[128,3,2048]{2,0,1:T(8,128)(2,1)} %param.8) | copy-start | bytes 4718596
  25.8 1.2 %collective-permute-start = (f32[3,128]{1,0:T(4,128)S(1)}, f32[3,128]{1,0:T(4,128)S(1)}, u32[]{:S(2)}, u32[]{:S(2)}) collective-permute-start(f32[3,128]{1,0:T(4,128)S(1)} %fusion), channel_id=1, source_target_pairs={{0,1},{1,0},{2,3},{3,2},{4,5},{5,4},{6,7},{7,6},{8,9},{9,8},{10,11... | collective-permute-start | bytes 4616 | tf_op jit(solution)/shard_map/ppermute | solution.py:470
  27.0 6.4 %collective-permute-start.7 = (bf16[256,256]{1,0:T(8,128)(2,1)S(1)}, bf16[256,256]{1,0:T(8,128)(2,1)S(1)}, u32[]{:S(2)}, u32[]{:S(2)}) collective-permute-start(bf16[256,256]{1,0:T(8,128)(2,1)S(1)} %collective-permute-done.6.near_ref), channel_id=1, source_target_pairs={{0,16},{16,0},{1,17},{17,1},{2,18},{18,2},{3,19},{19,3},{4,20},{20... | collective-permute-start | bytes 393224 | tf_op jit(solution)/shard_map/ppermute | solution.py:523
  29.1 15.0 %collective-permute-start.2 = (bf16[256,384]{1,0:T(8,128)(2,1)S(1)}, bf16[256,384]{1,0:T(8,128)(2,1)S(1)}, u32[]{:S(2)}, u32[]{:S(2)}) collective-permute-start(bf16[256,384]{1,0:T(8,128)(2,1)S(1)} %collective-permute-done.1.near_ref), channel_id=1, source_target_pairs={{0,16},{16,0},{1,17},{17,1},{2,18},{18,2},{3,19},{19,3},{4,20},{20... | collective-permute-start | bytes 589832 | tf_op jit(solution)/shard_map/ppermute | solution.py:523
  35.5 14.5 %collective-permute-start.8 = (bf16[192,256]{1,0:T(8,128)(2,1)}, bf16[192,256]{1,0:T(8,128)(2,1)S(1)}, u32[]{:S(2)}, u32[]{:S(2)}) collective-permute-start(bf16[192,256]{1,0:T(8,128)(2,1)} %get-tuple-element.33), channel_id=1, source_target_pairs={{0,2},{2,0},{4,6},{6,4},{8,10},{10,8},{12,14},{14,12},{1,3},{3,1},... | collective-permute-start | bytes 294920 | tf_op jit(solution)/shard_map/ppermute | solution.py:527
  37.7 24.8 %collective-permute-start.9 = (bf16[192,256]{1,0:T(8,128)(2,1)}, bf16[192,256]{1,0:T(8,128)(2,1)S(1)}, u32[]{:S(2)}, u32[]{:S(2)}) collective-permute-start(bf16[192,256]{1,0:T(8,128)(2,1)} %get-tuple-element.34), channel_id=1, source_target_pairs={{0,4},{2,6},{4,0},{6,2},{8,12},{10,14},{12,8},{14,10},{1,5},{3,7},... | collective-permute-start | bytes 294920 | tf_op jit(solution)/shard_map/ppermute | solution.py:527
  44.1 20.5 %collective-permute-start.10 = (bf16[192,256]{1,0:T(8,128)(2,1)}, bf16[192,256]{1,0:T(8,128)(2,1)S(1)}, u32[]{:S(2)}, u32[]{:S(2)}) collective-permute-start(bf16[192,256]{1,0:T(8,128)(2,1)} %get-tuple-element.35), channel_id=1, source_target_pairs={{0,6},{2,4},{4,2},{6,0},{8,14},{10,12},{12,10},{14,8},{1,7},{3,5},... | collective-permute-start | bytes 294920 | tf_op jit(solution)/shard_map/ppermute | solution.py:527
  46.5 18.1 %collective-permute-start.3 = (bf16[192,384]{1,0:T(8,128)(2,1)}, bf16[192,384]{1,0:T(8,128)(2,1)S(1)}, u32[]{:S(2)}, u32[]{:S(2)}) collective-permute-start(bf16[192,384]{1,0:T(8,128)(2,1)} %get-tuple-element.27), channel_id=1, source_target_pairs={{0,2},{2,0},{4,6},{6,4},{8,10},{10,8},{12,14},{14,12},{1,3},{3,1},... | collective-permute-start | bytes 442376 | tf_op jit(solution)/shard_map/ppermute | solution.py:527
  48.1 18.9 %collective-permute-start.4 = (bf16[192,384]{1,0:T(8,128)(2,1)}, bf16[192,384]{1,0:T(8,128)(2,1)S(1)}, u32[]{:S(2)}, u32[]{:S(2)}) collective-permute-start(bf16[192,384]{1,0:T(8,128)(2,1)} %get-tuple-element.28), channel_id=1, source_target_pairs={{0,4},{2,6},{4,0},{6,2},{8,12},{10,14},{12,8},{14,10},{1,5},{3,7},... | collective-permute-start | bytes 442376 | tf_op jit(solution)/shard_map/ppermute | solution.py:527
  50.0 18.5 %collective-permute-start.5 = (bf16[192,384]{1,0:T(8,128)(2,1)}, bf16[192,384]{1,0:T(8,128)(2,1)S(1)}, u32[]{:S(2)}, u32[]{:S(2)}) collective-permute-start(bf16[192,384]{1,0:T(8,128)(2,1)} %get-tuple-element.29), channel_id=1, source_target_pairs={{0,6},{2,4},{4,2},{6,0},{8,14},{10,12},{12,10},{14,8},{1,7},{3,5},... | collective-permute-start | bytes 442376 | tf_op jit(solution)/shard_map/ppermute | solution.py:527
  73.4 3.3 %copy-start.1 = (bf16[128,3,2048]{2,0,1:T(8,128)(2,1)S(1)}, bf16[128,3,2048]{2,0,1:T(8,128)(2,1)}, u32[]{:S(2)}) copy-start(bf16[128,3,2048]{2,0,1:T(8,128)(2,1)} %param.8) | copy-start | bytes 4718596
  75.4 1.2 %collective-permute-start.11 = (f32[8,128]{1,0:T(8,128)S(1)}, f32[8,128]{1,0:T(8,128)S(1)}, u32[]{:S(2)}, u32[]{:S(2)}) collective-permute-start(f32[8,128]{1,0:T(8,128)S(1)} %get-tuple-element.36.own_ref), channel_id=1, source_target_pairs={{0,1},{1,0},{2,3},{3,2},{4,5},{5,4},{6,7},{7,6},{8,9},{9,8},{10,11... | collective-permute-start | bytes 12296 | tf_op jit(solution)/shard_map/ppermute | solution.py:470

commit v8 on v6

--- a/solution.py
+++ b/solution.py
@@ -503,7 +503,7 @@
         far = lax.ppermute(near, "groups", [(0, 1), (1, 0)])
         rows_here = list(pick_early(wanted, draft_head, near, far, spread, start, parts))
         if few:
-            for i in range(1, half):
+            for i in reversed(range(1, half)):
                 rows_here[i] = lax.ppermute(rows_here[i], "dp", [(j, j ^ i) for j in range(peers)])
         else:
             halves = [list(range(half)), list(range(half, peers))]

time: 92.5 us -> 92.5 us (level)
  no operation moved by 1% of the time
where the time goes in v8:
time: 92.5 us; the launch traced here: 92 us
  waiting for transfers between devices  34.9 us (38%)
  starting transfers between devices  25.1 us (27%)
  Pallas kernels  13.8 us (15%)
  blocking collectives  12.6 us (14%)
  other arithmetic  4.35 us (5%)
  between operations  1.02 us (1%)
    ppermute x6, waiting for transfers between devices, local(): lax.ppermute(rows_here[i], 'dp', [(j, j ^ i) for j in range(peers)])  19.8 us
    all_to_all x1, blocking collectives, exchange(): lax.all_to_all(value, 'dp', split_axis=0, concat_axis=0, tiled=True, axis...  12.6 us
    all_to_all x2, waiting for transfers between devices, exchange(): lax.all_to_all(value, 'dp', split_axis=0, concat_axis=0, tiled=True, axis...  11 us
    all_to_all x2, starting transfers between devices, exchange(): lax.all_to_all(value, 'dp', split_axis=0, concat_axis=0, tiled=True, axis...  10.9 us
    ppermute x6, starting transfers between devices, local(): lax.ppermute(rows_here[i], 'dp', [(j, j ^ i) for j in range(peers)])  8.94 us
    pallas_call x2, Pallas kernels, pick_early(): pl.pallas_call(functools.partial(early_kernel, spread=spread, start=start...  4.39 us
    pallas_call x1, Pallas kernels, pick(): pl.pallas_call(functools.partial(pick_kernel, spread=spread), in_specs=[V...  3.69 us
    ppermute x2, starting transfers between devices, local(): lax.ppermute(near, 'dp', across)  2.97 us
  transfers between devices with their start and end apart: 14, of which 8 were waited for; matrix products, arithmetic and copies ran while one was open for 5% of the time, Pallas kernels for 9%

profile of v8, /device:TPU:0, one launch (start us, length us, event | category | flops | bytes accessed | tf_op | source)
XLA Modules:
  0.0 92.0 jit_solution(13184863985825097326)
XLA Ops:
  0.7 1.5 %begin.1 = (s32[16,128]{1,0:T(8,128)}, bf16[256,256]{1,0:T(8,128)(2,1)S(1)}, bf16[256,384]{1,0:T(8,128)(2,1)S(1)}) custom-call(s32[1]{0:T(128)} %bitcast.11.group_ref, s32[4,128]{1,0:T(4,128)} %bitcast.39, s32[4,128]{1,0:T(4,128)} %bitcast.41, bf16[512,2048]{1,0:T(8,128)(2,1)} %head_hbm.7), custom_call_target="tpu_custom_call" | custom-call | tf_op jit(solution)/shard_map/begin/pallas_call | solution.py:342
  2.2 7.3 %all-to-all-start = ((s32[8,2,128]{2,1,0:T(2,128)}), s32[8,2,128]{2,1,0:T(2,128)S(1)}, u32[]{:S(2)}, u32[]{:S(2)}) async-start(s32[8,2,128]{2,1,0:T(2,128)} %bitcast.43), calls=%async_computation | async-start | bytes 16384 | tf_op jit(solution)/shard_map/all_to_all | solution.py:454
  9.4 2.9 %collective-permute-start.6 = (bf16[256,384]{1,0:T(8,128)(2,1)S(1)}, bf16[256,384]{1,0:T(8,128)(2,1)S(1)}, u32[]{:S(2)}, u32[]{:S(2)}) collective-permute-start(bf16[256,384]{1,0:T(8,128)(2,1)S(1)} %get-tuple-element.27), channel_id=1, source_target_pairs={{0,8},{2,10},{4,12},{6,14},{8,0},{10,2},{12,4},{14,6},{1,9},{3,11}... | collective-permute-start | bytes 589832 | tf_op jit(solution)/shard_map/ppermute | solution.py:487
  12.4 0.4 fusion
  12.9 0.2 reduce-window.7
  13.1 0.1 fusion.8
  13.3 0.2 convert_reduce_fusion
  13.7 8.1 %all-to-all-done = s32[8,2,128]{2,1,0:T(2,128)S(1)} async-done(((s32[8,2,128]{2,1,0:T(2,128)}), s32[8,2,128]{2,1,0:T(2,128)S(1)}, u32[]{:S(2)}, u32[]{:S(2)}) %all-to-all-start) | async-done | bytes 8224 | tf_op jit(solution)/shard_map/all_to_all | solution.py:454
  21.8 3.7 %pick.1 = bf16[768,1408]{1,0:T(8,128)(2,1)} custom-call(s32[16,128]{1,0:T(8,128)S(1)} %bitcast.35, bf16[512,2048]{1,0:T(8,128)(2,1)} %head_hbm.7), custom_call_target="tpu_custom_call" | custom-call | tf_op jit(solution)/shard_map/pick/pallas_call | solution.py:324
  25.5 3.6 %all-to-all-start.1 = ((bf16[8,96,1408]{2,1,0:T(8,128)(2,1)}), bf16[8,96,1408]{2,1,0:T(8,128)(2,1)S(1)}, u32[]{:S(2)}, u32[]{:S(2)}) async-start(bf16[8,96,1408]{2,1,0:T(8,128)(2,1)} %bitcast.38), calls=%async_computation.1 | async-start | bytes 4325376 | tf_op jit(solution)/shard_map/all_to_all | solution.py:454
  29.3 2.0 %fusion.2 = f32[128,2048]{1,0:T(8,128)S(1)} fusion(f32[3,128]{1,0:T(4,128)S(1)} %add_rsqrt_fusion, f32[3,2048]{1,0:T(4,128)S(1)} %copy-done.2, bf16[128,3,2048]{2,0,1:T(8,128)(2,1)} %param.8), kind=kLoop, calls=%fused_computation.4 | loop fusion | flops 2883584 | bytes 2647552 | tf_op jit(solution)/shard_map/reduce_sum | solution.py:523
  31.3 1.6 %collective-permute-start.2 = (bf16[256,256]{1,0:T(8,128)(2,1)S(1)}, bf16[256,256]{1,0:T(8,128)(2,1)S(1)}, u32[]{:S(2)}, u32[]{:S(2)}) collective-permute-start(bf16[256,256]{1,0:T(8,128)(2,1)S(1)} %collective-permute-done.1.near_ref), channel_id=1, source_target_pairs={{0,16},{16,0},{1,17},{17,1},{2,18},{18,2},{3,19},{19,3},{4,20},{20... | collective-permute-start | bytes 393224 | tf_op jit(solution)/shard_map/ppermute | solution.py:503
  32.9 0.6 collective-permute-start.7
  33.5 2.9 %collective-permute-done.2.far_ref = bf16[256,256]{1,0:T(8,128)(2,1)S(1)} collective-permute-done((bf16[256,256]{1,0:T(8,128)(2,1)S(1)}, bf16[256,256]{1,0:T(8,128)(2,1)S(1)}, u32[]{:S(2)}, u32[]{:S(2)}) %collective-permute-start.2) | collective-permute-done | bytes 131104 | tf_op jit(solution)/shard_map/ppermute | solution.py:503
  36.4 2.0 %pick_early.2 = (bf16[192,256]{1,0:T(8,128)(2,1)S(1)}, bf16[192,256]{1,0:T(8,128)(2,1)}, bf16[192,256]{1,0:T(8,128)(2,1)}, bf16[192,256]{1,0:T(8,128)(2,1)}) custom-call(s32[8,128]{1,0:T(8,128)S(1)} %add_select_fusion.3.asked_ref, bf16[512,2048]{1,0:T(8,128)(2,1)} %head_hbm.7, bf16[256,256]{1,0:T(8,128)(2,1)S(1)} %collective-permute-done.1.near_ref, ...), custom_call_target="tpu_custom_call" | custom-call | tf_op jit(solution)/shard_map/pick_early/pallas_call | solution.py:362
  38.4 2.0 %collective-permute-start.3 = (bf16[192,256]{1,0:T(8,128)(2,1)}, bf16[192,256]{1,0:T(8,128)(2,1)S(1)}, u32[]{:S(2)}, u32[]{:S(2)}) collective-permute-start(bf16[192,256]{1,0:T(8,128)(2,1)} %get-tuple-element.24), channel_id=1, source_target_pairs={{0,2},{2,0},{4,6},{6,4},{8,10},{10,8},{12,14},{14,12},{1,3},{3,1},... | collective-permute-start | bytes 294920 | tf_op jit(solution)/shard_map/ppermute | solution.py:507
  40.4 0.2 reduce-precision_convert_fusion
  40.6 3.3 %collective-permute-start.4 = (bf16[192,256]{1,0:T(8,128)(2,1)}, bf16[192,256]{1,0:T(8,128)(2,1)S(1)}, u32[]{:S(2)}, u32[]{:S(2)}) collective-permute-start(bf16[192,256]{1,0:T(8,128)(2,1)} %get-tuple-element.25), channel_id=1, source_target_pairs={{0,4},{2,6},{4,0},{6,2},{8,12},{10,14},{12,8},{14,10},{1,5},{3,7},... | collective-permute-start | bytes 294920 | tf_op jit(solution)/shard_map/ppermute | solution.py:507
  43.9 2.3 %pick_early.3 = (bf16[192,384]{1,0:T(8,128)(2,1)S(1)}, bf16[192,384]{1,0:T(8,128)(2,1)}, bf16[192,384]{1,0:T(8,128)(2,1)}, bf16[192,384]{1,0:T(8,128)(2,1)}) custom-call(s32[8,128]{1,0:T(8,128)S(1)} %add_select_fusion.3.asked_ref, bf16[512,2048]{1,0:T(8,128)(2,1)} %head_hbm.7, bf16[256,384]{1,0:T(8,128)(2,1)S(1)} %collective-permute-done.6.near_ref, ...), custom_call_target="tpu_custom_call" | custom-call | tf_op jit(solution)/shard_map/pick_early/pallas_call | solution.py:362
  46.3 3.0 %collective-permute-start.10 = (bf16[192,384]{1,0:T(8,128)(2,1)}, bf16[192,384]{1,0:T(8,128)(2,1)S(1)}, u32[]{:S(2)}, u32[]{:S(2)}) collective-permute-start(bf16[192,384]{1,0:T(8,128)(2,1)} %get-tuple-element.32), channel_id=1, source_target_pairs={{0,6},{2,4},{4,2},{6,0},{8,14},{10,12},{12,10},{14,8},{1,7},{3,5},... | collective-permute-start | bytes 442376 | tf_op jit(solution)/shard_map/ppermute | solution.py:507
  49.3 0.6 collective-permute-start.9
  49.9 1.1 %pad_maximum_fusion.mixed_hbm = bf16[256,2048]{1,0:T(8,128)(2,1)} fusion(bf16[128,2048]{1,0:T(8,128)(2,1)S(1)} %get-tuple-element.39, bf16[128,2048]{1,0:T(8,128)(2,1)S(1)} %get-tuple-element.38), kind=kLoop, calls=%fused_computation.8 | loop fusion | flops 2097152 | bytes 2097152 | tf_op jit(solution)/shard_map/concatenate | solution.py:525
  51.1 15.6 %collective-permute-done.4.refs_2_ = bf16[192,256]{1,0:T(8,128)(2,1)S(1)} collective-permute-done((bf16[192,256]{1,0:T(8,128)(2,1)}, bf16[192,256]{1,0:T(8,128)(2,1)S(1)}, u32[]{:S(2)}, u32[]{:S(2)}) %collective-permute-start.4) | collective-permute-done | bytes 98336 | tf_op jit(solution)/shard_map/ppermute | solution.py:507
  66.7 1.1 %collective-permute-done.5.refs_3_ = bf16[192,256]{1,0:T(8,128)(2,1)S(1)} collective-permute-done((bf16[192,256]{1,0:T(8,128)(2,1)}, bf16[192,256]{1,0:T(8,128)(2,1)S(1)}, u32[]{:S(2)}, u32[]{:S(2)}) %collective-permute-start.5) | collective-permute-done | bytes 98336 | tf_op jit(solution)/shard_map/ppermute | solution.py:507
  67.7 1.6 %collective-permute-done.10.refs_7_ = bf16[192,384]{1,0:T(8,128)(2,1)S(1)} collective-permute-done((bf16[192,384]{1,0:T(8,128)(2,1)}, bf16[192,384]{1,0:T(8,128)(2,1)S(1)}, u32[]{:S(2)}, u32[]{:S(2)}) %collective-permute-start.10) | collective-permute-done | bytes 147488 | tf_op jit(solution)/shard_map/ppermute | solution.py:507
  69.3 1.6 %collective-permute-done.9.refs_6_ = bf16[192,384]{1,0:T(8,128)(2,1)S(1)} collective-permute-done((bf16[192,384]{1,0:T(8,128)(2,1)}, bf16[192,384]{1,0:T(8,128)(2,1)S(1)}, u32[]{:S(2)}, u32[]{:S(2)}) %collective-permute-start.9) | collective-permute-done | bytes 147488 | tf_op jit(solution)/shard_map/ppermute | solution.py:507
  70.9 3.0 %all-to-all-done.1 = bf16[8,96,1408]{2,1,0:T(8,128)(2,1)S(1)} async-done(((bf16[8,96,1408]{2,1,0:T(8,128)(2,1)}), bf16[8,96,1408]{2,1,0:T(8,128)(2,1)S(1)}, u32[]{:S(2)}, u32[]{:S(2)}) %all-to-all-start.1) | async-done | bytes 2162720 | tf_op jit(solution)/shard_map/all_to_all | solution.py:454
  73.9 2.6 %score.1 = (f32[8,128]{1,0:T(8,128)S(1)}, bf16[768,128]{1,0:T(8,128)(2,1)S(1)}, bf16[768,128]{1,0:T(8,128)(2,1)S(1)}) custom-call(f32[40,128]{1,0:T(8,128)S(1)} %pad.9.pack_ref, bf16[256,2048]{1,0:T(8,128)(2,1)} %pad_maximum_fusion.mixed_hbm, bf16[768,1408]{1,0:T(8,128)(2,1)S(1)} %bitcast.32, bf16[192,256]{1,0:T(8,128)(2,1)S(1)} %get-tuple-element.23.refs_0_, ...), custom_call_target="tpu_custom_call" | custom-call | tf_op jit(solution)/shard_map/score/pallas_call | solution.py:381
  76.6 1.2 %collective-permute-done.11.other_ref = f32[8,128]{1,0:T(8,128)S(1)} collective-permute-done((f32[8,128]{1,0:T(8,128)S(1)}, f32[8,128]{1,0:T(8,128)S(1)}, u32[]{:S(2)}, u32[]{:S(2)}) %collective-permute-start.11) | collective-permute-done | bytes 4128 | tf_op jit(solution)/shard_map/ppermute | solution.py:450
  77.7 1.0 %gradient.1 = bf16[8,64,128]{2,1,0:T(8,128)(2,1)S(1)} custom-call(f32[8,128]{1,0:T(8,128)S(1)} %get-tuple-element.33.own_ref, f32[8,128]{1,0:T(8,128)S(1)} %collective-permute-done.11.other_ref, f32[40,128]{1,0:T(8,128)S(1)} %pad.9.pack_ref, bf16[768,128]{1,0:T(8,128)(2,1)S(1)} %get-tuple-element.34.late_mask_ref, ...), custom_call_target="tpu_custom_call" | custom-call | tf_op jit(solution)/shard_map/gradient/pallas_call | solution.py:400
  78.8 12.6 %all_to_all.15.parts_ref = bf16[8,64,128]{2,1,0:T(8,128)(2,1)S(1)} all-to-all(bf16[8,64,128]{2,1,0:T(8,128)(2,1)S(1)} %gradient.1), channel_id=1, replica_groups=mesh['groups'=2,'dp'=8,'mp'=2] {'dp'}, dimensions={0} | all-to-all | bytes 262144 | tf_op jit(solution)/shard_map/all_to_all | solution.py:454
  91.3 0.6 add_up.1
  (59 shorter events, 0.8 us)
Async XLA Ops:
  0.6 12.2 %copy-start.3 = (s32[128,4]{0,1:T(4,128)S(1)}, s32[128,4]{0,1:T(4,128)}, u32[]{:S(2)}) copy-start(s32[128,4]{0,1:T(4,128)} %param.10) | copy-start | bytes 6148
  0.6 12.2 %copy-start.5 = (s32[128,4]{0,1:T(4,128)S(1)}, s32[128,4]{0,1:T(4,128)}, u32[]{:S(2)}) copy-start(s32[128,4]{0,1:T(4,128)} %param.11) | copy-start | bytes 6148
  0.7 11.8 %copy-start = (bf16[128,3,2048]{2,0,1:T(8,128)(2,1)S(1)}, bf16[128,3,2048]{2,0,1:T(8,128)(2,1)}, u32[]{:S(2)}) copy-start(bf16[128,3,2048]{2,0,1:T(8,128)(2,1)} %param.8) | copy-start | bytes 4718596
  0.7 12.3 %copy-start.6 = (s32[1,4]{1,0:T(1,128)S(1)}, s32[1,4]{1,0:T(1,128)}, u32[]{:S(2)}) copy-start(s32[1,4]{1,0:T(1,128)} %param.13) | copy-start | bytes 52
  0.7 12.6 %copy-start.7 = (s32[128,1]{0,1:T(1,128)S(1)}, s32[128,1]{0,1:T(1,128)}, u32[]{:S(2)}) copy-start(s32[128,1]{0,1:T(1,128)} %param.9) | copy-start | bytes 1540
  0.7 12.8 %copy-start.4 = (bf16[128,4]{0,1:T(4,128)(2,1)S(1)}, bf16[128,4]{0,1:T(4,128)(2,1)}, u32[]{:S(2)}) copy-start(bf16[128,4]{0,1:T(4,128)(2,1)} %param.12) | copy-start | bytes 3076
  2.2 19.6 %all-to-all-start = ((s32[8,2,128]{2,1,0:T(2,128)}), s32[8,2,128]{2,1,0:T(2,128)S(1)}, u32[]{:S(2)}, u32[]{:S(2)}) async-start(s32[8,2,128]{2,1,0:T(2,128)} %bitcast.43), calls=%async_computation | async-start | bytes 16384 | tf_op jit(solution)/shard_map/all_to_all | solution.py:454
  9.4 23.5 %collective-permute-start.6 = (bf16[256,384]{1,0:T(8,128)(2,1)S(1)}, bf16[256,384]{1,0:T(8,128)(2,1)S(1)}, u32[]{:S(2)}, u32[]{:S(2)}) collective-permute-start(bf16[256,384]{1,0:T(8,128)(2,1)S(1)} %get-tuple-element.27), channel_id=1, source_target_pairs={{0,8},{2,10},{4,12},{6,14},{8,0},{10,2},{12,4},{14,6},{1,9},{3,11}... | collective-permute-start | bytes 589832 | tf_op jit(solution)/shard_map/ppermute | solution.py:487
  12.4 19.0 %collective-permute-start.1 = (bf16[256,256]{1,0:T(8,128)(2,1)S(1)}, bf16[256,256]{1,0:T(8,128)(2,1)S(1)}, u32[]{:S(2)}, u32[]{:S(2)}) collective-permute-start(bf16[256,256]{1,0:T(8,128)(2,1)S(1)} %get-tuple-element.21), channel_id=1, source_target_pairs={{0,8},{2,10},{4,12},{6,14},{8,0},{10,2},{12,4},{14,6},{1,9},{3,11}... | collective-permute-start | bytes 393224 | tf_op jit(solution)/shard_map/ppermute | solution.py:487
  12.8 16.5 %collective-permute-start = (f32[3,128]{1,0:T(4,128)S(1)}, f32[3,128]{1,0:T(4,128)S(1)}, u32[]{:S(2)}, u32[]{:S(2)}) collective-permute-start(f32[3,128]{1,0:T(4,128)S(1)} %fusion), channel_id=1, source_target_pairs={{0,1},{1,0},{2,3},{3,2},{4,5},{5,4},{6,7},{7,6},{8,9},{9,8},{10,11... | collective-permute-start | bytes 4616 | tf_op jit(solution)/shard_map/ppermute | solution.py:450
  25.5 3.8 %copy-start.2 = (f32[3,2048]{1,0:T(4,128)S(1)}, f32[3,2048]{1,0:T(4,128)}, u32[]{:S(2)}) copy-start(f32[3,2048]{1,0:T(4,128)} %param.14) | copy-start | bytes 73732
  25.5 48.4 %all-to-all-start.1 = ((bf16[8,96,1408]{2,1,0:T(8,128)(2,1)}), bf16[8,96,1408]{2,1,0:T(8,128)(2,1)S(1)}, u32[]{:S(2)}, u32[]{:S(2)}) async-start(bf16[8,96,1408]{2,1,0:T(8,128)(2,1)} %bitcast.38), calls=%async_computation.1 | async-start | bytes 4325376 | tf_op jit(solution)/shard_map/all_to_all | solution.py:454
  31.3 5.0 %collective-permute-start.2 = (bf16[256,256]{1,0:T(8,128)(2,1)S(1)}, bf16[256,256]{1,0:T(8,128)(2,1)S(1)}, u32[]{:S(2)}, u32[]{:S(2)}) collective-permute-start(bf16[256,256]{1,0:T(8,128)(2,1)S(1)} %collective-permute-done.1.near_ref), channel_id=1, source_target_pairs={{0,16},{16,0},{1,17},{17,1},{2,18},{18,2},{3,19},{19,3},{4,20},{20... | collective-permute-start | bytes 393224 | tf_op jit(solution)/shard_map/ppermute | solution.py:503
  32.9 11.0 %collective-permute-start.7 = (bf16[256,384]{1,0:T(8,128)(2,1)S(1)}, bf16[256,384]{1,0:T(8,128)(2,1)S(1)}, u32[]{:S(2)}, u32[]{:S(2)}) collective-permute-start(bf16[256,384]{1,0:T(8,128)(2,1)S(1)} %collective-permute-done.6.near_ref), channel_id=1, source_target_pairs={{0,16},{16,0},{1,17},{17,1},{2,18},{18,2},{3,19},{19,3},{4,20},{20... | collective-permute-start | bytes 589832 | tf_op jit(solution)/shard_map/ppermute | solution.py:503
  38.4 10.8 %collective-permute-start.3 = (bf16[192,256]{1,0:T(8,128)(2,1)}, bf16[192,256]{1,0:T(8,128)(2,1)S(1)}, u32[]{:S(2)}, u32[]{:S(2)}) collective-permute-start(bf16[192,256]{1,0:T(8,128)(2,1)} %get-tuple-element.24), channel_id=1, source_target_pairs={{0,2},{2,0},{4,6},{6,4},{8,10},{10,8},{12,14},{14,12},{1,3},{3,1},... | collective-permute-start | bytes 294920 | tf_op jit(solution)/shard_map/ppermute | solution.py:507
  40.6 26.1 %collective-permute-start.4 = (bf16[192,256]{1,0:T(8,128)(2,1)}, bf16[192,256]{1,0:T(8,128)(2,1)S(1)}, u32[]{:S(2)}, u32[]{:S(2)}) collective-permute-start(bf16[192,256]{1,0:T(8,128)(2,1)} %get-tuple-element.25), channel_id=1, source_target_pairs={{0,4},{2,6},{4,0},{6,2},{8,12},{10,14},{12,8},{14,10},{1,5},{3,7},... | collective-permute-start | bytes 294920 | tf_op jit(solution)/shard_map/ppermute | solution.py:507
  43.9 23.8 %collective-permute-start.5 = (bf16[192,256]{1,0:T(8,128)(2,1)}, bf16[192,256]{1,0:T(8,128)(2,1)S(1)}, u32[]{:S(2)}, u32[]{:S(2)}) collective-permute-start(bf16[192,256]{1,0:T(8,128)(2,1)} %get-tuple-element.26), channel_id=1, source_target_pairs={{0,6},{2,4},{4,2},{6,0},{8,14},{10,12},{12,10},{14,8},{1,7},{3,5},... | collective-permute-start | bytes 294920 | tf_op jit(solution)/shard_map/ppermute | solution.py:507
  46.3 23.1 %collective-permute-start.10 = (bf16[192,384]{1,0:T(8,128)(2,1)}, bf16[192,384]{1,0:T(8,128)(2,1)S(1)}, u32[]{:S(2)}, u32[]{:S(2)}) collective-permute-start(bf16[192,384]{1,0:T(8,128)(2,1)} %get-tuple-element.32), channel_id=1, source_target_pairs={{0,6},{2,4},{4,2},{6,0},{8,14},{10,12},{12,10},{14,8},{1,7},{3,5},... | collective-permute-start | bytes 442376 | tf_op jit(solution)/shard_map/ppermute | solution.py:507
  49.2 20.1 %collective-permute-start.8 = (bf16[192,384]{1,0:T(8,128)(2,1)}, bf16[192,384]{1,0:T(8,128)(2,1)S(1)}, u32[]{:S(2)}, u32[]{:S(2)}) collective-permute-start(bf16[192,384]{1,0:T(8,128)(2,1)} %get-tuple-element.30), channel_id=1, source_target_pairs={{0,2},{2,0},{4,6},{6,4},{8,10},{10,8},{12,14},{14,12},{1,3},{3,1},... | collective-permute-start | bytes 442376 | tf_op jit(solution)/shard_map/ppermute | solution.py:507
  49.3 21.6 %collective-permute-start.9 = (bf16[192,384]{1,0:T(8,128)(2,1)}, bf16[192,384]{1,0:T(8,128)(2,1)S(1)}, u32[]{:S(2)}, u32[]{:S(2)}) collective-permute-start(bf16[192,384]{1,0:T(8,128)(2,1)} %get-tuple-element.31), channel_id=1, source_target_pairs={{0,4},{2,6},{4,0},{6,2},{8,12},{10,14},{12,8},{14,10},{1,5},{3,7},... | collective-permute-start | bytes 442376 | tf_op jit(solution)/shard_map/ppermute | solution.py:507
  73.9 3.9 %copy-start.1 = (bf16[128,3,2048]{2,0,1:T(8,128)(2,1)S(1)}, bf16[128,3,2048]{2,0,1:T(8,128)(2,1)}, u32[]{:S(2)}) copy-start(bf16[128,3,2048]{2,0,1:T(8,128)(2,1)} %param.8) | copy-start | bytes 4718596
  76.5 1.2 %collective-permute-start.11 = (f32[8,128]{1,0:T(8,128)S(1)}, f32[8,128]{1,0:T(8,128)S(1)}, u32[]{:S(2)}, u32[]{:S(2)}) collective-permute-start(f32[8,128]{1,0:T(8,128)S(1)} %get-tuple-element.33.own_ref), channel_id=1, source_target_pairs={{0,1},{1,0},{2,3},{3,2},{4,5},{5,4},{6,7},{7,6},{8,9},{9,8},{10,11... | collective-permute-start | bytes 12296 | tf_op jit(solution)/shard_map/ppermute | solution.py:450

commit v9 on v6

--- a/solution.py
+++ b/solution.py
@@ -12,7 +12,7 @@
 F32 = jnp.float32
 BF16 = jnp.bfloat16
 VMEM_LIMIT = 16 * 1024 * 1024
-CHUNKS = (256, 384)
+CHUNKS = (128, 512)
 
 
 def iota(shape, axis):

time: 92.5 us -> 92.7 us (level)
    ppermute x2, waiting for transfers between devices: 2.87 us -> 6.39 us  [local(): far = lax.ppermute(near, 'groups', [(0, 1), (1, 0)])]
    ppermute x6, waiting for transfers between devices: 19.8 us -> 17 us  [local(): lax.ppermute(rows_here[i], 'dp', [(j, j ^ i) for j in range(peers)])]
    ppermute x6, starting transfers between devices: 8.94 us -> 7.3 us  [local(): lax.ppermute(rows_here[i], 'dp', [(j, j ^ i) for j in range(peers)])]
    ppermute x2, starting transfers between devices: 2.16 us -> 3.1 us  [local(): far = lax.ppermute(near, 'groups', [(0, 1), (1, 0)])]
  transfers between devices with their start and end apart: 14 -> 14, of which waited for: 8 -> 9; matrix products, arithmetic and copies ran while one was open for 5% -> 5% of each run, Pallas kernels for 9% -> 9%
where the time goes in v9:
time: 92.7 us; the launch traced here: 92.2 us
  waiting for transfers between devices  35.6 us (38%)
  starting transfers between devices  24.4 us (26%)
  Pallas kernels  13.8 us (15%)
  blocking collectives  12.8 us (14%)
  other arithmetic  4.35 us (5%)
  between operations  1.02 us (1%)
    ppermute x6, waiting for transfers between devices, local(): lax.ppermute(rows_here[i], 'dp', [(j, j ^ i) for j in range(peers)])  17 us
    all_to_all x1, blocking collectives, exchange(): lax.all_to_all(value, 'dp', split_axis=0, concat_axis=0, tiled=True, axis...  12.8 us
    all_to_all x2, waiting for transfers between devices, exchange(): lax.all_to_all(value, 'dp', split_axis=0, concat_axis=0, tiled=True, axis...  11 us
    all_to_all x2, starting transfers between devices, exchange(): lax.all_to_all(value, 'dp', split_axis=0, concat_axis=0, tiled=True, axis...  10.9 us
    ppermute x6, starting transfers between devices, local(): lax.ppermute(rows_here[i], 'dp', [(j, j ^ i) for j in range(peers)])  7.3 us
    ppermute x2, waiting for transfers between devices, local(): far = lax.ppermute(near, 'groups', [(0, 1), (1, 0)])  6.39 us
    pallas_call x2, Pallas kernels, pick_early(): pl.pallas_call(functools.partial(early_kernel, spread=spread, start=start...  4.37 us
    pallas_call x1, Pallas kernels, pick(): pl.pallas_call(functools.partial(pick_kernel, spread=spread), in_specs=[V...  3.69 us
  transfers between devices with their start and end apart: 14, of which 9 were waited for; matrix products, arithmetic and copies ran while one was open for 5% of the time, Pallas kernels for 9%

profile of v9, /device:TPU:0, one launch (start us, length us, event | category | flops | bytes accessed | tf_op | source)
XLA Modules:
  0.0 92.2 jit_solution(10300733269401258876)
XLA Ops:
  0.7 1.5 %begin.1 = (s32[16,128]{1,0:T(8,128)}, bf16[256,128]{1,0:T(8,128)(2,1)S(1)}, bf16[256,512]{1,0:T(8,128)(2,1)S(1)}) custom-call(s32[1]{0:T(128)} %bitcast.11.group_ref, s32[4,128]{1,0:T(4,128)} %bitcast.39, s32[4,128]{1,0:T(4,128)} %bitcast.41, bf16[512,2048]{1,0:T(8,128)(2,1)} %head_hbm.7), custom_call_target="tpu_custom_call" | custom-call | tf_op jit(solution)/shard_map/begin/pallas_call | solution.py:342
  2.2 7.3 %all-to-all-start = ((s32[8,2,128]{2,1,0:T(2,128)}), s32[8,2,128]{2,1,0:T(2,128)S(1)}, u32[]{:S(2)}, u32[]{:S(2)}) async-start(s32[8,2,128]{2,1,0:T(2,128)} %bitcast.43), calls=%async_computation | async-start | bytes 16384 | tf_op jit(solution)/shard_map/all_to_all | solution.py:454
  9.4 2.9 %collective-permute-start.6 = (bf16[256,512]{1,0:T(8,128)(2,1)S(1)}, bf16[256,512]{1,0:T(8,128)(2,1)S(1)}, u32[]{:S(2)}, u32[]{:S(2)}) collective-permute-start(bf16[256,512]{1,0:T(8,128)(2,1)S(1)} %get-tuple-element.27), channel_id=1, source_target_pairs={{0,8},{2,10},{4,12},{6,14},{8,0},{10,2},{12,4},{14,6},{1,9},{3,11}... | collective-permute-start | bytes 786440 | tf_op jit(solution)/shard_map/ppermute | solution.py:487
  12.4 0.4 fusion
  12.9 0.2 reduce-window.7
  13.7 8.1 %all-to-all-done = s32[8,2,128]{2,1,0:T(2,128)S(1)} async-done(((s32[8,2,128]{2,1,0:T(2,128)}), s32[8,2,128]{2,1,0:T(2,128)S(1)}, u32[]{:S(2)}, u32[]{:S(2)}) %all-to-all-start) | async-done | bytes 8224 | tf_op jit(solution)/shard_map/all_to_all | solution.py:454
  21.8 3.7 %pick.1 = bf16[768,1408]{1,0:T(8,128)(2,1)} custom-call(s32[16,128]{1,0:T(8,128)S(1)} %bitcast.35, bf16[512,2048]{1,0:T(8,128)(2,1)} %head_hbm.7), custom_call_target="tpu_custom_call" | custom-call | tf_op jit(solution)/shard_map/pick/pallas_call | solution.py:324
  25.5 3.6 %all-to-all-start.1 = ((bf16[8,96,1408]{2,1,0:T(8,128)(2,1)}), bf16[8,96,1408]{2,1,0:T(8,128)(2,1)S(1)}, u32[]{:S(2)}, u32[]{:S(2)}) async-start(bf16[8,96,1408]{2,1,0:T(8,128)(2,1)} %bitcast.38), calls=%async_computation.1 | async-start | bytes 4325376 | tf_op jit(solution)/shard_map/all_to_all | solution.py:454
  29.3 2.0 %fusion.2 = f32[128,2048]{1,0:T(8,128)S(1)} fusion(f32[3,128]{1,0:T(4,128)S(1)} %add_rsqrt_fusion, f32[3,2048]{1,0:T(4,128)S(1)} %copy-done.2, bf16[128,3,2048]{2,0,1:T(8,128)(2,1)} %param.8), kind=kLoop, calls=%fused_computation.4 | loop fusion | flops 2883584 | bytes 2647552 | tf_op jit(solution)/shard_map/reduce_sum | solution.py:523
  31.3 1.6 %collective-permute-start.2 = (bf16[256,128]{1,0:T(8,128)(2,1)S(1)}, bf16[256,128]{1,0:T(8,128)(2,1)S(1)}, u32[]{:S(2)}, u32[]{:S(2)}) collective-permute-start(bf16[256,128]{1,0:T(8,128)(2,1)S(1)} %collective-permute-done.1.near_ref), channel_id=1, source_target_pairs={{0,16},{16,0},{1,17},{17,1},{2,18},{18,2},{3,19},{19,3},{4,20},{20... | collective-permute-start | bytes 196616 | tf_op jit(solution)/shard_map/ppermute | solution.py:503
  32.9 3.3 %collective-permute-done.2.far_ref = bf16[256,128]{1,0:T(8,128)(2,1)S(1)} collective-permute-done((bf16[256,128]{1,0:T(8,128)(2,1)S(1)}, bf16[256,128]{1,0:T(8,128)(2,1)S(1)}, u32[]{:S(2)}, u32[]{:S(2)}) %collective-permute-start.2) | collective-permute-done | bytes 65568 | tf_op jit(solution)/shard_map/ppermute | solution.py:503
  36.3 2.0 %pick_early.2 = (bf16[192,128]{1,0:T(8,128)(2,1)S(1)}, bf16[192,128]{1,0:T(8,128)(2,1)}, bf16[192,128]{1,0:T(8,128)(2,1)}, bf16[192,128]{1,0:T(8,128)(2,1)}) custom-call(s32[8,128]{1,0:T(8,128)S(1)} %add_select_fusion.3.asked_ref, bf16[512,2048]{1,0:T(8,128)(2,1)} %head_hbm.7, bf16[256,128]{1,0:T(8,128)(2,1)S(1)} %collective-permute-done.1.near_ref, ...), custom_call_target="tpu_custom_call" | custom-call | tf_op jit(solution)/shard_map/pick_early/pallas_call | solution.py:362
  38.2 2.1 %collective-permute-start.3 = (bf16[192,128]{1,0:T(8,128)(2,1)}, bf16[192,128]{1,0:T(8,128)(2,1)S(1)}, u32[]{:S(2)}, u32[]{:S(2)}) collective-permute-start(bf16[192,128]{1,0:T(8,128)(2,1)} %get-tuple-element.24), channel_id=1, source_target_pairs={{0,2},{2,0},{4,6},{6,4},{8,10},{10,8},{12,14},{14,12},{1,3},{3,1},... | collective-permute-start | bytes 147464 | tf_op jit(solution)/shard_map/ppermute | solution.py:507
  40.4 1.5 %collective-permute-start.7 = (bf16[256,512]{1,0:T(8,128)(2,1)S(1)}, bf16[256,512]{1,0:T(8,128)(2,1)S(1)}, u32[]{:S(2)}, u32[]{:S(2)}) collective-permute-start(bf16[256,512]{1,0:T(8,128)(2,1)S(1)} %collective-permute-done.6.near_ref), channel_id=1, source_target_pairs={{0,16},{16,0},{1,17},{17,1},{2,18},{18,2},{3,19},{19,3},{4,20},{20... | collective-permute-start | bytes 786440 | tf_op jit(solution)/shard_map/ppermute | solution.py:503
  42.0 1.1 %collective-permute-start.4 = (bf16[192,128]{1,0:T(8,128)(2,1)}, bf16[192,128]{1,0:T(8,128)(2,1)S(1)}, u32[]{:S(2)}, u32[]{:S(2)}) collective-permute-start(bf16[192,128]{1,0:T(8,128)(2,1)} %get-tuple-element.25), channel_id=1, source_target_pairs={{0,4},{2,6},{4,0},{6,2},{8,12},{10,14},{12,8},{14,10},{1,5},{3,7},... | collective-permute-start | bytes 147464 | tf_op jit(solution)/shard_map/ppermute | solution.py:507
  43.2 0.5 collective-permute-start.5
  43.7 3.1 %collective-permute-done.7.far_ref = bf16[256,512]{1,0:T(8,128)(2,1)S(1)} collective-permute-done((bf16[256,512]{1,0:T(8,128)(2,1)S(1)}, bf16[256,512]{1,0:T(8,128)(2,1)S(1)}, u32[]{:S(2)}, u32[]{:S(2)}) %collective-permute-start.7) | collective-permute-done | bytes 262176 | tf_op jit(solution)/shard_map/ppermute | solution.py:503
  46.7 2.4 %pick_early.3 = (bf16[192,512]{1,0:T(8,128)(2,1)S(1)}, bf16[192,512]{1,0:T(8,128)(2,1)}, bf16[192,512]{1,0:T(8,128)(2,1)}, bf16[192,512]{1,0:T(8,128)(2,1)}) custom-call(s32[8,128]{1,0:T(8,128)S(1)} %add_select_fusion.3.asked_ref, bf16[512,2048]{1,0:T(8,128)(2,1)} %head_hbm.7, bf16[256,512]{1,0:T(8,128)(2,1)S(1)} %collective-permute-done.6.near_ref, ...), custom_call_target="tpu_custom_call" | custom-call | tf_op jit(solution)/shard_map/pick_early/pallas_call | solution.py:362
  49.2 1.3 %collective-permute-start.10 = (bf16[192,512]{1,0:T(8,128)(2,1)}, bf16[192,512]{1,0:T(8,128)(2,1)S(1)}, u32[]{:S(2)}, u32[]{:S(2)}) collective-permute-start(bf16[192,512]{1,0:T(8,128)(2,1)} %get-tuple-element.32), channel_id=1, source_target_pairs={{0,6},{2,4},{4,2},{6,0},{8,14},{10,12},{12,10},{14,8},{1,7},{3,5},... | collective-permute-start | bytes 589832 | tf_op jit(solution)/shard_map/ppermute | solution.py:507
  50.5 1.7 %collective-permute-start.8 = (bf16[192,512]{1,0:T(8,128)(2,1)}, bf16[192,512]{1,0:T(8,128)(2,1)S(1)}, u32[]{:S(2)}, u32[]{:S(2)}) collective-permute-start(bf16[192,512]{1,0:T(8,128)(2,1)} %get-tuple-element.30), channel_id=1, source_target_pairs={{0,2},{2,0},{4,6},{6,4},{8,10},{10,8},{12,14},{14,12},{1,3},{3,1},... | collective-permute-start | bytes 589832 | tf_op jit(solution)/shard_map/ppermute | solution.py:507
  52.1 0.6 collective-permute-start.9
  52.7 1.1 %pad_maximum_fusion.mixed_hbm = bf16[256,2048]{1,0:T(8,128)(2,1)} fusion(bf16[128,2048]{1,0:T(8,128)(2,1)S(1)} %get-tuple-element.39, bf16[128,2048]{1,0:T(8,128)(2,1)S(1)} %get-tuple-element.38), kind=kLoop, calls=%fused_computation.8 | loop fusion | flops 2097152 | bytes 2097152 | tf_op jit(solution)/shard_map/concatenate | solution.py:525
  53.9 12.2 %collective-permute-done.4.refs_2_ = bf16[192,128]{1,0:T(8,128)(2,1)S(1)} collective-permute-done((bf16[192,128]{1,0:T(8,128)(2,1)}, bf16[192,128]{1,0:T(8,128)(2,1)S(1)}, u32[]{:S(2)}, u32[]{:S(2)}) %collective-permute-start.4) | collective-permute-done | bytes 49184 | tf_op jit(solution)/shard_map/ppermute | solution.py:507
  66.2 0.5 collective-permute-done.5.refs_3_
  66.7 2.1 %collective-permute-done.10.refs_7_ = bf16[192,512]{1,0:T(8,128)(2,1)S(1)} collective-permute-done((bf16[192,512]{1,0:T(8,128)(2,1)}, bf16[192,512]{1,0:T(8,128)(2,1)S(1)}, u32[]{:S(2)}, u32[]{:S(2)}) %collective-permute-start.10) | collective-permute-done | bytes 196640 | tf_op jit(solution)/shard_map/ppermute | solution.py:507
  68.8 2.1 %collective-permute-done.9.refs_6_ = bf16[192,512]{1,0:T(8,128)(2,1)S(1)} collective-permute-done((bf16[192,512]{1,0:T(8,128)(2,1)}, bf16[192,512]{1,0:T(8,128)(2,1)S(1)}, u32[]{:S(2)}, u32[]{:S(2)}) %collective-permute-start.9) | collective-permute-done | bytes 196640 | tf_op jit(solution)/shard_map/ppermute | solution.py:507
  70.9 3.0 %all-to-all-done.1 = bf16[8,96,1408]{2,1,0:T(8,128)(2,1)S(1)} async-done(((bf16[8,96,1408]{2,1,0:T(8,128)(2,1)}), bf16[8,96,1408]{2,1,0:T(8,128)(2,1)S(1)}, u32[]{:S(2)}, u32[]{:S(2)}) %all-to-all-start.1) | async-done | bytes 2162720 | tf_op jit(solution)/shard_map/all_to_all | solution.py:454
  73.9 2.6 %score.1 = (f32[8,128]{1,0:T(8,128)S(1)}, bf16[768,128]{1,0:T(8,128)(2,1)S(1)}, bf16[768,128]{1,0:T(8,128)(2,1)S(1)}) custom-call(f32[40,128]{1,0:T(8,128)S(1)} %pad.9.pack_ref, bf16[256,2048]{1,0:T(8,128)(2,1)} %pad_maximum_fusion.mixed_hbm, bf16[768,1408]{1,0:T(8,128)(2,1)S(1)} %bitcast.32, bf16[192,128]{1,0:T(8,128)(2,1)S(1)} %get-tuple-element.23.refs_0_, ...), custom_call_target="tpu_custom_call" | custom-call | tf_op jit(solution)/shard_map/score/pallas_call | solution.py:381
  76.6 1.2 %collective-permute-done.11.other_ref = f32[8,128]{1,0:T(8,128)S(1)} collective-permute-done((f32[8,128]{1,0:T(8,128)S(1)}, f32[8,128]{1,0:T(8,128)S(1)}, u32[]{:S(2)}, u32[]{:S(2)}) %collective-permute-start.11) | collective-permute-done | bytes 4128 | tf_op jit(solution)/shard_map/ppermute | solution.py:450
  77.7 1.0 %gradient.1 = bf16[8,64,128]{2,1,0:T(8,128)(2,1)S(1)} custom-call(f32[8,128]{1,0:T(8,128)S(1)} %get-tuple-element.33.own_ref, f32[8,128]{1,0:T(8,128)S(1)} %collective-permute-done.11.other_ref, f32[40,128]{1,0:T(8,128)S(1)} %pad.9.pack_ref, bf16[768,128]{1,0:T(8,128)(2,1)S(1)} %get-tuple-element.34.late_mask_ref, ...), custom_call_target="tpu_custom_call" | custom-call | tf_op jit(solution)/shard_map/gradient/pallas_call | solution.py:400
  78.7 12.8 %all_to_all.15.parts_ref = bf16[8,64,128]{2,1,0:T(8,128)(2,1)S(1)} all-to-all(bf16[8,64,128]{2,1,0:T(8,128)(2,1)S(1)} %gradient.1), channel_id=1, replica_groups=mesh['groups'=2,'dp'=8,'mp'=2] {'dp'}, dimensions={0} | all-to-all | bytes 262144 | tf_op jit(solution)/shard_map/all_to_all | solution.py:454
  91.5 0.6 add_up.1
  (59 shorter events, 1.2 us)
Async XLA Ops:
  0.6 12.2 %copy-start.3 = (s32[128,4]{0,1:T(4,128)S(1)}, s32[128,4]{0,1:T(4,128)}, u32[]{:S(2)}) copy-start(s32[128,4]{0,1:T(4,128)} %param.10) | copy-start | bytes 6148
  0.6 12.2 %copy-start.5 = (s32[128,4]{0,1:T(4,128)S(1)}, s32[128,4]{0,1:T(4,128)}, u32[]{:S(2)}) copy-start(s32[128,4]{0,1:T(4,128)} %param.11) | copy-start | bytes 6148
  0.7 11.8 %copy-start = (bf16[128,3,2048]{2,0,1:T(8,128)(2,1)S(1)}, bf16[128,3,2048]{2,0,1:T(8,128)(2,1)}, u32[]{:S(2)}) copy-start(bf16[128,3,2048]{2,0,1:T(8,128)(2,1)} %param.8) | copy-start | bytes 4718596
  0.7 12.3 %copy-start.6 = (s32[1,4]{1,0:T(1,128)S(1)}, s32[1,4]{1,0:T(1,128)}, u32[]{:S(2)}) copy-start(s32[1,4]{1,0:T(1,128)} %param.13) | copy-start | bytes 52
  0.7 12.6 %copy-start.7 = (s32[128,1]{0,1:T(1,128)S(1)}, s32[128,1]{0,1:T(1,128)}, u32[]{:S(2)}) copy-start(s32[128,1]{0,1:T(1,128)} %param.9) | copy-start | bytes 1540
  0.7 12.8 %copy-start.4 = (bf16[128,4]{0,1:T(4,128)(2,1)S(1)}, bf16[128,4]{0,1:T(4,128)(2,1)}, u32[]{:S(2)}) copy-start(bf16[128,4]{0,1:T(4,128)(2,1)} %param.12) | copy-start | bytes 3076
  2.2 19.6 %all-to-all-start = ((s32[8,2,128]{2,1,0:T(2,128)}), s32[8,2,128]{2,1,0:T(2,128)S(1)}, u32[]{:S(2)}, u32[]{:S(2)}) async-start(s32[8,2,128]{2,1,0:T(2,128)} %bitcast.43), calls=%async_computation | async-start | bytes 16384 | tf_op jit(solution)/shard_map/all_to_all | solution.py:454
  9.4 30.9 %collective-permute-start.6 = (bf16[256,512]{1,0:T(8,128)(2,1)S(1)}, bf16[256,512]{1,0:T(8,128)(2,1)S(1)}, u32[]{:S(2)}, u32[]{:S(2)}) collective-permute-start(bf16[256,512]{1,0:T(8,128)(2,1)S(1)} %get-tuple-element.27), channel_id=1, source_target_pairs={{0,8},{2,10},{4,12},{6,14},{8,0},{10,2},{12,4},{14,6},{1,9},{3,11}... | collective-permute-start | bytes 786440 | tf_op jit(solution)/shard_map/ppermute | solution.py:487
  12.4 19.0 %collective-permute-start.1 = (bf16[256,128]{1,0:T(8,128)(2,1)S(1)}, bf16[256,128]{1,0:T(8,128)(2,1)S(1)}, u32[]{:S(2)}, u32[]{:S(2)}) collective-permute-start(bf16[256,128]{1,0:T(8,128)(2,1)S(1)} %get-tuple-element.21), channel_id=1, source_target_pairs={{0,8},{2,10},{4,12},{6,14},{8,0},{10,2},{12,4},{14,6},{1,9},{3,11}... | collective-permute-start | bytes 196616 | tf_op jit(solution)/shard_map/ppermute | solution.py:487
  12.8 16.5 %collective-permute-start = (f32[3,128]{1,0:T(4,128)S(1)}, f32[3,128]{1,0:T(4,128)S(1)}, u32[]{:S(2)}, u32[]{:S(2)}) collective-permute-start(f32[3,128]{1,0:T(4,128)S(1)} %fusion), channel_id=1, source_target_pairs={{0,1},{1,0},{2,3},{3,2},{4,5},{5,4},{6,7},{7,6},{8,9},{9,8},{10,11... | collective-permute-start | bytes 4616 | tf_op jit(solution)/shard_map/ppermute | solution.py:450
  25.5 3.8 %copy-start.2 = (f32[3,2048]{1,0:T(4,128)S(1)}, f32[3,2048]{1,0:T(4,128)}, u32[]{:S(2)}) copy-start(f32[3,2048]{1,0:T(4,128)} %param.14) | copy-start | bytes 73732
  25.5 48.4 %all-to-all-start.1 = ((bf16[8,96,1408]{2,1,0:T(8,128)(2,1)}), bf16[8,96,1408]{2,1,0:T(8,128)(2,1)S(1)}, u32[]{:S(2)}, u32[]{:S(2)}) async-start(bf16[8,96,1408]{2,1,0:T(8,128)(2,1)} %bitcast.38), calls=%async_computation.1 | async-start | bytes 4325376 | tf_op jit(solution)/shard_map/all_to_all | solution.py:454
  31.3 4.9 %collective-permute-start.2 = (bf16[256,128]{1,0:T(8,128)(2,1)S(1)}, bf16[256,128]{1,0:T(8,128)(2,1)S(1)}, u32[]{:S(2)}, u32[]{:S(2)}) collective-permute-start(bf16[256,128]{1,0:T(8,128)(2,1)S(1)} %collective-permute-done.1.near_ref), channel_id=1, source_target_pairs={{0,16},{16,0},{1,17},{17,1},{2,18},{18,2},{3,19},{19,3},{4,20},{20... | collective-permute-start | bytes 196616 | tf_op jit(solution)/shard_map/ppermute | solution.py:503
  38.2 13.9 %collective-permute-start.3 = (bf16[192,128]{1,0:T(8,128)(2,1)}, bf16[192,128]{1,0:T(8,128)(2,1)S(1)}, u32[]{:S(2)}, u32[]{:S(2)}) collective-permute-start(bf16[192,128]{1,0:T(8,128)(2,1)} %get-tuple-element.24), channel_id=1, source_target_pairs={{0,2},{2,0},{4,6},{6,4},{8,10},{10,8},{12,14},{14,12},{1,3},{3,1},... | collective-permute-start | bytes 147464 | tf_op jit(solution)/shard_map/ppermute | solution.py:507
  40.4 6.4 %collective-permute-start.7 = (bf16[256,512]{1,0:T(8,128)(2,1)S(1)}, bf16[256,512]{1,0:T(8,128)(2,1)S(1)}, u32[]{:S(2)}, u32[]{:S(2)}) collective-permute-start(bf16[256,512]{1,0:T(8,128)(2,1)S(1)} %collective-permute-done.6.near_ref), channel_id=1, source_target_pairs={{0,16},{16,0},{1,17},{17,1},{2,18},{18,2},{3,19},{19,3},{4,20},{20... | collective-permute-start | bytes 786440 | tf_op jit(solution)/shard_map/ppermute | solution.py:503
  42.0 24.1 %collective-permute-start.4 = (bf16[192,128]{1,0:T(8,128)(2,1)}, bf16[192,128]{1,0:T(8,128)(2,1)S(1)}, u32[]{:S(2)}, u32[]{:S(2)}) collective-permute-start(bf16[192,128]{1,0:T(8,128)(2,1)} %get-tuple-element.25), channel_id=1, source_target_pairs={{0,4},{2,6},{4,0},{6,2},{8,12},{10,14},{12,8},{14,10},{1,5},{3,7},... | collective-permute-start | bytes 147464 | tf_op jit(solution)/shard_map/ppermute | solution.py:507
  43.2 23.5 %collective-permute-start.5 = (bf16[192,128]{1,0:T(8,128)(2,1)}, bf16[192,128]{1,0:T(8,128)(2,1)S(1)}, u32[]{:S(2)}, u32[]{:S(2)}) collective-permute-start(bf16[192,128]{1,0:T(8,128)(2,1)} %get-tuple-element.26), channel_id=1, source_target_pairs={{0,6},{2,4},{4,2},{6,0},{8,14},{10,12},{12,10},{14,8},{1,7},{3,5},... | collective-permute-start | bytes 147464 | tf_op jit(solution)/shard_map/ppermute | solution.py:507
  49.2 19.6 %collective-permute-start.10 = (bf16[192,512]{1,0:T(8,128)(2,1)}, bf16[192,512]{1,0:T(8,128)(2,1)S(1)}, u32[]{:S(2)}, u32[]{:S(2)}) collective-permute-start(bf16[192,512]{1,0:T(8,128)(2,1)} %get-tuple-element.32), channel_id=1, source_target_pairs={{0,6},{2,4},{4,2},{6,0},{8,14},{10,12},{12,10},{14,8},{1,7},{3,5},... | collective-permute-start | bytes 589832 | tf_op jit(solution)/shard_map/ppermute | solution.py:507
  50.5 18.3 %collective-permute-start.8 = (bf16[192,512]{1,0:T(8,128)(2,1)}, bf16[192,512]{1,0:T(8,128)(2,1)S(1)}, u32[]{:S(2)}, u32[]{:S(2)}) collective-permute-start(bf16[192,512]{1,0:T(8,128)(2,1)} %get-tuple-element.30), channel_id=1, source_target_pairs={{0,2},{2,0},{4,6},{6,4},{8,10},{10,8},{12,14},{14,12},{1,3},{3,1},... | collective-permute-start | bytes 589832 | tf_op jit(solution)/shard_map/ppermute | solution.py:507
  52.1 18.8 %collective-permute-start.9 = (bf16[192,512]{1,0:T(8,128)(2,1)}, bf16[192,512]{1,0:T(8,128)(2,1)S(1)}, u32[]{:S(2)}, u32[]{:S(2)}) collective-permute-start(bf16[192,512]{1,0:T(8,128)(2,1)} %get-tuple-element.31), channel_id=1, source_target_pairs={{0,4},{2,6},{4,0},{6,2},{8,12},{10,14},{12,8},{14,10},{1,5},{3,7},... | collective-permute-start | bytes 589832 | tf_op jit(solution)/shard_map/ppermute | solution.py:507
  73.9 3.9 %copy-start.1 = (bf16[128,3,2048]{2,0,1:T(8,128)(2,1)S(1)}, bf16[128,3,2048]{2,0,1:T(8,128)(2,1)}, u32[]{:S(2)}) copy-start(bf16[128,3,2048]{2,0,1:T(8,128)(2,1)} %param.8) | copy-start | bytes 4718596
  76.5 1.2 %collective-permute-start.11 = (f32[8,128]{1,0:T(8,128)S(1)}, f32[8,128]{1,0:T(8,128)S(1)}, u32[]{:S(2)}, u32[]{:S(2)}) collective-permute-start(f32[8,128]{1,0:T(8,128)S(1)} %get-tuple-element.33.own_ref), channel_id=1, source_target_pairs={{0,1},{1,0},{2,3},{3,2},{4,5},{5,4},{6,7},{7,6},{8,9},{9,8},{10,11... | collective-permute-start | bytes 12296 | tf_op jit(solution)/shard_map/ppermute | solution.py:450
